TPU v7x, 32 devices: a whole 2x2x4 slice. The times are simulated.
32 devices in a mesh: ctx: 8 (over z, y), fsdp: 4 (over x, core).
Axes of the slice: x: 2, y: 2, z: 4, core: 2. Of those that a mesh axis runs over, the one named last changes fastest.
Arguments:
- tokens: bfloat16 [4, 16, 128, 1024], P('fsdp', None, 'ctx'), may hold values from -6 to 6
- lengths: int32 [4, 3], P('fsdp'), may hold values from 512 to 1024, as said below
- packing: int32 [4, 3], P('fsdp'), may hold values from 0 to 2, each once within a row
- query_w: bfloat16 [1024, 1024], P('fsdp'), may hold values from -0.1875 to 0.1875
- query_b: float32 [1024], replicated, may hold values from -3 to 3
- key_w: bfloat16 [1024, 1024], P('fsdp'), may hold values from -0.1875 to 0.1875
- value_w: bfloat16 [1024, 1024], P('fsdp'), may hold values from -0.1875 to 0.1875
- value_b: float32 [1024], replicated, may hold values from -3 to 3
- output_w: bfloat16 [1024, 1024], P('fsdp'), may hold values from -3 to 3
- output_b: float32 [1024], replicated, may hold values from -3 to 3
- attn_gain: float32 [1024], replicated, may hold values from 0.5 to 1.5
- attn_shift: float32 [1024], replicated, may hold values from -2 to 2
- expand_w: bfloat16 [1024, 4096], P('fsdp'), may hold values from -0.1875 to 0.1875
- expand_b: float32 [4096], replicated, may hold values from -3 to 3
- reduce_w: bfloat16 [4096, 1024], P('fsdp'), may hold values from -0.09375 to 0.09375
- reduce_b: float32 [1024], replicated, may hold values from -3 to 3
- ffn_gain: float32 [1024], replicated, may hold values from 0.5 to 1.5
- ffn_shift: float32 [1024], replicated, may hold values from -2 to 2
- cotangent: bfloat16 [4, 16, 128, 1024], P('fsdp', None, 'ctx'), may hold values from -6 to 6
Outputs:
- layer_out: bfloat16 [4, 16, 128, 1024], P('fsdp', None, 'ctx')
- grad_tokens: float32 [4, 16, 128, 1024], P('fsdp', None, 'ctx')
- grad_query_w: float32 [1024, 1024], P('fsdp')
- grad_query_b: float32 [1024], replicated
- grad_key_w: float32 [1024, 1024], P('fsdp')
- grad_value_w: float32 [1024, 1024], P('fsdp')
- grad_value_b: float32 [1024], replicated
- grad_output_w: float32 [1024, 1024], P('fsdp')
- grad_output_b: float32 [1024], replicated
- grad_attn_gain: float32 [1024], replicated
- grad_attn_shift: float32 [1024], replicated
- grad_expand_w: float32 [1024, 4096], P('fsdp')
- grad_expand_b: float32 [4096], replicated
- grad_reduce_w: float32 [4096, 1024], P('fsdp')
- grad_reduce_b: float32 [1024], replicated
- grad_ffn_gain: float32 [1024], replicated
- grad_ffn_shift: float32 [1024], replicated
Inputs may be any that keep to these rules, and one draw needn't show every extreme that they name: Each row's 3 lengths sum to 2048. Each row of packing names every sequence once.
All inputs are finite; a program needn't handle non-finite values.
Results may differ from a plain program's by a relative error of at most 0.02.
Values may be sent and summed in bfloat16 or wider, within the bound.
A program may use at most 192 MiB of HBM per device.

v0:
```python
import jax
import jax.numpy as jnp
from jax import lax
from jax.sharding import PartitionSpec as P

H = 16
HD = 64


def from_behind(block, axis, distance):
    devices = range(lax.axis_size(axis))
    route = [((i - distance) % len(devices), i) for i in devices]
    return lax.ppermute(block, axis, route)


def dense(left, right):
    return jnp.dot(left, right, preferred_element_type=jnp.float32)


def dense_back(left, right):
    return lax.dot_general(
        left, right, (((1,), (1,)), ((), ())), preferred_element_type=jnp.float32
    )


def norm_fwd(hidden, gain, shift):
    mean_row = jnp.mean(hidden, axis=-1, keepdims=True)
    centred = hidden - mean_row
    variance = jnp.mean(centred * centred, axis=-1, keepdims=True)
    inv_std = lax.rsqrt(variance + 1e-05)
    x_hat = centred * inv_std
    return (x_hat * gain + shift, x_hat, inv_std)


def norm_back(incoming, x_hat, inv_std, gain):
    scaled = incoming * gain
    grad_in = inv_std * (
        scaled
        - jnp.mean(scaled, axis=-1, keepdims=True)
        - x_hat * jnp.mean(scaled * x_hat, axis=-1, keepdims=True)
    )
    return (grad_in, jnp.sum(incoming * x_hat, axis=0), jnp.sum(incoming, axis=0))


def gelu_slope(pre_act):
    return (
        0.5 * (1.0 + lax.erf(pre_act * 0.7071067811865476))
        + pre_act * jnp.exp(-0.5 * pre_act * pre_act) * 0.3989422804014327
    )


def online_update(running, query_heads, query_seg, key_rows, value_rows, key_seg):
    accum, run_max, run_sum = running
    rows_here = key_rows.shape[0]
    scores = 0.125 * jnp.einsum(
        "qhd,khd->hqk",
        query_heads,
        key_rows.reshape(rows_here, H, HD),
        preferred_element_type=jnp.float32,
    )
    same_seg = (query_seg[:, None] == key_seg[None, :])[None]
    masked = jnp.where(same_seg, scores, -1e30)
    new_max = jnp.maximum(run_max, jnp.max(masked, axis=-1))
    scale_old = jnp.exp(run_max - new_max)
    exp_scores = jnp.where(same_seg, jnp.exp(masked - new_max[:, :, None]), 0.0)
    run_sum = run_sum * scale_old + jnp.sum(exp_scores, axis=-1)
    update = jnp.einsum(
        "hqk,khd->qhd",
        exp_scores.astype(jnp.bfloat16),
        value_rows.reshape(rows_here, H, HD),
        preferred_element_type=jnp.float32,
    )
    accum = accum * scale_old.T[:, :, None] + update
    return (accum, new_max, run_sum)


def pair_grads(query_rows, grad_rows, log_sum, delta_row, query_seg, key_rows, value_rows, key_seg):
    q_heads = query_rows.reshape(-1, H, HD)
    g_heads = grad_rows.reshape(-1, H, HD)
    k_heads = key_rows.reshape(-1, H, HD)
    v_heads = value_rows.reshape(-1, H, HD)
    scores = 0.125 * jnp.einsum(
        "qhd,khd->hqk", q_heads, k_heads, preferred_element_type=jnp.float32
    )
    same_seg = (query_seg[:, None] == key_seg[None, :])[None]
    probs = jnp.where(
        same_seg, jnp.exp(jnp.where(same_seg, scores, -1e30) - log_sum[:, :, None]), 0.0
    )
    grad_prob = jnp.einsum("qhd,khd->hqk", g_heads, v_heads, preferred_element_type=jnp.float32)
    grad_score = (probs * (grad_prob - delta_row[:, :, None])).astype(jnp.bfloat16)
    grad_q = 0.125 * jnp.einsum(
        "hqk,khd->qhd", grad_score, k_heads, preferred_element_type=jnp.float32
    )
    grad_k = 0.125 * jnp.einsum(
        "hqk,qhd->khd", grad_score, q_heads, preferred_element_type=jnp.float32
    )
    grad_v = jnp.einsum(
        "hqk,qhd->khd", probs.astype(jnp.bfloat16), g_heads, preferred_element_type=jnp.float32
    )
    return (
        grad_q.reshape(query_rows.shape),
        grad_k.reshape(key_rows.shape),
        grad_v.reshape(key_rows.shape),
    )


def owner_rows(layer_in, layer_grad):
    return lax.psum_scatter(
        lax.dot_general(
            layer_in, layer_grad, (((0,), (0,)), ((), ())), preferred_element_type=jnp.float32
        ).astype(jnp.bfloat16),
        "fsdp",
        scatter_dimension=0,
        tiled=True,
    ).astype(jnp.float32)


def body(
    tokens,
    lengths,
    packing,
    query_w,
    query_b,
    key_w,
    value_w,
    value_b,
    output_w,
    output_b,
    attn_gain,
    attn_shift,
    expand_w,
    expand_b,
    reduce_w,
    reduce_b,
    ffn_gain,
    ffn_shift,
    cotangent,
):
    tok_shape = tokens.shape
    stripe = tok_shape[2]
    block_len = tok_shape[1] * tok_shape[2]
    model_width = tok_shape[3]
    n_ctx = lax.axis_size("ctx")
    ctx_index = lax.axis_index("ctx")
    seq_lens = lengths[0]
    slot_ids = packing[0]
    ordered = jnp.sum(
        jnp.where(
            slot_ids[:, None] == jnp.arange(seq_lens.shape[0], dtype=jnp.int32)[None, :],
            seq_lens[None, :],
            0,
        ),
        axis=1,
    )
    slot_ends = jnp.cumsum(ordered)
    gathered = jnp.arange(n_ctx * block_len, dtype=jnp.int32)
    owner_dev = gathered // block_len
    local_row = gathered % block_len
    position = local_row // stripe * (stripe * n_ctx) + owner_dev * stripe + local_row % stripe
    seg_all = jnp.sum((position[:, None] >= slot_ends[None, :]).astype(jnp.int32), axis=1)
    query_seg = lax.dynamic_slice_in_dim(seg_all, ctx_index * block_len, block_len)
    inputs = tokens.reshape(block_len, model_width)
    w_query, w_key, w_value, w_output, w_up, w_down = (
        lax.all_gather(query_w, "fsdp", axis=0, tiled=True),
        lax.all_gather(key_w, "fsdp", axis=0, tiled=True),
        lax.all_gather(value_w, "fsdp", axis=0, tiled=True),
        lax.all_gather(output_w, "fsdp", axis=0, tiled=True),
        lax.all_gather(expand_w, "fsdp", axis=0, tiled=True),
        lax.all_gather(reduce_w, "fsdp", axis=0, tiled=True),
    )
    queries = (dense(inputs, w_query) + query_b).astype(jnp.bfloat16)
    key_rows = dense(inputs, w_key).astype(jnp.bfloat16)
    values = (dense(inputs, w_value) + value_b).astype(jnp.bfloat16)
    query_heads = queries.reshape(block_len, H, HD)
    start_state = (
        jnp.zeros((block_len, H, HD), jnp.float32),
        jnp.full((H, block_len), -1e30, jnp.float32),
        jnp.zeros((H, block_len), jnp.float32),
    )
    key_piece = lax.all_gather(key_rows, "ctx", axis=0, tiled=True)
    value_piece = lax.all_gather(values, "ctx", axis=0, tiled=True)
    shards = key_piece.shape[0] // block_len

    def one_shard(index, inner):
        key_part = lax.dynamic_slice_in_dim(key_piece, index * block_len, block_len)
        value_part = lax.dynamic_slice_in_dim(value_piece, index * block_len, block_len)
        key_seg = lax.dynamic_slice_in_dim(seg_all, index * block_len, block_len)
        return online_update(inner, query_heads, query_seg, key_part, value_part, key_seg)

    accum, run_max, run_sum = lax.fori_loop(0, shards, one_shard, start_state)
    attended = (accum / run_sum.T[:, :, None]).reshape(block_len, model_width).astype(jnp.bfloat16)
    log_sum = run_max + jnp.log(run_sum)
    branch = dense(attended, w_output) + output_b
    normed, x_hat1, inv_std1 = norm_fwd(inputs.astype(jnp.float32) + branch, attn_gain, attn_shift)
    normed_low = normed.astype(jnp.bfloat16)
    pre_act = dense(normed_low, w_up) + expand_b
    hidden = jax.nn.gelu(pre_act, approximate=False).astype(jnp.bfloat16)
    ffn_out = dense(hidden, w_down) + reduce_b
    outputs, x_hat2, inv_std2 = norm_fwd(normed + ffn_out, ffn_gain, ffn_shift)
    layer_out = outputs.astype(jnp.bfloat16).reshape(tok_shape)
    upstream = cotangent.reshape(block_len, model_width).astype(jnp.float32)
    grad_mid2, grad_ffn_gain, grad_ffn_shift = norm_back(upstream, x_hat2, inv_std2, ffn_gain)
    grad_ffn = grad_mid2.astype(jnp.bfloat16)
    grad_reduce_b = jnp.sum(grad_ffn.astype(jnp.float32), axis=0)
    share_down = owner_rows(hidden, grad_ffn)
    grad_pre = (dense_back(grad_ffn, w_down) * gelu_slope(pre_act)).astype(jnp.bfloat16)
    grad_expand_b = jnp.sum(grad_pre.astype(jnp.float32), axis=0)
    share_up = owner_rows(normed_low, grad_pre)
    grad_normed = dense_back(grad_pre, w_up) + grad_mid2
    grad_mid1, grad_attn_gain, grad_attn_shift = norm_back(grad_normed, x_hat1, inv_std1, attn_gain)
    grad_branch = grad_mid1.astype(jnp.bfloat16)
    grad_output_b = jnp.sum(grad_branch.astype(jnp.float32), axis=0)
    share_out = owner_rows(attended, grad_branch)
    grad_att = dense_back(grad_branch, w_output).astype(jnp.bfloat16)
    delta_row = jnp.einsum(
        "qhd,qhd->hq",
        grad_att.astype(jnp.float32).reshape(block_len, H, HD),
        attended.astype(jnp.float32).reshape(block_len, H, HD),
    )
    zero_rows = jnp.zeros((block_len, model_width), jnp.float32)

    def key_step(step, state):
        visit_keys, visit_values, sum_k, sum_v, sum_q = state
        anchor = (ctx_index - step) % n_ctx
        key_seg = lax.dynamic_slice_in_dim(seg_all, anchor * block_len, block_len)
        part_q, part_k, part_v = pair_grads(
            queries, grad_att, log_sum, delta_row, query_seg, visit_keys, visit_values, key_seg
        )
        sum_q = sum_q + part_q
        visit_keys, visit_values = from_behind((visit_keys, visit_values), "ctx", 1)
        sum_k, sum_v = (
            from_behind((sum_k + part_k).astype(jnp.bfloat16), "ctx", 1).astype(jnp.float32),
            from_behind((sum_v + part_v).astype(jnp.bfloat16), "ctx", 1).astype(jnp.float32),
        )
        return (visit_keys, visit_values, sum_k, sum_v, sum_q)

    final = lax.fori_loop(0, n_ctx, key_step, (key_rows, values, zero_rows, zero_rows, zero_rows))
    sum_k, sum_v, sum_q = (final[2], final[3], final[4])
    grad_q = sum_q.astype(jnp.bfloat16)
    grad_k = sum_k.astype(jnp.bfloat16)
    grad_v = sum_v.astype(jnp.bfloat16)
    grad_query_b = jnp.sum(grad_q.astype(jnp.float32), axis=0)
    grad_value_b = jnp.sum(grad_v.astype(jnp.float32), axis=0)
    share_query = owner_rows(inputs, grad_q)
    share_key = owner_rows(inputs, grad_k)
    share_value = owner_rows(inputs, grad_v)
    grad_inputs = (
        dense_back(grad_q, w_query)
        + dense_back(grad_k, w_key)
        + dense_back(grad_v, w_value)
        + grad_mid1
    )
    share_query, share_key, share_value, share_out, share_up, share_down = lax.psum(
        (share_query, share_key, share_value, share_out, share_up, share_down), "ctx"
    )
    (
        grad_query_b,
        grad_value_b,
        grad_output_b,
        grad_attn_gain,
        grad_attn_shift,
        grad_expand_b,
        grad_reduce_b,
        grad_ffn_gain,
        grad_ffn_shift,
    ) = lax.psum(
        (
            grad_query_b,
            grad_value_b,
            grad_output_b,
            grad_attn_gain,
            grad_attn_shift,
            grad_expand_b,
            grad_reduce_b,
            grad_ffn_gain,
            grad_ffn_shift,
        ),
        ("ctx", "fsdp"),
    )
    return (
        layer_out,
        grad_inputs.reshape(tok_shape),
        share_query,
        grad_query_b,
        share_key,
        share_value,
        grad_value_b,
        share_out,
        grad_output_b,
        grad_attn_gain,
        grad_attn_shift,
        share_up,
        grad_expand_b,
        share_down,
        grad_reduce_b,
        grad_ffn_gain,
        grad_ffn_shift,
    )


def solution(mesh):
    return jax.shard_map(
        body,
        mesh=mesh,
        in_specs=(
            P("fsdp", None, "ctx", None),
            P("fsdp", None),
            P("fsdp", None),
            P("fsdp", None),
            P(),
            P("fsdp", None),
            P("fsdp", None),
            P(),
            P("fsdp", None),
            P(),
            P(),
            P(),
            P("fsdp", None),
            P(),
            P("fsdp", None),
            P(),
            P(),
            P(),
            P("fsdp", None, "ctx", None),
        ),
        out_specs=(
            P("fsdp", None, "ctx", None),
            P("fsdp", None, "ctx", None),
            P("fsdp", None),
            P(),
            P("fsdp", None),
            P("fsdp", None),
            P(),
            P("fsdp", None),
            P(),
            P(),
            P(),
            P("fsdp", None),
            P(),
            P("fsdp", None),
            P(),
            P(),
            P(),
        ),
        check_vma=False,
    )
```

profile of v0, /device:TPU:0, one launch (start us, length us, event | category | flops | bytes accessed | tf_op | source)
XLA Modules:
  0.0 1580.3 jit_solution(11764506689131481254)
XLA Ops:
  9.5 25.4 %all-gather.9.cloned.1.call-done = bf16[1024,1024]{1,0:T(8,128)(2,1)} async-done(((bf16[256,1024]{1,0:T(8,128)(2,1)}), bf16[1024,1024]{1,0:T(8,128)(2,1)}) %all-gather.9.cloned.1.call-update) | async-done | bytes 2097168 | tf_op jit(solution)/shard_map/all_gather | solution.py:165
  38.3 20.8 %all-gather.15.cloned.1.call-done = bf16[1024,1024]{1,0:T(8,128)(2,1)} async-done(((bf16[256,1024]{1,0:T(8,128)(2,1)}), bf16[1024,1024]{1,0:T(8,128)(2,1)}) %all-gather.15.cloned.1.call-update) | async-done | bytes 2097168 | tf_op jit(solution)/shard_map/all_gather | solution.py:166
  67.9 15.4 all-gather.13.cloned.1.call-done
  85.8 73.5 %all-gather.11.cloned.1.call-done = bf16[2048,1024]{1,0:T(8,128)(2,1)} async-done(((bf16[256,1024]{1,0:T(8,128)(2,1)}), bf16[2048,1024]{1,0:T(8,128)(2,1)}) %all-gather.11.cloned.1.call-update) | async-done | bytes 4194320 | tf_op jit(solution)/shard_map/all_gather | solution.py:180
  159.3 74.2 %all-gather.17.cloned.1.call-done = bf16[2048,1024]{1,0:T(8,128)(2,1)} async-done(((bf16[256,1024]{1,0:T(8,128)(2,1)}), bf16[2048,1024]{1,0:T(8,128)(2,1)}) %all-gather.17.cloned.1.call-update) | async-done | bytes 4194320 | tf_op jit(solution)/shard_map/all_gather | solution.py:181
  233.5 103.5 %while.42 = (s32[]{:T(128)}, f32[256,16,64]{0,2,1:T(8,128)}, f32[16,256]{1,0:T(8,128)S(1)}, f32[16,256]{1,0:T(8,128)S(1)}, s32[256]{0:T(256)S(1)}, /*index=5*/s3...) while((s32[]{:T(128)}, f32[256,16,64]{0,2,1:T(8,128)}, ...), condition=%wide.region_6.7_spmd.clone, body=%wide.region_3.6_spmd.clone.sunk | while | flops 282943488 | bytes 20975804 | solution.py:190
  267.2 5.8 fusion.155
  341.4 15.5 fusion.29
  356.9 18.7 %all-gather.23.cloned.1.call-done = bf16[4096,1024]{1,0:T(8,128)(2,1)} async-done(((bf16[1024,1024]{1,0:T(8,128)(2,1)}), bf16[4096,1024]{1,0:T(8,128)(2,1)}) %all-gather.23.cloned.1.call-update) | async-done | bytes 8388624 | tf_op jit(solution)/shard_map/all_gather | solution.py:169
  375.6 6.6 fusion.88
  393.9 406.9 %while.43 = (s32[]{:T(128)}, bf16[256,1024]{0,1:T(8,128)(2,1)}, bf16[256,1024]{0,1:T(8,128)(2,1)}, f32[256,1024]{0,1:T(8,128)}, f32[256,1024]{0,1:T(8,128)}, /*i...) while((s32[]{:T(128)}, bf16[256,1024]{0,1:T(8,128)(2,1)}, ...), condition=%wide.region_16.17_spmd.clone, body=%wide.region_15.16_spmd.clone.sunk | while | flops 686882816 | bytes 68932264 | solution.py:237
  414.1 21.3 %collective-permute-done.2 = bf16[256,1024]{0,1:T(8,128)(2,1)} collective-permute-done((bf16[256,1024]{0,1:T(8,128)(2,1)}, bf16[256,1024]{0,1:T(8,128)(2,1)}, u32[]{:S(2)}, u32[]{:S(2)}) %collective-permute-start.2) | collective-permute-done | bytes 524320 | tf_op jit(solution)/shard_map/while/body/eval_jaxpr/ppermute | solution.py:13
  437.5 8.5 collective-permute-done.3
  466.3 23.2 %collective-permute-done.2 = bf16[256,1024]{0,1:T(8,128)(2,1)} collective-permute-done((bf16[256,1024]{0,1:T(8,128)(2,1)}, bf16[256,1024]{0,1:T(8,128)(2,1)}, u32[]{:S(2)}, u32[]{:S(2)}) %collective-permute-start.2) | collective-permute-done | bytes 524320 | tf_op jit(solution)/shard_map/while/body/eval_jaxpr/ppermute | solution.py:13
  491.6 7.6 collective-permute-done.3
  517.6 25.0 %collective-permute-done.2 = bf16[256,1024]{0,1:T(8,128)(2,1)} collective-permute-done((bf16[256,1024]{0,1:T(8,128)(2,1)}, bf16[256,1024]{0,1:T(8,128)(2,1)}, u32[]{:S(2)}, u32[]{:S(2)}) %collective-permute-start.2) | collective-permute-done | bytes 524320 | tf_op jit(solution)/shard_map/while/body/eval_jaxpr/ppermute | solution.py:13
  544.7 6.6 collective-permute-done.3
  568.1 26.8 %collective-permute-done.2 = bf16[256,1024]{0,1:T(8,128)(2,1)} collective-permute-done((bf16[256,1024]{0,1:T(8,128)(2,1)}, bf16[256,1024]{0,1:T(8,128)(2,1)}, u32[]{:S(2)}, u32[]{:S(2)}) %collective-permute-start.2) | collective-permute-done | bytes 524320 | tf_op jit(solution)/shard_map/while/body/eval_jaxpr/ppermute | solution.py:13
  597.0 5.7 collective-permute-done.3
  619.0 27.2 %collective-permute-done.2 = bf16[256,1024]{0,1:T(8,128)(2,1)} collective-permute-done((bf16[256,1024]{0,1:T(8,128)(2,1)}, bf16[256,1024]{0,1:T(8,128)(2,1)}, u32[]{:S(2)}, u32[]{:S(2)}) %collective-permute-start.2) | collective-permute-done | bytes 524320 | tf_op jit(solution)/shard_map/while/body/eval_jaxpr/ppermute | solution.py:13
  648.3 4.8 collective-permute-done.3
  669.3 27.2 %collective-permute-done.2 = bf16[256,1024]{0,1:T(8,128)(2,1)} collective-permute-done((bf16[256,1024]{0,1:T(8,128)(2,1)}, bf16[256,1024]{0,1:T(8,128)(2,1)}, u32[]{:S(2)}, u32[]{:S(2)}) %collective-permute-start.2) | collective-permute-done | bytes 524320 | tf_op jit(solution)/shard_map/while/body/eval_jaxpr/ppermute | solution.py:13
  718.8 26.7 %collective-permute-done.2 = bf16[256,1024]{0,1:T(8,128)(2,1)} collective-permute-done((bf16[256,1024]{0,1:T(8,128)(2,1)}, bf16[256,1024]{0,1:T(8,128)(2,1)}, u32[]{:S(2)}, u32[]{:S(2)}) %collective-permute-start.2) | collective-permute-done | bytes 524320 | tf_op jit(solution)/shard_map/while/body/eval_jaxpr/ppermute | solution.py:13
  767.4 25.7 %collective-permute-done.2 = bf16[256,1024]{0,1:T(8,128)(2,1)} collective-permute-done((bf16[256,1024]{0,1:T(8,128)(2,1)}, bf16[256,1024]{0,1:T(8,128)(2,1)}, u32[]{:S(2)}, u32[]{:S(2)}) %collective-permute-start.2) | collective-permute-done | bytes 524320 | tf_op jit(solution)/shard_map/while/body/eval_jaxpr/ppermute | solution.py:13
  812.5 7.3 convolution_convert_fusion.1
  821.0 7.2 convolution_convert_fusion
  829.7 38.5 %all-reduce = (f32[1024]{0:T(1024)}, f32[1024]{0:T(1024)}, f32[1024]{0:T(1024)}, f32[1024]{0:T(1024)}, f32[1024]{0:T(1024)}, /*index=5*/f32[4096]{0:T(1024)}, f32[1024]{0:T(1024)}, f32[1024]{0:T(1024)}, f32[1024]{0:T(1024)}) all-reduce(f32[1024]{0:T(1024)S(1)} %convert_reduce_fusion.5, ...), channel_id=1, replica_groups=mesh['ctx'=8,'fsdp'=4] {'ctx','fsdp'}, use_global_device_ids=true, to_apply=%region_20.21 | all-reduce | flops 12288 | bytes 98304 | tf_op jit(solution)/shard_map/psum | solution.py:266
  874.9 26.7 %reduce-scatter.11.cloned.1.call-done = bf16[256,1024]{0,1:T(8,128)(2,1)} async-done(((bf16[1024,1024]{0,1:T(8,128)(2,1)}), bf16[256,1024]{0,1:T(8,128)(2,1)}) %reduce-scatter.11.cloned.1.call-update) | async-done | bytes 524304 | tf_op jit(solution)/shard_map/reduce_scatter | solution.py:108
  901.6 34.0 %reduce-scatter.13.cloned.1.call-done = bf16[256,1024]{1,0:T(8,128)(2,1)} async-done(((bf16[1024,1024]{1,0:T(8,128)(2,1)}), bf16[256,1024]{1,0:T(8,128)(2,1)}) %reduce-scatter.13.cloned.1.call-update) | async-done | bytes 524304 | tf_op jit(solution)/shard_map/reduce_scatter | solution.py:108
  935.5 74.3 %reduce-scatter.15.cloned.1.call-done = bf16[256,4096]{1,0:T(8,128)(2,1)} async-done(((bf16[1024,4096]{1,0:T(8,128)(2,1)}), bf16[256,4096]{1,0:T(8,128)(2,1)}) %reduce-scatter.15.cloned.1.call-update) | async-done | bytes 2097168 | tf_op jit(solution)/shard_map/reduce_scatter | solution.py:108
  1009.9 74.4 %reduce-scatter.17.cloned.1.call-done = bf16[1024,1024]{1,0:T(8,128)(2,1)} async-done(((bf16[4096,1024]{1,0:T(8,128)(2,1)}), bf16[1024,1024]{1,0:T(8,128)(2,1)}) %reduce-scatter.17.cloned.1.call-update) | async-done | bytes 2097168 | tf_op jit(solution)/shard_map/reduce_scatter | solution.py:108
  1084.2 485.2 %all-reduce.3 = (f32[256,1024]{0,1:T(8,128)S(1)}, f32[256,1024]{0,1:T(8,128)S(1)}, f32[256,1024]{0,1:T(8,128)S(1)}, f32[256,1024]{1,0:T(8,128)}, f32[256,4096]{1,0:T(8,128)}, /*index=5*/f32[1024,1024]{1,0:T(8,128)}) all-reduce(bf16[256,1024]{0,1:T(8,128)(2,1)} %reduce-scatter.7.cloned.1.call-done, ...), channel_id=1, replica_groups=mesh['ctx'=8,'fsdp'=4] {'ctx'}, use_global_device_ids=true, to_apply=%region_18.19 | all-reduce | flops 3145728 | bytes 18874368 | tf_op jit(solution)/shard_map/psum | solution.py:253
  (503 shorter events, 323.9 us)
Async XLA Ops:
  7.9 51.2 %all-gather.15.cloned.1.call-start = ((), (), s32[]{:S(2)}) async-start(), calls=%async_computation.9 | async-start | bytes 2621440 | tf_op jit(solution)/shard_map/all_gather | solution.py:166
  8.7 74.6 %all-gather.13.cloned.1.call-start = ((), (), s32[]{:S(2)}) async-start(), calls=%async_computation.8 | async-start | bytes 2621440 | tf_op jit(solution)/shard_map/all_gather | solution.py:164
  9.4 149.9 %all-gather.11.cloned.1.call-start = ((), (), s32[]{:S(2)}) async-start(), calls=%async_computation.7 | async-start | bytes 4718592 | tf_op jit(solution)/shard_map/all_gather | solution.py:180
  38.3 195.3 %all-gather.17.cloned.1.call-start = ((), (), s32[]{:S(2)}) async-start(), calls=%async_computation.10 | async-start | bytes 4718592 | tf_op jit(solution)/shard_map/all_gather | solution.py:181
  62.2 276.2 %all-gather.19.cloned.1.call-start = ((), (), s32[]{:S(2)}) async-start(), calls=%async_computation.11 | async-start | bytes 2621440 | tf_op jit(solution)/shard_map/all_gather | solution.py:167
  62.8 278.6 %all-gather.21.cloned.1.call-start = ((), (), s32[]{:S(2)}) async-start(), calls=%async_computation.12 | async-start | bytes 10485760 | tf_op jit(solution)/shard_map/all_gather | solution.py:168
  63.6 312.0 %all-gather.23.cloned.1.call-start = ((), (), s32[]{:S(2)}) async-start(), calls=%async_computation.13 | async-start | bytes 10485760 | tf_op jit(solution)/shard_map/all_gather | solution.py:169
  64.3 810.5 %reduce-scatter.7.cloned.1.call-start = ((), (), s32[]{:S(2)}) async-start(), calls=%async_computation.14 | async-start | bytes 2621440 | tf_op jit(solution)/shard_map/reduce_scatter | solution.py:108
  395.4 52.7 %collective-permute-start = (bf16[256,1024]{0,1:T(8,128)(2,1)S(1)}, bf16[256,1024]{0,1:T(8,128)(2,1)}, u32[]{:S(2)}, u32[]{:S(2)}) collective-permute-start(bf16[256,1024]{0,1:T(8,128)(2,1)S(1)} %copy.106), channel_id=1, source_target_pairs={{28,0},{0,4},{4,8},{8,12},{12,16},{16,20},{20,24},{24,28},{29,1},{... | collective-permute-start | bytes 1572872 | tf_op jit(solution)/shard_map/while/body/eval_jaxpr/ppermute | solution.py:13
  398.7 49.4 %collective-permute-start.1 = (bf16[256,1024]{0,1:T(8,128)(2,1)}, bf16[256,1024]{0,1:T(8,128)(2,1)}, u32[]{:S(2)}, u32[]{:S(2)}) collective-permute-start(bf16[256,1024]{0,1:T(8,128)(2,1)} %copy.107), channel_id=1, source_target_pairs={{28,0},{0,4},{4,8},{8,12},{12,16},{16,20},{20,24},{24,28},{29,1},{... | collective-permute-start | bytes 1572872 | tf_op jit(solution)/shard_map/while/body/eval_jaxpr/ppermute | solution.py:13
  449.4 51.9 %collective-permute-start = (bf16[256,1024]{0,1:T(8,128)(2,1)S(1)}, bf16[256,1024]{0,1:T(8,128)(2,1)}, u32[]{:S(2)}, u32[]{:S(2)}) collective-permute-start(bf16[256,1024]{0,1:T(8,128)(2,1)S(1)} %copy.106), channel_id=1, source_target_pairs={{28,0},{0,4},{4,8},{8,12},{12,16},{16,20},{20,24},{24,28},{29,1},{... | collective-permute-start | bytes 1572872 | tf_op jit(solution)/shard_map/while/body/eval_jaxpr/ppermute | solution.py:13
  451.2 50.0 %collective-permute-start.1 = (bf16[256,1024]{0,1:T(8,128)(2,1)}, bf16[256,1024]{0,1:T(8,128)(2,1)}, u32[]{:S(2)}, u32[]{:S(2)}) collective-permute-start(bf16[256,1024]{0,1:T(8,128)(2,1)} %copy.107), channel_id=1, source_target_pairs={{28,0},{0,4},{4,8},{8,12},{12,16},{16,20},{20,24},{24,28},{29,1},{... | collective-permute-start | bytes 1572872 | tf_op jit(solution)/shard_map/while/body/eval_jaxpr/ppermute | solution.py:13
  462.4 36.7 %collective-permute-start.3 = (bf16[256,1024]{0,1:T(8,128)(2,1)}, bf16[256,1024]{0,1:T(8,128)(2,1)}, u32[]{:S(2)}, u32[]{:S(2)}) collective-permute-start(bf16[256,1024]{0,1:T(8,128)(2,1)} %fusion.171), channel_id=1, source_target_pairs={{28,0},{0,4},{4,8},{8,12},{12,16},{16,20},{20,24},{24,28},{29,1},{... | collective-permute-start | bytes 1572872 | tf_op jit(solution)/shard_map/while/body/eval_jaxpr/ppermute | solution.py:13
  502.5 51.0 %collective-permute-start = (bf16[256,1024]{0,1:T(8,128)(2,1)S(1)}, bf16[256,1024]{0,1:T(8,128)(2,1)}, u32[]{:S(2)}, u32[]{:S(2)}) collective-permute-start(bf16[256,1024]{0,1:T(8,128)(2,1)S(1)} %copy.106), channel_id=1, source_target_pairs={{28,0},{0,4},{4,8},{8,12},{12,16},{16,20},{20,24},{24,28},{29,1},{... | collective-permute-start | bytes 1572872 | tf_op jit(solution)/shard_map/while/body/eval_jaxpr/ppermute | solution.py:13
  504.4 49.1 %collective-permute-start.1 = (bf16[256,1024]{0,1:T(8,128)(2,1)}, bf16[256,1024]{0,1:T(8,128)(2,1)}, u32[]{:S(2)}, u32[]{:S(2)}) collective-permute-start(bf16[256,1024]{0,1:T(8,128)(2,1)} %copy.107), channel_id=1, source_target_pairs={{28,0},{0,4},{4,8},{8,12},{12,16},{16,20},{20,24},{24,28},{29,1},{... | collective-permute-start | bytes 1572872 | tf_op jit(solution)/shard_map/while/body/eval_jaxpr/ppermute | solution.py:13
  514.0 37.4 %collective-permute-start.3 = (bf16[256,1024]{0,1:T(8,128)(2,1)}, bf16[256,1024]{0,1:T(8,128)(2,1)}, u32[]{:S(2)}, u32[]{:S(2)}) collective-permute-start(bf16[256,1024]{0,1:T(8,128)(2,1)} %fusion.171), channel_id=1, source_target_pairs={{28,0},{0,4},{4,8},{8,12},{12,16},{16,20},{20,24},{24,28},{29,1},{... | collective-permute-start | bytes 1572872 | tf_op jit(solution)/shard_map/while/body/eval_jaxpr/ppermute | solution.py:13
  554.7 50.0 %collective-permute-start = (bf16[256,1024]{0,1:T(8,128)(2,1)S(1)}, bf16[256,1024]{0,1:T(8,128)(2,1)}, u32[]{:S(2)}, u32[]{:S(2)}) collective-permute-start(bf16[256,1024]{0,1:T(8,128)(2,1)S(1)} %copy.106), channel_id=1, source_target_pairs={{28,0},{0,4},{4,8},{8,12},{12,16},{16,20},{20,24},{24,28},{29,1},{... | collective-permute-start | bytes 1572872 | tf_op jit(solution)/shard_map/while/body/eval_jaxpr/ppermute | solution.py:13
  556.6 48.2 %collective-permute-start.1 = (bf16[256,1024]{0,1:T(8,128)(2,1)}, bf16[256,1024]{0,1:T(8,128)(2,1)}, u32[]{:S(2)}, u32[]{:S(2)}) collective-permute-start(bf16[256,1024]{0,1:T(8,128)(2,1)} %copy.107), channel_id=1, source_target_pairs={{28,0},{0,4},{4,8},{8,12},{12,16},{16,20},{20,24},{24,28},{29,1},{... | collective-permute-start | bytes 1572872 | tf_op jit(solution)/shard_map/while/body/eval_jaxpr/ppermute | solution.py:13
  566.2 36.5 %collective-permute-start.3 = (bf16[256,1024]{0,1:T(8,128)(2,1)}, bf16[256,1024]{0,1:T(8,128)(2,1)}, u32[]{:S(2)}, u32[]{:S(2)}) collective-permute-start(bf16[256,1024]{0,1:T(8,128)(2,1)} %fusion.171), channel_id=1, source_target_pairs={{28,0},{0,4},{4,8},{8,12},{12,16},{16,20},{20,24},{24,28},{29,1},{... | collective-permute-start | bytes 1572872 | tf_op jit(solution)/shard_map/while/body/eval_jaxpr/ppermute | solution.py:13
  606.1 49.1 %collective-permute-start = (bf16[256,1024]{0,1:T(8,128)(2,1)S(1)}, bf16[256,1024]{0,1:T(8,128)(2,1)}, u32[]{:S(2)}, u32[]{:S(2)}) collective-permute-start(bf16[256,1024]{0,1:T(8,128)(2,1)S(1)} %copy.106), channel_id=1, source_target_pairs={{28,0},{0,4},{4,8},{8,12},{12,16},{16,20},{20,24},{24,28},{29,1},{... | collective-permute-start | bytes 1572872 | tf_op jit(solution)/shard_map/while/body/eval_jaxpr/ppermute | solution.py:13
  607.9 47.2 %collective-permute-start.1 = (bf16[256,1024]{0,1:T(8,128)(2,1)}, bf16[256,1024]{0,1:T(8,128)(2,1)}, u32[]{:S(2)}, u32[]{:S(2)}) collective-permute-start(bf16[256,1024]{0,1:T(8,128)(2,1)} %copy.107), channel_id=1, source_target_pairs={{28,0},{0,4},{4,8},{8,12},{12,16},{16,20},{20,24},{24,28},{29,1},{... | collective-permute-start | bytes 1572872 | tf_op jit(solution)/shard_map/while/body/eval_jaxpr/ppermute | solution.py:13
  656.5 48.2 %collective-permute-start = (bf16[256,1024]{0,1:T(8,128)(2,1)S(1)}, bf16[256,1024]{0,1:T(8,128)(2,1)}, u32[]{:S(2)}, u32[]{:S(2)}) collective-permute-start(bf16[256,1024]{0,1:T(8,128)(2,1)S(1)} %copy.106), channel_id=1, source_target_pairs={{28,0},{0,4},{4,8},{8,12},{12,16},{16,20},{20,24},{24,28},{29,1},{... | collective-permute-start | bytes 1572872 | tf_op jit(solution)/shard_map/while/body/eval_jaxpr/ppermute | solution.py:13
  658.3 46.3 %collective-permute-start.1 = (bf16[256,1024]{0,1:T(8,128)(2,1)}, bf16[256,1024]{0,1:T(8,128)(2,1)}, u32[]{:S(2)}, u32[]{:S(2)}) collective-permute-start(bf16[256,1024]{0,1:T(8,128)(2,1)} %copy.107), channel_id=1, source_target_pairs={{28,0},{0,4},{4,8},{8,12},{12,16},{16,20},{20,24},{24,28},{29,1},{... | collective-permute-start | bytes 1572872 | tf_op jit(solution)/shard_map/while/body/eval_jaxpr/ppermute | solution.py:13
  705.9 47.3 %collective-permute-start = (bf16[256,1024]{0,1:T(8,128)(2,1)S(1)}, bf16[256,1024]{0,1:T(8,128)(2,1)}, u32[]{:S(2)}, u32[]{:S(2)}) collective-permute-start(bf16[256,1024]{0,1:T(8,128)(2,1)S(1)} %copy.106), channel_id=1, source_target_pairs={{28,0},{0,4},{4,8},{8,12},{12,16},{16,20},{20,24},{24,28},{29,1},{... | collective-permute-start | bytes 1572872 | tf_op jit(solution)/shard_map/while/body/eval_jaxpr/ppermute | solution.py:13
  707.8 45.4 %collective-permute-start.1 = (bf16[256,1024]{0,1:T(8,128)(2,1)}, bf16[256,1024]{0,1:T(8,128)(2,1)}, u32[]{:S(2)}, u32[]{:S(2)}) collective-permute-start(bf16[256,1024]{0,1:T(8,128)(2,1)} %copy.107), channel_id=1, source_target_pairs={{28,0},{0,4},{4,8},{8,12},{12,16},{16,20},{20,24},{24,28},{29,1},{... | collective-permute-start | bytes 1572872 | tf_op jit(solution)/shard_map/while/body/eval_jaxpr/ppermute | solution.py:13
  754.5 46.3 %collective-permute-start = (bf16[256,1024]{0,1:T(8,128)(2,1)S(1)}, bf16[256,1024]{0,1:T(8,128)(2,1)}, u32[]{:S(2)}, u32[]{:S(2)}) collective-permute-start(bf16[256,1024]{0,1:T(8,128)(2,1)S(1)} %copy.106), channel_id=1, source_target_pairs={{28,0},{0,4},{4,8},{8,12},{12,16},{16,20},{20,24},{24,28},{29,1},{... | collective-permute-start | bytes 1572872 | tf_op jit(solution)/shard_map/while/body/eval_jaxpr/ppermute | solution.py:13
  756.3 44.5 %collective-permute-start.1 = (bf16[256,1024]{0,1:T(8,128)(2,1)}, bf16[256,1024]{0,1:T(8,128)(2,1)}, u32[]{:S(2)}, u32[]{:S(2)}) collective-permute-start(bf16[256,1024]{0,1:T(8,128)(2,1)} %copy.107), channel_id=1, source_target_pairs={{28,0},{0,4},{4,8},{8,12},{12,16},{16,20},{20,24},{24,28},{29,1},{... | collective-permute-start | bytes 1572872 | tf_op jit(solution)/shard_map/while/body/eval_jaxpr/ppermute | solution.py:13
  804.4 70.5 %reduce-scatter.9.cloned.1.call-start = ((), (), s32[]{:S(2)}) async-start(), calls=%async_computation.15 | async-start | bytes 2621440 | tf_op jit(solution)/shard_map/reduce_scatter | solution.py:108
  806.5 95.0 %reduce-scatter.11.cloned.1.call-start = ((), (), s32[]{:S(2)}) async-start(), calls=%async_computation.16 | async-start | bytes 2621440 | tf_op jit(solution)/shard_map/reduce_scatter | solution.py:108
  808.7 126.8 %reduce-scatter.13.cloned.1.call-start = ((), (), s32[]{:S(2)}) async-start(), calls=%async_computation.17 | async-start | bytes 2621440 | tf_op jit(solution)/shard_map/reduce_scatter | solution.py:108
  812.4 197.5 %reduce-scatter.15.cloned.1.call-start = ((), (), s32[]{:S(2)}) async-start(), calls=%async_computation.18 | async-start | bytes 10485760 | tf_op jit(solution)/shard_map/reduce_scatter | solution.py:108
  819.8 264.4 %reduce-scatter.17.cloned.1.call-start = ((), (), s32[]{:S(2)}) async-start(), calls=%async_computation.19 | async-start | bytes 10485760 | tf_op jit(solution)/shard_map/reduce_scatter | solution.py:108
  (98 other events, 1656.0 us)
Sparse Core Ops, SparseCore 0:
  9.6 25.2 all-gather.8
  36.5 22.5 all-gather.14
  60.7 22.5 all-gather.12
  85.8 73.3 all-gather.10
  161.8 71.6 all-gather.16
  234.9 20.8 all-gather.18
  257.4 58.2 all-gather.20
  317.3 58.2 all-gather.22
  804.5 27.8 reduce-scatter.6
  835.0 32.4 reduce-scatter.8
  870.0 31.5 reduce-scatter.10
  904.1 31.3 reduce-scatter.12
  938.1 71.7 reduce-scatter.14
  1012.5 71.6 reduce-scatter.16
where the time goes:
time: 1590 us; the launch traced here: 1580 us
  waiting for transfers between devices  689 us (43%)
  blocking collectives  524 us (33%)
  matrix products  194 us (12%)
  other arithmetic  85.1 us (5%)
  local copies, waits for them, and re-layouts  59 us (4%)
    psum x1, blocking collectives, body(): lax.psum((share_query, share_key, share_value, share_out, share_up, share...  485 us
    ppermute x32, waiting for transfers between devices, from_behind(): return lax.ppermute(block, axis, route)  247 us
    reduce_scatter x6, waiting for transfers between devices, owner_rows(): lax.psum_scatter(lax.dot_general(layer_in, layer_grad, (((0,), (0,)), (()...  209 us
    all_gather x1, waiting for transfers between devices, body(): value_piece = lax.all_gather(values, 'ctx', axis=0, tiled=True)  74.2 us
    all_gather x1, waiting for transfers between devices, body(): key_piece = lax.all_gather(key_rows, 'ctx', axis=0, tiled=True)  73.5 us
    psum x1, blocking collectives, body(): lax.psum((grad_query_b, grad_value_b, grad_output_b, grad_attn_gain, grad...  38.5 us
    dot_general x8, matrix products, online_update(): jnp.einsum('hqk,khd->qhd', exp_scores.astype(jnp.bfloat16), value_rows.re...  37.9 us
    while x120, local copies, waits for them, and re-layouts  34.6 us
  transfers between devices with their start and end apart: 46, of which 26 were waited for; matrix products, arithmetic and copies ran while one was open for 18% of the time, Pallas kernels for 0%

commit v1 on v0

--- a/solution.py
+++ b/solution.py
@@ -152,7 +152,8 @@
         ),
         axis=1,
     )
-    slot_ends = jnp.cumsum(ordered)
+    slots = jnp.arange(seq_lens.shape[0], dtype=jnp.int32)
+    slot_ends = jnp.sum(jnp.where(slots[None, :] <= slots[:, None], ordered[None, :], 0), axis=1)
     gathered = jnp.arange(n_ctx * block_len, dtype=jnp.int32)
     owner_dev = gathered // block_len
     local_row = gathered % block_len

time: 1590 us -> 1590 us (level)
  no operation moved by 1% of the time
where the time goes in v1:
time: 1590 us; the launch traced here: 1580 us
  waiting for transfers between devices  689 us (43%)
  blocking collectives  524 us (33%)
  matrix products  194 us (12%)
  other arithmetic  85.1 us (5%)
  local copies, waits for them, and re-layouts  59 us (4%)
    psum x1, blocking collectives, body(): lax.psum((share_query, share_key, share_value, share_out, share_up, share...  485 us
    ppermute x32, waiting for transfers between devices, from_behind(): return lax.ppermute(block, axis, route)  247 us
    reduce_scatter x6, waiting for transfers between devices, owner_rows(): lax.psum_scatter(lax.dot_general(layer_in, layer_grad, (((0,), (0,)), (()...  209 us
    all_gather x1, waiting for transfers between devices, body(): value_piece = lax.all_gather(values, 'ctx', axis=0, tiled=True)  74.2 us
    all_gather x1, waiting for transfers between devices, body(): key_piece = lax.all_gather(key_rows, 'ctx', axis=0, tiled=True)  73.5 us
    psum x1, blocking collectives, body(): lax.psum((grad_query_b, grad_value_b, grad_output_b, grad_attn_gain, grad...  38.5 us
    dot_general x8, matrix products, online_update(): jnp.einsum('hqk,khd->qhd', exp_scores.astype(jnp.bfloat16), value_rows.re...  37.9 us
    while x120, local copies, waits for them, and re-layouts  34.6 us
  transfers between devices with their start and end apart: 46, of which 26 were waited for; matrix products, arithmetic and copies ran while one was open for 18% of the time, Pallas kernels for 0%

profile of v1, /device:TPU:0, one launch (start us, length us, event | category | flops | bytes accessed | tf_op | source)
XLA Modules:
  0.0 1580.4 jit_solution(7767871707761352350)
XLA Ops:
  9.5 25.4 %all-gather.9.cloned.1.call-done = bf16[1024,1024]{1,0:T(8,128)(2,1)} async-done(((bf16[256,1024]{1,0:T(8,128)(2,1)}), bf16[1024,1024]{1,0:T(8,128)(2,1)}) %all-gather.9.cloned.1.call-update) | async-done | bytes 2097168 | tf_op jit(solution)/shard_map/all_gather | solution.py:166
  38.3 20.8 %all-gather.15.cloned.1.call-done = bf16[1024,1024]{1,0:T(8,128)(2,1)} async-done(((bf16[256,1024]{1,0:T(8,128)(2,1)}), bf16[1024,1024]{1,0:T(8,128)(2,1)}) %all-gather.15.cloned.1.call-update) | async-done | bytes 2097168 | tf_op jit(solution)/shard_map/all_gather | solution.py:167
  67.9 15.4 all-gather.13.cloned.1.call-done
  85.8 73.5 %all-gather.11.cloned.1.call-done = bf16[2048,1024]{1,0:T(8,128)(2,1)} async-done(((bf16[256,1024]{1,0:T(8,128)(2,1)}), bf16[2048,1024]{1,0:T(8,128)(2,1)}) %all-gather.11.cloned.1.call-update) | async-done | bytes 4194320 | tf_op jit(solution)/shard_map/all_gather | solution.py:181
  159.3 74.2 %all-gather.17.cloned.1.call-done = bf16[2048,1024]{1,0:T(8,128)(2,1)} async-done(((bf16[256,1024]{1,0:T(8,128)(2,1)}), bf16[2048,1024]{1,0:T(8,128)(2,1)}) %all-gather.17.cloned.1.call-update) | async-done | bytes 4194320 | tf_op jit(solution)/shard_map/all_gather | solution.py:182
  233.6 103.5 %while.42 = (s32[]{:T(128)}, f32[256,16,64]{0,2,1:T(8,128)}, f32[16,256]{1,0:T(8,128)S(1)}, f32[16,256]{1,0:T(8,128)S(1)}, s32[256]{0:T(256)S(1)}, /*index=5*/s3...) while((s32[]{:T(128)}, f32[256,16,64]{0,2,1:T(8,128)}, ...), condition=%wide.region_6.7_spmd.clone, body=%wide.region_3.6_spmd.clone.sunk | while | flops 282943488 | bytes 20975804 | solution.py:191
  267.2 5.8 fusion.155
  341.4 15.5 fusion.29
  356.9 18.7 %all-gather.23.cloned.1.call-done = bf16[4096,1024]{1,0:T(8,128)(2,1)} async-done(((bf16[1024,1024]{1,0:T(8,128)(2,1)}), bf16[4096,1024]{1,0:T(8,128)(2,1)}) %all-gather.23.cloned.1.call-update) | async-done | bytes 8388624 | tf_op jit(solution)/shard_map/all_gather | solution.py:170
  375.6 6.6 fusion.88
  393.9 406.9 %while.43 = (s32[]{:T(128)}, bf16[256,1024]{0,1:T(8,128)(2,1)}, bf16[256,1024]{0,1:T(8,128)(2,1)}, f32[256,1024]{0,1:T(8,128)}, f32[256,1024]{0,1:T(8,128)}, /*i...) while((s32[]{:T(128)}, bf16[256,1024]{0,1:T(8,128)(2,1)}, ...), condition=%wide.region_16.17_spmd.clone, body=%wide.region_15.16_spmd.clone.sunk | while | flops 686882816 | bytes 68932264 | solution.py:238
  414.1 21.3 %collective-permute-done.2 = bf16[256,1024]{0,1:T(8,128)(2,1)} collective-permute-done((bf16[256,1024]{0,1:T(8,128)(2,1)}, bf16[256,1024]{0,1:T(8,128)(2,1)}, u32[]{:S(2)}, u32[]{:S(2)}) %collective-permute-start.2) | collective-permute-done | bytes 524320 | tf_op jit(solution)/shard_map/while/body/eval_jaxpr/ppermute | solution.py:13
  437.5 8.5 collective-permute-done.3
  466.3 23.2 %collective-permute-done.2 = bf16[256,1024]{0,1:T(8,128)(2,1)} collective-permute-done((bf16[256,1024]{0,1:T(8,128)(2,1)}, bf16[256,1024]{0,1:T(8,128)(2,1)}, u32[]{:S(2)}, u32[]{:S(2)}) %collective-permute-start.2) | collective-permute-done | bytes 524320 | tf_op jit(solution)/shard_map/while/body/eval_jaxpr/ppermute | solution.py:13
  491.6 7.6 collective-permute-done.3
  517.7 25.0 %collective-permute-done.2 = bf16[256,1024]{0,1:T(8,128)(2,1)} collective-permute-done((bf16[256,1024]{0,1:T(8,128)(2,1)}, bf16[256,1024]{0,1:T(8,128)(2,1)}, u32[]{:S(2)}, u32[]{:S(2)}) %collective-permute-start.2) | collective-permute-done | bytes 524320 | tf_op jit(solution)/shard_map/while/body/eval_jaxpr/ppermute | solution.py:13
  544.8 6.6 collective-permute-done.3
  568.0 26.8 %collective-permute-done.2 = bf16[256,1024]{0,1:T(8,128)(2,1)} collective-permute-done((bf16[256,1024]{0,1:T(8,128)(2,1)}, bf16[256,1024]{0,1:T(8,128)(2,1)}, u32[]{:S(2)}, u32[]{:S(2)}) %collective-permute-start.2) | collective-permute-done | bytes 524320 | tf_op jit(solution)/shard_map/while/body/eval_jaxpr/ppermute | solution.py:13
  597.0 5.7 collective-permute-done.3
  619.0 27.2 %collective-permute-done.2 = bf16[256,1024]{0,1:T(8,128)(2,1)} collective-permute-done((bf16[256,1024]{0,1:T(8,128)(2,1)}, bf16[256,1024]{0,1:T(8,128)(2,1)}, u32[]{:S(2)}, u32[]{:S(2)}) %collective-permute-start.2) | collective-permute-done | bytes 524320 | tf_op jit(solution)/shard_map/while/body/eval_jaxpr/ppermute | solution.py:13
  648.3 4.8 collective-permute-done.3
  669.3 27.2 %collective-permute-done.2 = bf16[256,1024]{0,1:T(8,128)(2,1)} collective-permute-done((bf16[256,1024]{0,1:T(8,128)(2,1)}, bf16[256,1024]{0,1:T(8,128)(2,1)}, u32[]{:S(2)}, u32[]{:S(2)}) %collective-permute-start.2) | collective-permute-done | bytes 524320 | tf_op jit(solution)/shard_map/while/body/eval_jaxpr/ppermute | solution.py:13
  718.8 26.7 %collective-permute-done.2 = bf16[256,1024]{0,1:T(8,128)(2,1)} collective-permute-done((bf16[256,1024]{0,1:T(8,128)(2,1)}, bf16[256,1024]{0,1:T(8,128)(2,1)}, u32[]{:S(2)}, u32[]{:S(2)}) %collective-permute-start.2) | collective-permute-done | bytes 524320 | tf_op jit(solution)/shard_map/while/body/eval_jaxpr/ppermute | solution.py:13
  767.4 25.7 %collective-permute-done.2 = bf16[256,1024]{0,1:T(8,128)(2,1)} collective-permute-done((bf16[256,1024]{0,1:T(8,128)(2,1)}, bf16[256,1024]{0,1:T(8,128)(2,1)}, u32[]{:S(2)}, u32[]{:S(2)}) %collective-permute-start.2) | collective-permute-done | bytes 524320 | tf_op jit(solution)/shard_map/while/body/eval_jaxpr/ppermute | solution.py:13
  812.5 7.3 convolution_convert_fusion.1
  821.0 7.2 convolution_convert_fusion
  829.7 38.5 %all-reduce = (f32[1024]{0:T(1024)}, f32[1024]{0:T(1024)}, f32[1024]{0:T(1024)}, f32[1024]{0:T(1024)}, f32[1024]{0:T(1024)}, /*index=5*/f32[4096]{0:T(1024)}, f32[1024]{0:T(1024)}, f32[1024]{0:T(1024)}, f32[1024]{0:T(1024)}) all-reduce(f32[1024]{0:T(1024)S(1)} %convert_reduce_fusion.5, ...), channel_id=1, replica_groups=mesh['ctx'=8,'fsdp'=4] {'ctx','fsdp'}, use_global_device_ids=true, to_apply=%region_20.21 | all-reduce | flops 12288 | bytes 98304 | tf_op jit(solution)/shard_map/psum | solution.py:267
  874.9 26.8 %reduce-scatter.11.cloned.1.call-done = bf16[256,1024]{0,1:T(8,128)(2,1)} async-done(((bf16[1024,1024]{0,1:T(8,128)(2,1)}), bf16[256,1024]{0,1:T(8,128)(2,1)}) %reduce-scatter.11.cloned.1.call-update) | async-done | bytes 524304 | tf_op jit(solution)/shard_map/reduce_scatter | solution.py:108
  901.6 34.0 %reduce-scatter.13.cloned.1.call-done = bf16[256,1024]{1,0:T(8,128)(2,1)} async-done(((bf16[1024,1024]{1,0:T(8,128)(2,1)}), bf16[256,1024]{1,0:T(8,128)(2,1)}) %reduce-scatter.13.cloned.1.call-update) | async-done | bytes 524304 | tf_op jit(solution)/shard_map/reduce_scatter | solution.py:108
  935.6 74.3 %reduce-scatter.15.cloned.1.call-done = bf16[256,4096]{1,0:T(8,128)(2,1)} async-done(((bf16[1024,4096]{1,0:T(8,128)(2,1)}), bf16[256,4096]{1,0:T(8,128)(2,1)}) %reduce-scatter.15.cloned.1.call-update) | async-done | bytes 2097168 | tf_op jit(solution)/shard_map/reduce_scatter | solution.py:108
  1009.9 74.4 %reduce-scatter.17.cloned.1.call-done = bf16[1024,1024]{1,0:T(8,128)(2,1)} async-done(((bf16[4096,1024]{1,0:T(8,128)(2,1)}), bf16[1024,1024]{1,0:T(8,128)(2,1)}) %reduce-scatter.17.cloned.1.call-update) | async-done | bytes 2097168 | tf_op jit(solution)/shard_map/reduce_scatter | solution.py:108
  1084.3 485.2 %all-reduce.3 = (f32[256,1024]{0,1:T(8,128)S(1)}, f32[256,1024]{0,1:T(8,128)S(1)}, f32[256,1024]{0,1:T(8,128)S(1)}, f32[256,1024]{1,0:T(8,128)}, f32[256,4096]{1,0:T(8,128)}, /*index=5*/f32[1024,1024]{1,0:T(8,128)}) all-reduce(bf16[256,1024]{0,1:T(8,128)(2,1)} %reduce-scatter.7.cloned.1.call-done, ...), channel_id=1, replica_groups=mesh['ctx'=8,'fsdp'=4] {'ctx'}, use_global_device_ids=true, to_apply=%region_18.19 | all-reduce | flops 3145728 | bytes 18874368 | tf_op jit(solution)/shard_map/psum | solution.py:254
  (503 shorter events, 323.8 us)
Async XLA Ops:
  7.9 51.2 %all-gather.15.cloned.1.call-start = ((), (), s32[]{:S(2)}) async-start(), calls=%async_computation.9 | async-start | bytes 2621440 | tf_op jit(solution)/shard_map/all_gather | solution.py:167
  8.7 74.6 %all-gather.13.cloned.1.call-start = ((), (), s32[]{:S(2)}) async-start(), calls=%async_computation.8 | async-start | bytes 2621440 | tf_op jit(solution)/shard_map/all_gather | solution.py:165
  9.4 149.9 %all-gather.11.cloned.1.call-start = ((), (), s32[]{:S(2)}) async-start(), calls=%async_computation.7 | async-start | bytes 4718592 | tf_op jit(solution)/shard_map/all_gather | solution.py:181
  38.3 195.3 %all-gather.17.cloned.1.call-start = ((), (), s32[]{:S(2)}) async-start(), calls=%async_computation.10 | async-start | bytes 4718592 | tf_op jit(solution)/shard_map/all_gather | solution.py:182
  62.2 276.2 %all-gather.19.cloned.1.call-start = ((), (), s32[]{:S(2)}) async-start(), calls=%async_computation.11 | async-start | bytes 2621440 | tf_op jit(solution)/shard_map/all_gather | solution.py:168
  62.8 278.6 %all-gather.21.cloned.1.call-start = ((), (), s32[]{:S(2)}) async-start(), calls=%async_computation.12 | async-start | bytes 10485760 | tf_op jit(solution)/shard_map/all_gather | solution.py:169
  63.6 312.1 %all-gather.23.cloned.1.call-start = ((), (), s32[]{:S(2)}) async-start(), calls=%async_computation.13 | async-start | bytes 10485760 | tf_op jit(solution)/shard_map/all_gather | solution.py:170
  64.3 810.5 %reduce-scatter.7.cloned.1.call-start = ((), (), s32[]{:S(2)}) async-start(), calls=%async_computation.14 | async-start | bytes 2621440 | tf_op jit(solution)/shard_map/reduce_scatter | solution.py:108
  395.4 52.7 %collective-permute-start = (bf16[256,1024]{0,1:T(8,128)(2,1)S(1)}, bf16[256,1024]{0,1:T(8,128)(2,1)}, u32[]{:S(2)}, u32[]{:S(2)}) collective-permute-start(bf16[256,1024]{0,1:T(8,128)(2,1)S(1)} %copy.106), channel_id=1, source_target_pairs={{28,0},{0,4},{4,8},{8,12},{12,16},{16,20},{20,24},{24,28},{29,1},{... | collective-permute-start | bytes 1572872 | tf_op jit(solution)/shard_map/while/body/eval_jaxpr/ppermute | solution.py:13
  398.8 49.3 %collective-permute-start.1 = (bf16[256,1024]{0,1:T(8,128)(2,1)}, bf16[256,1024]{0,1:T(8,128)(2,1)}, u32[]{:S(2)}, u32[]{:S(2)}) collective-permute-start(bf16[256,1024]{0,1:T(8,128)(2,1)} %copy.107), channel_id=1, source_target_pairs={{28,0},{0,4},{4,8},{8,12},{12,16},{16,20},{20,24},{24,28},{29,1},{... | collective-permute-start | bytes 1572872 | tf_op jit(solution)/shard_map/while/body/eval_jaxpr/ppermute | solution.py:13
  449.4 51.9 %collective-permute-start = (bf16[256,1024]{0,1:T(8,128)(2,1)S(1)}, bf16[256,1024]{0,1:T(8,128)(2,1)}, u32[]{:S(2)}, u32[]{:S(2)}) collective-permute-start(bf16[256,1024]{0,1:T(8,128)(2,1)S(1)} %copy.106), channel_id=1, source_target_pairs={{28,0},{0,4},{4,8},{8,12},{12,16},{16,20},{20,24},{24,28},{29,1},{... | collective-permute-start | bytes 1572872 | tf_op jit(solution)/shard_map/while/body/eval_jaxpr/ppermute | solution.py:13
  451.2 50.0 %collective-permute-start.1 = (bf16[256,1024]{0,1:T(8,128)(2,1)}, bf16[256,1024]{0,1:T(8,128)(2,1)}, u32[]{:S(2)}, u32[]{:S(2)}) collective-permute-start(bf16[256,1024]{0,1:T(8,128)(2,1)} %copy.107), channel_id=1, source_target_pairs={{28,0},{0,4},{4,8},{8,12},{12,16},{16,20},{20,24},{24,28},{29,1},{... | collective-permute-start | bytes 1572872 | tf_op jit(solution)/shard_map/while/body/eval_jaxpr/ppermute | solution.py:13
  462.5 36.7 %collective-permute-start.3 = (bf16[256,1024]{0,1:T(8,128)(2,1)}, bf16[256,1024]{0,1:T(8,128)(2,1)}, u32[]{:S(2)}, u32[]{:S(2)}) collective-permute-start(bf16[256,1024]{0,1:T(8,128)(2,1)} %fusion.171), channel_id=1, source_target_pairs={{28,0},{0,4},{4,8},{8,12},{12,16},{16,20},{20,24},{24,28},{29,1},{... | collective-permute-start | bytes 1572872 | tf_op jit(solution)/shard_map/while/body/eval_jaxpr/ppermute | solution.py:13
  502.5 51.0 %collective-permute-start = (bf16[256,1024]{0,1:T(8,128)(2,1)S(1)}, bf16[256,1024]{0,1:T(8,128)(2,1)}, u32[]{:S(2)}, u32[]{:S(2)}) collective-permute-start(bf16[256,1024]{0,1:T(8,128)(2,1)S(1)} %copy.106), channel_id=1, source_target_pairs={{28,0},{0,4},{4,8},{8,12},{12,16},{16,20},{20,24},{24,28},{29,1},{... | collective-permute-start | bytes 1572872 | tf_op jit(solution)/shard_map/while/body/eval_jaxpr/ppermute | solution.py:13
  504.4 49.1 %collective-permute-start.1 = (bf16[256,1024]{0,1:T(8,128)(2,1)}, bf16[256,1024]{0,1:T(8,128)(2,1)}, u32[]{:S(2)}, u32[]{:S(2)}) collective-permute-start(bf16[256,1024]{0,1:T(8,128)(2,1)} %copy.107), channel_id=1, source_target_pairs={{28,0},{0,4},{4,8},{8,12},{12,16},{16,20},{20,24},{24,28},{29,1},{... | collective-permute-start | bytes 1572872 | tf_op jit(solution)/shard_map/while/body/eval_jaxpr/ppermute | solution.py:13
  514.0 37.4 %collective-permute-start.3 = (bf16[256,1024]{0,1:T(8,128)(2,1)}, bf16[256,1024]{0,1:T(8,128)(2,1)}, u32[]{:S(2)}, u32[]{:S(2)}) collective-permute-start(bf16[256,1024]{0,1:T(8,128)(2,1)} %fusion.171), channel_id=1, source_target_pairs={{28,0},{0,4},{4,8},{8,12},{12,16},{16,20},{20,24},{24,28},{29,1},{... | collective-permute-start | bytes 1572872 | tf_op jit(solution)/shard_map/while/body/eval_jaxpr/ppermute | solution.py:13
  554.8 50.0 %collective-permute-start = (bf16[256,1024]{0,1:T(8,128)(2,1)S(1)}, bf16[256,1024]{0,1:T(8,128)(2,1)}, u32[]{:S(2)}, u32[]{:S(2)}) collective-permute-start(bf16[256,1024]{0,1:T(8,128)(2,1)S(1)} %copy.106), channel_id=1, source_target_pairs={{28,0},{0,4},{4,8},{8,12},{12,16},{16,20},{20,24},{24,28},{29,1},{... | collective-permute-start | bytes 1572872 | tf_op jit(solution)/shard_map/while/body/eval_jaxpr/ppermute | solution.py:13
  556.6 48.2 %collective-permute-start.1 = (bf16[256,1024]{0,1:T(8,128)(2,1)}, bf16[256,1024]{0,1:T(8,128)(2,1)}, u32[]{:S(2)}, u32[]{:S(2)}) collective-permute-start(bf16[256,1024]{0,1:T(8,128)(2,1)} %copy.107), channel_id=1, source_target_pairs={{28,0},{0,4},{4,8},{8,12},{12,16},{16,20},{20,24},{24,28},{29,1},{... | collective-permute-start | bytes 1572872 | tf_op jit(solution)/shard_map/while/body/eval_jaxpr/ppermute | solution.py:13
  566.2 36.5 %collective-permute-start.3 = (bf16[256,1024]{0,1:T(8,128)(2,1)}, bf16[256,1024]{0,1:T(8,128)(2,1)}, u32[]{:S(2)}, u32[]{:S(2)}) collective-permute-start(bf16[256,1024]{0,1:T(8,128)(2,1)} %fusion.171), channel_id=1, source_target_pairs={{28,0},{0,4},{4,8},{8,12},{12,16},{16,20},{20,24},{24,28},{29,1},{... | collective-permute-start | bytes 1572872 | tf_op jit(solution)/shard_map/while/body/eval_jaxpr/ppermute | solution.py:13
  606.1 49.1 %collective-permute-start = (bf16[256,1024]{0,1:T(8,128)(2,1)S(1)}, bf16[256,1024]{0,1:T(8,128)(2,1)}, u32[]{:S(2)}, u32[]{:S(2)}) collective-permute-start(bf16[256,1024]{0,1:T(8,128)(2,1)S(1)} %copy.106), channel_id=1, source_target_pairs={{28,0},{0,4},{4,8},{8,12},{12,16},{16,20},{20,24},{24,28},{29,1},{... | collective-permute-start | bytes 1572872 | tf_op jit(solution)/shard_map/while/body/eval_jaxpr/ppermute | solution.py:13
  607.9 47.2 %collective-permute-start.1 = (bf16[256,1024]{0,1:T(8,128)(2,1)}, bf16[256,1024]{0,1:T(8,128)(2,1)}, u32[]{:S(2)}, u32[]{:S(2)}) collective-permute-start(bf16[256,1024]{0,1:T(8,128)(2,1)} %copy.107), channel_id=1, source_target_pairs={{28,0},{0,4},{4,8},{8,12},{12,16},{16,20},{20,24},{24,28},{29,1},{... | collective-permute-start | bytes 1572872 | tf_op jit(solution)/shard_map/while/body/eval_jaxpr/ppermute | solution.py:13
  656.5 48.2 %collective-permute-start = (bf16[256,1024]{0,1:T(8,128)(2,1)S(1)}, bf16[256,1024]{0,1:T(8,128)(2,1)}, u32[]{:S(2)}, u32[]{:S(2)}) collective-permute-start(bf16[256,1024]{0,1:T(8,128)(2,1)S(1)} %copy.106), channel_id=1, source_target_pairs={{28,0},{0,4},{4,8},{8,12},{12,16},{16,20},{20,24},{24,28},{29,1},{... | collective-permute-start | bytes 1572872 | tf_op jit(solution)/shard_map/while/body/eval_jaxpr/ppermute | solution.py:13
  658.3 46.3 %collective-permute-start.1 = (bf16[256,1024]{0,1:T(8,128)(2,1)}, bf16[256,1024]{0,1:T(8,128)(2,1)}, u32[]{:S(2)}, u32[]{:S(2)}) collective-permute-start(bf16[256,1024]{0,1:T(8,128)(2,1)} %copy.107), channel_id=1, source_target_pairs={{28,0},{0,4},{4,8},{8,12},{12,16},{16,20},{20,24},{24,28},{29,1},{... | collective-permute-start | bytes 1572872 | tf_op jit(solution)/shard_map/while/body/eval_jaxpr/ppermute | solution.py:13
  705.9 47.3 %collective-permute-start = (bf16[256,1024]{0,1:T(8,128)(2,1)S(1)}, bf16[256,1024]{0,1:T(8,128)(2,1)}, u32[]{:S(2)}, u32[]{:S(2)}) collective-permute-start(bf16[256,1024]{0,1:T(8,128)(2,1)S(1)} %copy.106), channel_id=1, source_target_pairs={{28,0},{0,4},{4,8},{8,12},{12,16},{16,20},{20,24},{24,28},{29,1},{... | collective-permute-start | bytes 1572872 | tf_op jit(solution)/shard_map/while/body/eval_jaxpr/ppermute | solution.py:13
  707.8 45.4 %collective-permute-start.1 = (bf16[256,1024]{0,1:T(8,128)(2,1)}, bf16[256,1024]{0,1:T(8,128)(2,1)}, u32[]{:S(2)}, u32[]{:S(2)}) collective-permute-start(bf16[256,1024]{0,1:T(8,128)(2,1)} %copy.107), channel_id=1, source_target_pairs={{28,0},{0,4},{4,8},{8,12},{12,16},{16,20},{20,24},{24,28},{29,1},{... | collective-permute-start | bytes 1572872 | tf_op jit(solution)/shard_map/while/body/eval_jaxpr/ppermute | solution.py:13
  754.5 46.3 %collective-permute-start = (bf16[256,1024]{0,1:T(8,128)(2,1)S(1)}, bf16[256,1024]{0,1:T(8,128)(2,1)}, u32[]{:S(2)}, u32[]{:S(2)}) collective-permute-start(bf16[256,1024]{0,1:T(8,128)(2,1)S(1)} %copy.106), channel_id=1, source_target_pairs={{28,0},{0,4},{4,8},{8,12},{12,16},{16,20},{20,24},{24,28},{29,1},{... | collective-permute-start | bytes 1572872 | tf_op jit(solution)/shard_map/while/body/eval_jaxpr/ppermute | solution.py:13
  756.3 44.5 %collective-permute-start.1 = (bf16[256,1024]{0,1:T(8,128)(2,1)}, bf16[256,1024]{0,1:T(8,128)(2,1)}, u32[]{:S(2)}, u32[]{:S(2)}) collective-permute-start(bf16[256,1024]{0,1:T(8,128)(2,1)} %copy.107), channel_id=1, source_target_pairs={{28,0},{0,4},{4,8},{8,12},{12,16},{16,20},{20,24},{24,28},{29,1},{... | collective-permute-start | bytes 1572872 | tf_op jit(solution)/shard_map/while/body/eval_jaxpr/ppermute | solution.py:13
  804.4 70.5 %reduce-scatter.9.cloned.1.call-start = ((), (), s32[]{:S(2)}) async-start(), calls=%async_computation.15 | async-start | bytes 2621440 | tf_op jit(solution)/shard_map/reduce_scatter | solution.py:108
  806.5 95.1 %reduce-scatter.11.cloned.1.call-start = ((), (), s32[]{:S(2)}) async-start(), calls=%async_computation.16 | async-start | bytes 2621440 | tf_op jit(solution)/shard_map/reduce_scatter | solution.py:108
  808.7 126.9 %reduce-scatter.13.cloned.1.call-start = ((), (), s32[]{:S(2)}) async-start(), calls=%async_computation.17 | async-start | bytes 2621440 | tf_op jit(solution)/shard_map/reduce_scatter | solution.py:108
  812.4 197.5 %reduce-scatter.15.cloned.1.call-start = ((), (), s32[]{:S(2)}) async-start(), calls=%async_computation.18 | async-start | bytes 10485760 | tf_op jit(solution)/shard_map/reduce_scatter | solution.py:108
  819.8 264.5 %reduce-scatter.17.cloned.1.call-start = ((), (), s32[]{:S(2)}) async-start(), calls=%async_computation.19 | async-start | bytes 10485760 | tf_op jit(solution)/shard_map/reduce_scatter | solution.py:108
  (98 other events, 1655.8 us)
Sparse Core Ops, SparseCore 0:
  9.6 25.2 all-gather.8
  36.5 22.5 all-gather.14
  60.7 22.5 all-gather.12
  85.8 73.4 all-gather.10
  161.9 71.6 all-gather.16
  235.0 20.8 all-gather.18
  257.4 58.2 all-gather.20
  317.3 58.2 all-gather.22
  804.5 27.9 reduce-scatter.6
  835.0 32.4 reduce-scatter.8
  870.1 31.5 reduce-scatter.10
  904.2 31.3 reduce-scatter.12
  938.2 71.7 reduce-scatter.14
  1012.6 71.7 reduce-scatter.16

commit v2 on v1

v2 whole, which is shorter than its diff:
```python
import functools
import jax
import jax.numpy as jnp
from jax import lax
from jax.experimental import pallas as pl
from jax.experimental.pallas import tpu as pltpu
from jax.sharding import PartitionSpec as P

H = 16
HD = 64
PAIR = 2 * HD
GROUP = 8
SWAP = (0, 2, 1, 3)
BF = jnp.bfloat16
F32 = jnp.float32


def dense(left, right):
    return jnp.dot(left, right, preferred_element_type=F32)


def dense_back(left, right):
    return lax.dot_general(left, right, (((1,), (1,)), ((), ())), preferred_element_type=F32)


def dense_in(left, right):
    return lax.dot_general(left, right, (((0,), (0,)), ((), ())), preferred_element_type=F32)


def norm_fwd(hidden, gain, shift):
    mean_row = jnp.mean(hidden, axis=-1, keepdims=True)
    centred = hidden - mean_row
    variance = jnp.mean(centred * centred, axis=-1, keepdims=True)
    inv_std = lax.rsqrt(variance + 1e-05)
    x_hat = centred * inv_std
    return (x_hat * gain + shift, x_hat, inv_std)


def norm_back(incoming, x_hat, inv_std, gain):
    scaled = incoming * gain
    grad_in = inv_std * (
        scaled
        - jnp.mean(scaled, axis=-1, keepdims=True)
        - x_hat * jnp.mean(scaled * x_hat, axis=-1, keepdims=True)
    )
    return (grad_in, jnp.sum(incoming * x_hat, axis=0), jnp.sum(incoming, axis=0))


def gelu_slope(pre_act):
    return (
        0.5 * (1.0 + lax.erf(pre_act * 0.7071067811865476))
        + pre_act * jnp.exp(-0.5 * pre_act * pre_act) * 0.3989422804014327
    )


def first_half(shape):
    return lax.broadcasted_iota(jnp.int32, shape, 1) < HD


def both_heads(block):
    left = first_half(block.shape)
    zero = jnp.zeros_like(block)
    return jnp.concatenate([jnp.where(left, block, zero), jnp.where(left, zero, block)], axis=0)


def by_head(stacked):
    rows = stacked.shape[0] // 2
    left = first_half((rows, stacked.shape[1]))
    return jnp.where(left, stacked[:rows], stacked[rows:])


def attend_kernel(bq, bk, chunks, lo_ref, hi_ref, q_ref, k_ref, v_ref, sq_ref, sk_ref, o_ref, lse_ref):
    nq = q_ref.shape[0] // bq
    per_chunk = k_ref.shape[0] // chunks // bk

    def q_step(i, carry):
        rows = pl.ds(pl.multiple_of(i * bq, bq), bq)
        q2 = both_heads(q_ref[rows, :] * BF(0.125))
        seg = sq_ref[rows, :]
        seg2 = jnp.concatenate([seg, seg], axis=0)

        def k_step(j, state):
            accum, run_max, run_sum = state
            keys = pl.ds(pl.multiple_of(j * bk, bk), bk)
            scores = dense_back(q2, k_ref[keys, :])
            same = seg2 == sk_ref[:, keys]
            scores = jnp.where(same, scores, -1e30)
            new_max = jnp.maximum(run_max, jnp.max(scores, axis=1, keepdims=True))
            probs = jnp.where(same, jnp.exp(scores - new_max), 0.0)
            scale = jnp.exp(run_max - new_max)
            run_sum = run_sum * scale + jnp.sum(probs, axis=1, keepdims=True)
            accum = accum * scale + dense(probs.astype(BF), v_ref[keys, :])
            return accum, new_max, run_sum

        state = (
            jnp.zeros((2 * bq, PAIR), F32),
            jnp.full((2 * bq, 1), -1e30, F32),
            jnp.zeros((2 * bq, 1), F32),
        )
        for s in range(chunks):
            base = s * per_chunk
            state = lax.fori_loop(base + lo_ref[i, s], base + hi_ref[i, s], k_step, state)
        accum, run_max, run_sum = state
        o_ref[rows, :] = by_head(accum / run_sum).astype(BF)
        lse_ref[pl.ds(pl.multiple_of(2 * i * bq, 2 * bq), 2 * bq), :] = run_max + jnp.log(run_sum)
        return carry

    lax.fori_loop(0, nq, q_step, 0)


def attend_back_kernel(
    bq, bk, chunks, lo_ref, hi_ref, q_ref, k_ref, v_ref, sq_ref, sk_ref, o_ref, lse_ref, g_ref,
    dq_ref, dk_ref, dv_ref, dk_sum, dv_sum,
):
    nq = q_ref.shape[0] // bq
    per_chunk = k_ref.shape[0] // chunks // bk
    dk_sum[...] = jnp.zeros_like(dk_sum)
    dv_sum[...] = jnp.zeros_like(dv_sum)

    def q_step(i, carry):
        rows = pl.ds(pl.multiple_of(i * bq, bq), bq)
        q2 = both_heads(q_ref[rows, :] * BF(0.125))
        grad = g_ref[rows, :]
        g2 = both_heads(grad)
        prod = grad.astype(F32) * o_ref[rows, :].astype(F32)
        left = first_half(prod.shape)
        delta = jnp.concatenate(
            [
                jnp.sum(jnp.where(left, prod, 0.0), axis=1, keepdims=True),
                jnp.sum(jnp.where(left, 0.0, prod), axis=1, keepdims=True),
            ],
            axis=0,
        )
        lse = lse_ref[pl.ds(pl.multiple_of(2 * i * bq, 2 * bq), 2 * bq), :]
        seg = sq_ref[rows, :]
        seg2 = jnp.concatenate([seg, seg], axis=0)

        def k_step(j, dq2):
            keys = pl.ds(pl.multiple_of(j * bk, bk), bk)
            key_rows = k_ref[keys, :]
            scores = dense_back(q2, key_rows)
            same = seg2 == sk_ref[:, keys]
            probs = jnp.where(same, jnp.exp(jnp.where(same, scores, -1e30) - lse), 0.0)
            grad_prob = dense_back(g2, v_ref[keys, :])
            grad_score = (probs * (grad_prob - delta)).astype(BF)
            dv_sum[keys, :] += dense_in(probs.astype(BF), g2)
            dk_sum[keys, :] += dense_in(grad_score, q2)
            return dq2 + dense(grad_score, key_rows)

        dq2 = jnp.zeros((2 * bq, PAIR), F32)
        for s in range(chunks):
            base = s * per_chunk
            dq2 = lax.fori_loop(base + lo_ref[i, s], base + hi_ref[i, s], k_step, dq2)
        dq_ref[rows, :] = (0.125 * by_head(dq2)).astype(BF)
        return carry

    lax.fori_loop(0, nq, q_step, 0)
    dk_ref[...] = dk_sum[...].astype(dk_ref.dtype)
    dv_ref[...] = dv_sum[...].astype(dv_ref.dtype)


SMEM = pl.BlockSpec(memory_space=pltpu.SMEM)
VMEM = pl.BlockSpec(memory_space=pltpu.VMEM)
BQ = 256
BK = 256


def attend(bounds, q, k, v, seg_q, seg_k, chunks):
    n = q.shape[0]
    return pl.pallas_call(
        functools.partial(attend_kernel, BQ, BK, chunks),
        out_shape=(jax.ShapeDtypeStruct((n, PAIR), BF), jax.ShapeDtypeStruct((2 * n, 1), F32)),
        in_specs=[SMEM, SMEM] + [VMEM] * 5,
        out_specs=(VMEM, VMEM),
        compiler_params=pltpu.CompilerParams(vmem_limit_bytes=48 * 2**20),
    )(*bounds, q, k, v, seg_q, seg_k)


def attend_back(bounds, q, k, v, seg_q, seg_k, out, lse, grad, chunks):
    n, m = q.shape[0], k.shape[0]
    kept = BF if chunks == 1 else F32
    return pl.pallas_call(
        functools.partial(attend_back_kernel, BQ, BK, chunks),
        out_shape=(
            jax.ShapeDtypeStruct((n, PAIR), BF),
            jax.ShapeDtypeStruct((m, PAIR), kept),
            jax.ShapeDtypeStruct((m, PAIR), kept),
        ),
        in_specs=[SMEM, SMEM] + [VMEM] * 8,
        out_specs=(VMEM, VMEM, VMEM),
        scratch_shapes=[pltpu.VMEM((m, PAIR), F32), pltpu.VMEM((m, PAIR), F32)],
        compiler_params=pltpu.CompilerParams(vmem_limit_bytes=56 * 2**20),
    )(*bounds, q, k, v, seg_q, seg_k, out, lse, grad)


def body(
    tokens, lengths, packing, query_w, query_b, key_w, value_w, value_b, output_w, output_b,
    attn_gain, attn_shift, expand_w, expand_b, reduce_w, reduce_b, ffn_gain, ffn_shift, cotangent,
):
    tok_shape = tokens.shape
    laps, stripe, width = tok_shape[1], tok_shape[2], tok_shape[3]
    mine = laps * stripe
    n_ctx = lax.axis_size("ctx")
    n_f = lax.axis_size("fsdp")
    per_group = n_ctx // n_f
    chunks = per_group // 2
    ctx = lax.axis_index("ctx")
    f = lax.axis_index("fsdp")
    g = ctx // per_group
    chunk = ctx % per_group // 2
    b = ctx % 2
    swap = jnp.array(SWAP, jnp.int32)
    u = swap[f] * 2 + b
    pairs = [[2 * j, 2 * j + 1] for j in range(n_ctx // 2)]

    route = []
    for c0 in range(n_ctx):
        for f0 in range(n_f):
            g0, b0 = divmod(c0, per_group)
            route.append((c0 * n_f + f0, (SWAP[f0] * per_group + b0) * n_f + SWAP[g0]))

    def relocate(block):
        return lax.ppermute(block, ("ctx", "fsdp"), route)

    def order(block):
        return jnp.stack([block[SWAP[i]] for i in range(n_f)])

    def gather_group(block):
        both = lax.all_gather(block, "ctx", axis_index_groups=pairs)
        everyone = order(lax.all_gather(both, "fsdp"))
        everyone = everyone.reshape(GROUP, laps, stripe, -1)
        return everyone.transpose(1, 0, 2, 3).reshape(GROUP * mine, -1)

    def swap_group(block):
        block = order(block.reshape(n_f, 2, mine, -1))
        block = lax.all_to_all(block, "fsdp", 0, 0)
        block = lax.all_to_all(block, "ctx", 1, 1, axis_index_groups=pairs)
        return order(block).reshape(GROUP, mine, -1)

    def to_tokens(block):
        parts = block.reshape(laps, GROUP, stripe, PAIR).transpose(1, 0, 2, 3).reshape(GROUP, mine, PAIR)
        return swap_group(parts).transpose(1, 0, 2).reshape(mine, width)

    def to_heads(block):
        parts = block.reshape(mine, GROUP, PAIR).transpose(1, 0, 2)
        got = swap_group(parts).reshape(GROUP, laps, stripe, PAIR)
        return got.transpose(1, 0, 2, 3).reshape(GROUP * mine, PAIR)

    def columns(w):
        return lax.all_to_all(w.reshape(w.shape[0], n_f, -1).transpose(1, 0, 2), "fsdp", 0, 0).reshape(
            n_f * w.shape[0], -1
        )

    def rows_back(w):
        return lax.all_to_all(w.reshape(n_f, w.shape[0] // n_f, w.shape[1]), "fsdp", 0, 0)

    row_id = swap[g]
    ordered_all = jnp.sum(
        jnp.where(
            packing[0][:, None] == jnp.arange(lengths.shape[1], dtype=jnp.int32)[None, :],
            lengths[0][None, :],
            0,
        ),
        axis=1,
    )
    ordered = lax.all_gather(ordered_all, "fsdp")[row_id]
    slots = jnp.arange(ordered.shape[0], dtype=jnp.int32)
    slot_ends = jnp.sum(jnp.where(slots[None, :] <= slots[:, None], ordered[None, :], 0), axis=1)
    span = GROUP * mine
    index = jnp.arange(span, dtype=jnp.int32)

    def segments(which):
        lap, rest = index // (GROUP * stripe), index % (GROUP * stripe)
        unit, place = rest // stripe, rest % stripe
        owner = unit // 2 * per_group + which * 2 + unit % 2
        position = lap * (n_ctx * stripe) + owner * stripe + place
        return jnp.sum((position[:, None] >= slot_ends[None, :]).astype(jnp.int32), axis=1)

    seg_q = segments(chunk)
    seg_k = jnp.concatenate([segments(s) for s in range(chunks)])
    q_first, q_last = seg_q[::BQ], seg_q[BQ - 1 :: BQ]
    k_first = seg_k[::BK].reshape(chunks, -1)
    k_last = seg_k[BK - 1 :: BK].reshape(chunks, -1)
    lo = jnp.sum((k_last[None] < q_first[:, None, None]).astype(jnp.int32), axis=2)
    hi = jnp.sum((k_first[None] <= q_last[:, None, None]).astype(jnp.int32), axis=2)
    bounds = (lo, hi)
    seg_q = seg_q[:, None]
    seg_k = seg_k[None, :]

    inputs = relocate(tokens.reshape(mine, width))
    upstream = relocate(cotangent.reshape(mine, width)).astype(F32)
    x_all = gather_group(inputs)
    w_three = jnp.stack([query_w, key_w, value_w]).reshape(3, -1, n_f, 2, PAIR)
    w_three = lax.dynamic_index_in_dim(w_three, b, 3, keepdims=False)
    w_three = order(w_three.transpose(2, 1, 0, 3).reshape(n_f, -1, 3 * PAIR))
    w_three = lax.all_to_all(w_three, "fsdp", 0, 0).reshape(width, 3 * PAIR)
    here = u * PAIR
    bias3 = jnp.concatenate(
        [
            lax.dynamic_slice_in_dim(query_b, here, PAIR),
            jnp.zeros((PAIR,), F32),
            lax.dynamic_slice_in_dim(value_b, here, PAIR),
        ]
    )
    three = (dense(x_all, w_three) + bias3).astype(BF)
    q, k_own, v_own = three[:, :PAIR], three[:, PAIR : 2 * PAIR], three[:, 2 * PAIR :]
    same_place = [
        [(gg * chunks + s) * 2 + bb for s in range(chunks)] for gg in range(n_f) for bb in range(2)
    ]
    if chunks == 1:
        k, v = k_own, v_own
    else:
        k = lax.all_gather(k_own, "ctx", axis_index_groups=same_place, tiled=True)
        v = lax.all_gather(v_own, "ctx", axis_index_groups=same_place, tiled=True)
    att_heads, lse = attend(bounds, q, k, v, seg_q, seg_k, chunks)

    w_output = lax.all_gather(output_w, "fsdp", axis=0, tiled=True)
    attended = to_tokens(att_heads)
    branch = dense(attended, w_output) + output_b
    normed, x_hat1, inv_std1 = norm_fwd(inputs.astype(F32) + branch, attn_gain, attn_shift)
    normed_low = lax.all_gather(normed.astype(BF), "fsdp", axis=0, tiled=True)

    w_up = columns(expand_w)
    units = w_up.shape[1]
    pre_act = dense(normed_low, w_up) + lax.dynamic_slice_in_dim(expand_b, f * units, units)
    hidden = jax.nn.gelu(pre_act, approximate=False).astype(BF)
    ffn_out = lax.psum_scatter(dense(hidden, reduce_w).astype(BF), "fsdp", tiled=True).astype(F32) + reduce_b
    outputs, x_hat2, inv_std2 = norm_fwd(normed + ffn_out, ffn_gain, ffn_shift)
    layer_out = relocate(outputs.astype(BF)).reshape(tok_shape)
    grad_mid2, grad_ffn_gain, grad_ffn_shift = norm_back(upstream, x_hat2, inv_std2, ffn_gain)
    grad_ffn_own = grad_mid2.astype(BF)
    grad_reduce_b = jnp.sum(grad_ffn_own.astype(F32), axis=0)
    grad_ffn = lax.all_gather(grad_ffn_own, "fsdp", axis=0, tiled=True)
    part_down = dense_in(hidden, grad_ffn).astype(BF)
    grad_pre = (dense_back(grad_ffn, reduce_w) * gelu_slope(pre_act)).astype(BF)
    grad_expand_b = lax.dynamic_update_slice_in_dim(
        jnp.zeros_like(expand_b), jnp.sum(grad_pre.astype(F32), axis=0), f * units, 0
    )
    part_up = dense_in(normed_low, grad_pre).astype(BF)
    grad_normed = lax.psum_scatter(dense_back(grad_pre, w_up).astype(BF), "fsdp", tiled=True).astype(F32) + grad_mid2
    grad_mid1, grad_attn_gain, grad_attn_shift = norm_back(grad_normed, x_hat1, inv_std1, attn_gain)
    grad_branch = grad_mid1.astype(BF)
    grad_output_b = jnp.sum(grad_branch.astype(F32), axis=0)
    part_out = lax.psum_scatter(dense_in(attended, grad_branch).astype(BF), "fsdp", tiled=True)
    grad_att = to_heads(dense_back(grad_branch, w_output).astype(BF))

    grad_q, grad_k, grad_v = attend_back(
        bounds, q, k, v, seg_q, seg_k, att_heads, lse, grad_att, chunks
    )
    if chunks > 1:
        grad_k = lax.psum_scatter(
            grad_k.astype(BF), "ctx", axis_index_groups=same_place, tiled=True
        )
        grad_v = lax.psum_scatter(
            grad_v.astype(BF), "ctx", axis_index_groups=same_place, tiled=True
        )
    grad_three = jnp.concatenate([grad_q, grad_k, grad_v], axis=1)
    sums3 = jnp.sum(grad_three.astype(F32), axis=0)
    grad_query_b = lax.dynamic_update_slice_in_dim(jnp.zeros_like(query_b), sums3[:PAIR], here, 0)
    grad_value_b = lax.dynamic_update_slice_in_dim(jnp.zeros_like(value_b), sums3[2 * PAIR :], here, 0)
    part_three = dense_in(x_all, grad_three).astype(BF)
    back = dense_back(grad_three, w_three).astype(BF)
    back = back.reshape(laps, GROUP, stripe, width).transpose(1, 0, 2, 3).reshape(n_f, 2, mine, width)
    back = lax.psum_scatter(order(back), "fsdp", scatter_dimension=0)
    back = lax.psum_scatter(back, "ctx", scatter_dimension=0, axis_index_groups=pairs)
    grad_inputs = relocate(back.astype(F32) + grad_mid1).reshape(tok_shape)

    got = order(rows_back(part_three)).reshape(n_f, -1, 3, PAIR)
    got = got.transpose(2, 1, 0, 3)[:, :, :, None, :]
    mask = (jnp.arange(2) == b)[None, None, None, :, None]
    share_three = jnp.where(mask, got, BF(0)).reshape(3, got.shape[1], width)
    share_up = rows_back(part_up).transpose(1, 0, 2).reshape(-1, n_f * units)
    share_three, share_out, share_up, share_down = lax.psum(
        (share_three, part_out, share_up, part_down), "ctx"
    )
    share_three = share_three.astype(F32)
    (
        grad_query_b, grad_value_b, grad_output_b, grad_attn_gain, grad_attn_shift, grad_expand_b,
        grad_reduce_b, grad_ffn_gain, grad_ffn_shift,
    ) = lax.psum(
        (
            grad_query_b, grad_value_b, grad_output_b, grad_attn_gain, grad_attn_shift, grad_expand_b,
            grad_reduce_b, grad_ffn_gain, grad_ffn_shift,
        ),
        ("ctx", "fsdp"),
    )
    return (
        layer_out,
        grad_inputs,
        share_three[0],
        grad_query_b,
        share_three[1],
        share_three[2],
        grad_value_b,
        share_out.astype(F32),
        grad_output_b,
        grad_attn_gain,
        grad_attn_shift,
        share_up.astype(F32),
        grad_expand_b,
        share_down.astype(F32),
        grad_reduce_b,
        grad_ffn_gain,
        grad_ffn_shift,
    )


def solution(mesh):
    acts = P("fsdp", None, "ctx", None)
    rows = P("fsdp", None)
    return jax.shard_map(
        body,
        mesh=mesh,
        in_specs=(
            acts, rows, rows, rows, P(), rows, rows, P(), rows, P(),
            P(), P(), rows, P(), rows, P(), P(), P(), acts,
        ),
        out_specs=(
            acts, acts, rows, P(), rows, rows, P(), rows, P(),
            P(), P(), rows, P(), rows, P(), P(), P(),
        ),
        check_vma=False,
    )
```

time: 1590 us -> 788 us (0.50)
  blocking collectives: 524 us -> 168 us
  waiting for transfers between devices: 689 us -> 382 us
  matrix products: 194 us -> 55.1 us
  other arithmetic: 85.1 us -> 31.5 us
  Pallas kernels: 0 us -> 41.3 us
    psum x1 -> x0, blocking collectives: 485 us -> none  [body(): lax.psum((share_query, share_key, share_value, share_out, share_up, share...]
    ppermute x32 -> x4, waiting for transfers between devices: 247 us -> 0.01 us  [relocate(): return lax.ppermute(block, ('ctx', 'fsdp'), route)]
    all_gather x8 -> x5, waiting for transfers between devices: 228 us -> 69.8 us  [the longest x1 43.2 us: gather_group(): both = lax.all_gather(block, 'ctx', axis_index_groups=pairs)]
    dot_general x68 -> x8, matrix products: 179 us -> 42 us  [the longest x4 22.9 us: dense(): return jnp.dot(left, right, preferred_element_type=F32)]
    psum x0 -> x1, waiting for transfers between devices: none -> 133 us  [body(): lax.psum((share_three, part_out, share_up, part_down), 'ctx')]
    psum x1, blocking collectives: 38.5 us -> 109 us  [body(): lax.psum((grad_query_b, grad_value_b, grad_output_b, grad_attn_gain, grad...]
    reduce_scatter x6 -> x5, waiting for transfers between devices: 209 us -> 140 us  [the longest x1 49.5 us: body(): back = lax.psum_scatter(order(back), 'fsdp', scatter_dimension=0)]
    all_to_all x0 -> x4, blocking collectives: none -> 43.1 us  [the longest x2 22.5 us: swap_group(): block = lax.all_to_all(block, 'fsdp', 0, 0)]
  transfers between devices with their start and end apart: 46 -> 19, of which waited for: 26 -> 11; matrix products, arithmetic and copies ran while one was open for 18% -> 11% of each run, Pallas kernels for 0% -> 2%
where the time goes in v2:
time: 788 us; the launch traced here: 777 us
  waiting for transfers between devices  382 us (48%)
  blocking collectives  168 us (21%)
  matrix products  55.1 us (7%)
  local copies, waits for them, and re-layouts  54.1 us (7%)
  Pallas kernels  41.3 us (5%)
  other arithmetic  31.5 us (4%)
  starting transfers between devices  27.5 us (3%)
  between operations  18.4 us (2%)
    psum x1, waiting for transfers between devices, body(): lax.psum((share_three, part_out, share_up, part_down), 'ctx')  133 us
    psum x1, blocking collectives, body(): lax.psum((grad_query_b, grad_value_b, grad_output_b, grad_attn_gain, grad...  109 us
    reduce_scatter x1, waiting for transfers between devices, body(): back = lax.psum_scatter(order(back), 'fsdp', scatter_dimension=0)  49.5 us
    all_gather x1, waiting for transfers between devices, gather_group(): both = lax.all_gather(block, 'ctx', axis_index_groups=pairs)  43.2 us
    all_to_all x1, waiting for transfers between devices, columns(): lax.all_to_all(w.reshape(w.shape[0], n_f, -1).transpose(1, 0, 2), 'fsdp',...  36.1 us
    reduce_scatter x1, waiting for transfers between devices, body(): lax.psum_scatter(dense_back(grad_pre, w_up).astype(BF), 'fsdp', tiled=True)  31.5 us
    reduce_scatter x1, waiting for transfers between devices, body(): lax.psum_scatter(dense(hidden, reduce_w).astype(BF), 'fsdp', tiled=True)  28.9 us
    all_gather x1, waiting for transfers between devices, body(): grad_ffn = lax.all_gather(grad_ffn_own, 'fsdp', axis=0, tiled=True)  24.2 us
  transfers between devices with their start and end apart: 19, of which 11 were waited for; matrix products, arithmetic and copies ran while one was open for 11% of the time, Pallas kernels for 2%

profile of v2, /device:TPU:0, one launch (start us, length us, event | category | flops | bytes accessed | tf_op | source)
XLA Modules:
  0.0 777.4 jit_solution(2188326634886015789)
XLA Ops:
  10.0 43.2 %all-gather.15.cloned.1.call-done = bf16[512,1024]{1,0:T(8,128)(2,1)} async-done(((bf16[256,1024]{1,0:T(8,128)(2,1)}), bf16[512,1024]{1,0:T(8,128)(2,1)}) %all-gather.15.cloned.1.call-update) | async-done | bytes 1048592 | tf_op jit(solution)/shard_map/all_gather | solution.py:229
  63.9 4.2 all-to-all-start
  72.5 16.0 %all-reduce.1 = s32[4,3]{1,0:T(4,128)S(1)} all-reduce(s32[4,3]{1,0:T(4,128)S(1)} %reshape.382), channel_id=2, replica_groups=mesh['ctx'=8,'fsdp'=4] {'fsdp'}, use_global_device_ids=true, to_apply=%add | all-reduce | flops 12 | bytes 96
  104.9 18.4 %shard_map.323 = (bf16[2048,128]{1,0:T(8,128)(2,1)S(1)}, f32[4096,1]{1,0:T(8,128)S(1)}) custom-call(s32[8,1]{1,0:T(8,128)S(1)} %copy.164.lo_ref, s32[8,1]{1,0:T(8,128)S(1)} %copy.165.hi_ref, bf16[2048,128]{1,0:T(8,128)(2,1)S(1)} %get-tuple-element.70.q_ref, bf16[2048,128]{1,0:T(8,128)(2,1)S(1)} %get-tuple-element.69.k_ref, ...), custom_call_target="tpu_custom_call" | custom-call | tf_op jit(solution)/shard_map/pallas_call | solution.py:170
  123.5 11.2 %all_to_all.40 = bf16[4,2,256,128]{3,2,1,0:T(8,128)(2,1)S(1)} all-to-all(bf16[4,2,256,128]{3,2,1,0:T(8,128)(2,1)S(1)} %pad_maximum_fusion.4), channel_id=1, replica_groups=mesh['ctx'=8,'fsdp'=4] {'fsdp'}, dimensions={0} | all-to-all | bytes 1048576 | tf_op jit(solution)/shard_map/all_to_all | solution.py:236
  134.8 10.3 %all_to_all.41 = bf16[4,2,256,128]{3,2,0,1:T(8,128)(2,1)S(1)} all-to-all(bf16[4,2,256,128]{3,2,0,1:T(8,128)(2,1)S(1)} %copy.168), channel_id=1, replica_groups={{0,4},{8,12},{16,20},{24,28},{1,5},{9,13},{17,21},{25,29},{2,6},{10,14}..., dimensions={1} | all-to-all | bytes 1048576 | tf_op jit(solution)/shard_map/all_to_all | solution.py:237
  150.3 4.1 copy.170
  154.4 4.5 all-to-all-start.3
  159.8 36.1 %all-to-all-done.3 = bf16[4,256,1024]{1,2,0:T(8,128)(2,1)} async-done(((bf16[4,256,1024]{1,2,0:T(8,128)(2,1)}), bf16[4,256,1024]{1,2,0:T(8,128)(2,1)}, u32[]{:S(2)}, u32[]{:S(2)}) %all-to-all-start.3) | async-done | bytes 2097184 | tf_op jit(solution)/shard_map/all_to_all | solution.py:250
  195.9 4.0 copy.171
  199.9 14.2 %fusion.2 = (bf16[1024,1024]{1,0:T(8,128)(2,1)S(1)}, f32[1024,1024]{1,0:T(8,128)}) fusion(f32[1024]{0:T(1024)S(1)} %dynamic_slice.28, bf16[1024,1024]{1,0:T(8,128)(2,1)} %all-gather.11.cloned.1.call-done, bf16[1024,1024]{1,0:T(8,128)(2,1)} %bitcast.153), kind=kOutput, calls=%fused_computation.4 | convolution fusion | flops 2216689664 | bytes 10489856 | tf_op jit(solution)/shard_map/dot_general | solution.py:19
  215.4 3.7 convolution_convert_fusion.5
  219.2 5.4 collective-permute-start.2
  224.5 28.9 %reduce-scatter.6.cloned.1.call-done = bf16[256,1024]{1,0:T(8,128)(2,1)} async-done(((bf16[1024,1024]{1,0:T(8,128)(2,1)}), bf16[256,1024]{1,0:T(8,128)(2,1)}) %reduce-scatter.6.cloned.1.call-update) | async-done | bytes 524304 | tf_op jit(solution)/shard_map/reduce_scatter | solution.py:327
  259.9 24.2 %all-gather.13.cloned.1.call-done = bf16[1024,1024]{1,0:T(8,128)(2,1)} async-done(((bf16[256,1024]{1,0:T(8,128)(2,1)}), bf16[1024,1024]{1,0:T(8,128)(2,1)}) %all-gather.13.cloned.1.call-update) | async-done | bytes 2097168 | tf_op jit(solution)/shard_map/all_gather | solution.py:333
  284.1 6.3 convert_reduce_fusion
  291.8 3.7 convolution_convert_fusion.4
  295.6 31.5 %reduce-scatter.8.cloned.1.call-done = bf16[256,1024]{1,0:T(8,128)(2,1)} async-done(((bf16[1024,1024]{1,0:T(8,128)(2,1)}), bf16[256,1024]{1,0:T(8,128)(2,1)}) %reduce-scatter.8.cloned.1.call-update) | async-done | bytes 524304 | tf_op jit(solution)/shard_map/reduce_scatter | solution.py:340
  331.3 11.2 %all_to_all.42 = bf16[4,2,256,128]{3,2,1,0:T(8,128)(2,1)S(1)} all-to-all(bf16[4,2,256,128]{3,2,1,0:T(8,128)(2,1)S(1)} %pad_maximum_fusion.6), channel_id=1, replica_groups=mesh['ctx'=8,'fsdp'=4] {'fsdp'}, dimensions={0} | all-to-all | bytes 1048576 | tf_op jit(solution)/shard_map/all_to_all | solution.py:236
  342.6 10.3 %all_to_all.43 = bf16[4,2,256,128]{3,2,0,1:T(8,128)(2,1)S(1)} all-to-all(bf16[4,2,256,128]{3,2,0,1:T(8,128)(2,1)S(1)} %copy.173), channel_id=1, replica_groups={{0,4},{8,12},{16,20},{24,28},{1,5},{9,13},{17,21},{25,29},{2,6},{10,14}..., dimensions={1} | all-to-all | bytes 1048576 | tf_op jit(solution)/shard_map/all_to_all | solution.py:237
  353.8 22.9 %shard_map.324 = (bf16[2048,128]{1,0:T(8,128)(2,1)}, bf16[2048,128]{1,0:T(8,128)(2,1)}, bf16[2048,128]{1,0:T(8,128)(2,1)}) custom-call(s32[8,1]{1,0:T(8,128)} %copy-done.10, s32[8,1]{1,0:T(8,128)} %copy-done.9, bf16[2048,128]{1,0:T(8,128)(2,1)} %copy-done.5, bf16[2048,128]{1,0:T(8,128)(2,1)} %copy-done.4, bf16[2048,128]{1,0:T(8,128)(2,1)} %copy-done.3, ...), custom_call_target="tpu_custom_call" | custom-call | tf_op jit(solution)/shard_map/pallas_call | solution.py:182
  389.3 6.0 convolution_convert_fusion.2
  395.3 4.5 all-to-all-start.7
  399.9 49.5 %reduce-scatter.10.cloned.1.call-done = bf16[1,2,256,1024]{3,2,1,0:T(8,128)(2,1)} async-done(((bf16[4,2,256,1024]{3,2,1,0:T(8,128)(2,1)}), bf16[1,2,256,1024]{3,2,1,0:T(8,128)(2,1)}) %reduce-scatter.10.cloned.1.call-update) | async-done | bytes 1048592 | tf_op jit(solution)/shard_map/reduce_scatter | solution.py:364
  449.4 5.0 convolution_convert_fusion.6
  455.6 3.5 all-to-all-start.6
  459.2 5.9 convolution_convert_fusion.1
  473.8 3.8 broadcast_in_dim.101
  480.4 7.9 %reduce-scatter.14.cloned.1.call-done = bf16[256,1024]{1,0:T(8,128)(2,1)} async-done(((bf16[1024,1024]{1,0:T(8,128)(2,1)}), bf16[256,1024]{1,0:T(8,128)(2,1)}) %reduce-scatter.14.cloned.1.call-update) | async-done | bytes 524304 | tf_op jit(solution)/shard_map/reduce_scatter | solution.py:344
  489.0 21.7 %reduce-scatter.12.cloned.1.call-done = bf16[1,256,1024]{2,1,0:T(8,128)(2,1)} async-done(((bf16[2,256,1024]{2,1,0:T(8,128)(2,1)}), bf16[1,256,1024]{2,1,0:T(8,128)(2,1)}) %reduce-scatter.12.cloned.1.call-update) | async-done | bytes 524304 | tf_op jit(solution)/shard_map/reduce_scatter | solution.py:365
  517.0 108.9 %all-reduce.2 = (f32[1024]{0:T(1024)}, f32[1024]{0:T(1024)}, f32[1024]{0:T(1024)}, f32[1024]{0:T(1024)}, f32[1024]{0:T(1024)}, /*index=5*/f32[4096]{0:T(1024)}, f32[1024]{0:T(1024)}, f32[1024]{0:T(1024)}, f32[1024]{0:T(1024)}) all-reduce(f32[1024]{0:T(1024)S(1)} %slice_dynamic-update-slice_fusio, ...), channel_id=1, replica_groups=mesh['ctx'=8,'fsdp'=4] {'ctx','fsdp'}, use_global_device_ids=true, to_apply=%region_20.21 | all-reduce | flops 12288 | bytes 98304 | tf_op jit(solution)/shard_map/psum | solution.py:380
  625.9 132.9 %all-reduce.6.cloned.1.call-done = (bf16[3,256,1024]{2,1,0:T(8,128)(2,1)}, bf16[256,1024]{1,0:T(8,128)(2,1)}, bf16[256,4096]{1,0:T(8,128)(2,1)}, bf16[1024,1024]{1,0:T(8,128)(2,1)}) async-done(((bf16[3,256,1024]{2,1,0:T(8,128)(2,1)}, bf16[256,1024]{1,0:T(8,128)(2,1)}, bf16[256,4096]{1,0:T(8,128)(2,1)}, bf16[1024,1024]{1,0:T(8,128)(2,1)}), (bf16[3,256,1024]{2,1,0:T(8,128)(2,1)}, bf16[256,1024]{1,0:T(8,128)(2,1)}, ...) | async-done | bytes 6291472 | tf_op jit(solution)/shard_map/psum | solution.py:373
  (217 shorter events, 95.1 us)
Async XLA Ops:
  7.2 208.2 %copy-start = (bf16[1024,1024]{1,0:T(8,128)(2,1)S(1)}, bf16[1024,1024]{1,0:T(8,128)(2,1)}, u32[]{:S(2)}) copy-start(bf16[1024,1024]{1,0:T(8,128)(2,1)} %param.34) | copy-start | bytes 6291460
  7.2 46.0 %all-gather.15.cloned.1.call-start = ((), (), s32[]{:S(2)}) async-start(), calls=%async_computation.21 | async-start | bytes 1572864 | tf_op jit(solution)/shard_map/all_gather | solution.py:229
  7.3 1.8 collective-permute-start
  9.9 87.9 %all-gather.17.cloned.1.call-start = ((), (), s32[]{:S(2)}) async-start(), calls=%async_computation.22 | async-start | bytes 5242880 | tf_op jit(solution)/shard_map/all_gather | solution.py:230
  63.9 29.2 %all-to-all-start = ((bf16[4,256,384]{1,2,0:T(8,128)(2,1)}), bf16[4,256,384]{1,2,0:T(8,128)(2,1)}, u32[]{:S(2)}, u32[]{:S(2)}) async-start(bf16[4,256,384]{1,2,0:T(8,128)(2,1)} %pad_maximum_fusion.2), calls=%async_computation | async-start | bytes 1572864 | tf_op jit(solution)/shard_map/all_to_all | solution.py:296
  68.0 78.3 %all-gather.9.cloned.1.call-start = ((), (), s32[]{:S(2)}) async-start(), calls=%async_computation.13 | async-start | bytes 2621440 | tf_op jit(solution)/shard_map/all_gather | solution.py:317
  68.8 131.1 %all-gather.11.cloned.1.call-start = ((), (), s32[]{:S(2)}) async-start(), calls=%async_computation.14 | async-start | bytes 2621440 | tf_op jit(solution)/shard_map/all_gather | solution.py:321
  104.8 40.3 %copy-start.3 = (bf16[2048,128]{1,0:T(8,128)(2,1)}, bf16[2048,128]{1,0:T(8,128)(2,1)S(1)}, u32[]{:S(2)}) copy-start(bf16[2048,128]{1,0:T(8,128)(2,1)S(1)} %get-tuple-element.68.v_ref) | copy-start | bytes 1572868
  104.8 40.3 %copy-start.4 = (bf16[2048,128]{1,0:T(8,128)(2,1)}, bf16[2048,128]{1,0:T(8,128)(2,1)S(1)}, u32[]{:S(2)}) copy-start(bf16[2048,128]{1,0:T(8,128)(2,1)S(1)} %get-tuple-element.69.k_ref) | copy-start | bytes 1572868
  104.8 40.3 %copy-start.5 = (bf16[2048,128]{1,0:T(8,128)(2,1)}, bf16[2048,128]{1,0:T(8,128)(2,1)S(1)}, u32[]{:S(2)}) copy-start(bf16[2048,128]{1,0:T(8,128)(2,1)S(1)} %get-tuple-element.70.q_ref) | copy-start | bytes 1572868
  123.3 21.9 %copy-start.6 = (f32[4096,1]{1,0:T(8,128)}, f32[4096,1]{1,0:T(8,128)S(1)}, u32[]{:S(2)}) copy-start(f32[4096,1]{1,0:T(8,128)S(1)} %get-tuple-element.23.lse_ref) | copy-start | bytes 49156
  123.4 21.9 %copy-start.7 = (bf16[2048,128]{1,0:T(8,128)(2,1)}, bf16[2048,128]{1,0:T(8,128)(2,1)S(1)}, u32[]{:S(2)}) copy-start(bf16[2048,128]{1,0:T(8,128)(2,1)S(1)} %get-tuple-element.22.o_ref) | copy-start | bytes 1572868
  123.4 22.9 %copy-start.27 = (f32[1024]{0:T(1024)S(1)}, f32[1024]{0:T(1024)}, u32[]{:S(2)}) copy-start(f32[1024]{0:T(1024)} %param.29) | copy-start | bytes 12292
  154.4 41.5 %all-to-all-start.3 = ((bf16[4,256,1024]{1,2,0:T(8,128)(2,1)}), bf16[4,256,1024]{1,2,0:T(8,128)(2,1)}, u32[]{:S(2)}, u32[]{:S(2)}) async-start(bf16[4,256,1024]{1,2,0:T(8,128)(2,1)} %bitcast.138), calls=%async_computation.3 | async-start | bytes 4194304 | tf_op jit(solution)/shard_map/all_to_all | solution.py:250
  158.9 94.5 %reduce-scatter.6.cloned.1.call-start = ((), (), s32[]{:S(2)}) async-start(), calls=%async_computation.15 | async-start | bytes 2621440 | tf_op jit(solution)/shard_map/reduce_scatter | solution.py:327
  215.4 38.0 %copy-start.30 = (f32[1024]{0:T(1024)S(1)}, f32[1024]{0:T(1024)}, u32[]{:S(2)}) copy-start(f32[1024]{0:T(1024)} %param.35) | copy-start | bytes 12292
  219.1 36.1 %copy-start.29 = (f32[1024]{0:T(1024)S(1)}, f32[1024]{0:T(1024)}, u32[]{:S(2)}) copy-start(f32[1024]{0:T(1024)} %param.36) | copy-start | bytes 12292
  219.1 37.7 %copy-start.31 = (f32[1024]{0:T(1024)S(1)}, f32[1024]{0:T(1024)}, u32[]{:S(2)}) copy-start(f32[1024]{0:T(1024)} %param.37) | copy-start | bytes 12292
  219.1 65.0 %all-gather.13.cloned.1.call-start = ((), (), s32[]{:S(2)}) async-start(), calls=%async_computation.16 | async-start | bytes 2621440 | tf_op jit(solution)/shard_map/all_gather | solution.py:333
  219.2 36.0 %collective-permute-start.2 = (bf16[256,1024]{1,0:T(8,128)(2,1)}, bf16[256,1024]{1,0:T(8,128)(2,1)}, u32[]{:S(2)}, u32[]{:S(2)}) collective-permute-start(bf16[256,1024]{1,0:T(8,128)(2,1)} %bitcast.179), channel_id=1, source_target_pairs={{0,0},{1,16},{2,8},{3,24},{4,4},{5,20},{6,12},{7,28},{8,2},{9,18},... | collective-permute-start | bytes 1572872 | tf_op jit(solution)/shard_map/ppermute | solution.py:223
  259.7 67.4 %reduce-scatter.8.cloned.1.call-start = ((), (), s32[]{:S(2)}) async-start(), calls=%async_computation.17 | async-start | bytes 2621440 | tf_op jit(solution)/shard_map/reduce_scatter | solution.py:340
  291.8 35.3 %copy-start.11 = (f32[256,1024]{1,0:T(8,128)S(1)}, f32[256,1024]{1,0:T(8,128)}, u32[]{:S(2)}) copy-start(f32[256,1024]{1,0:T(8,128)} %get-tuple-element.52) | copy-start | bytes 3145732
  295.5 153.8 %reduce-scatter.10.cloned.1.call-start = ((), (), s32[]{:S(2)}) async-start(), calls=%async_computation.18 | async-start | bytes 5242880 | tf_op jit(solution)/shard_map/reduce_scatter | solution.py:364
  353.8 26.3 %copy-start.21 = (bf16[4,256,384]{2,1,0:T(8,128)(2,1)S(1)}, bf16[4,256,384]{2,1,0:T(8,128)(2,1)}, u32[]{:S(2)}) copy-start(bf16[4,256,384]{2,1,0:T(8,128)(2,1)} %copy.163) | copy-start | bytes 2359300
  386.2 102.1 %reduce-scatter.14.cloned.1.call-start = ((), (), s32[]{:S(2)}) async-start(), calls=%async_computation.20 | async-start | bytes 2621440 | tf_op jit(solution)/shard_map/reduce_scatter | solution.py:344
  395.3 60.3 %all-to-all-start.7 = ((bf16[4,256,1024]{2,1,0:T(8,128)(2,1)}), bf16[4,256,1024]{2,1,0:T(8,128)(2,1)}, u32[]{:S(2)}, u32[]{:S(2)}) async-start(bf16[4,256,1024]{2,1,0:T(8,128)(2,1)} %bitcast.155), calls=%async_computation.12 | async-start | bytes 4194304 | tf_op jit(solution)/shard_map/all_to_all | solution.py:255
  399.8 110.9 %reduce-scatter.12.cloned.1.call-start = ((), (), s32[]{:S(2)}) async-start(), calls=%async_computation.19 | async-start | bytes 1572864 | tf_op jit(solution)/shard_map/reduce_scatter | solution.py:365
  455.6 15.1 %all-to-all-start.6 = ((bf16[4,256,384]{1,2,0:T(8,128)(2,1)}), bf16[4,256,384]{1,2,0:T(8,128)(2,1)S(1)}, u32[]{:S(2)}, u32[]{:S(2)}) async-start(bf16[4,256,384]{1,2,0:T(8,128)(2,1)} %copy.183), calls=%async_computation.10 | async-start | bytes 1572864 | tf_op jit(solution)/shard_map/all_to_all | solution.py:255
  459.1 299.7 %all-reduce.6.cloned.1.call-start = ((), (), s32[]{:S(2)}) async-start(), calls=%async_computation.23 | async-start | bytes 12582912 | tf_op jit(solution)/shard_map/psum | solution.py:373
  488.3 26.5 %collective-permute-start.1 = (bf16[256,1024]{1,0:T(8,128)(2,1)S(1)}, bf16[256,1024]{1,0:T(8,128)(2,1)S(1)}, u32[]{:S(2)}, u32[]{:S(2)}) collective-permute-start(bf16[256,1024]{1,0:T(8,128)(2,1)S(1)} %copy-done.22), channel_id=1, source_target_pairs={{0,0},{1,16},{2,8},{3,24},{4,4},{5,20},{6,12},{7,28},{8,2},{9,18},... | collective-permute-start | bytes 1572872 | tf_op jit(solution)/shard_map/ppermute | solution.py:223
  512.9 255.8 %collective-permute-start.3 = (f32[256,1024]{1,0:T(8,128)}, f32[256,1024]{1,0:T(8,128)S(1)}, u32[]{:S(2)}, u32[]{:S(2)}) collective-permute-start(f32[256,1024]{1,0:T(8,128)} %convert_add_fusion), channel_id=1, source_target_pairs={{0,0},{1,16},{2,8},{3,24},{4,4},{5,20},{6,12},{7,28},{8,2},{9,18},... | collective-permute-start | bytes 3145736 | tf_op jit(solution)/shard_map/ppermute | solution.py:223
  514.8 244.0 %copy-start.24 = (bf16[256,1024]{1,0:T(8,128)(2,1)}, bf16[256,1024]{1,0:T(8,128)(2,1)S(1)}, u32[]{:S(2)}) copy-start(bf16[256,1024]{1,0:T(8,128)(2,1)S(1)} %collective-permute-done.1) | copy-start | bytes 1572868
  (25 other events, 149.7 us)
Sparse Core Ops, SparseCore 0:
  10.2 42.9 all-gather.14
  54.7 42.9 all-gather.16
  99.3 22.5 all-gather.8
  150.5 37.5 all-gather.10
  219.2 34.1 reduce-scatter.5
  259.8 24.2 all-gather.12
  295.6 31.3 reduce-scatter.7
  386.3 62.9 reduce-scatter.9
  452.0 36.1 reduce-scatter.13
  490.4 20.3 reduce-scatter.11
  516.4 242.3 all-reduce.5

commit v3 on v2

--- a/solution.py
+++ b/solution.py
@@ -191,6 +191,411 @@
         scratch_shapes=[pltpu.VMEM((m, PAIR), F32), pltpu.VMEM((m, PAIR), F32)],
         compiler_params=pltpu.CompilerParams(vmem_limit_bytes=56 * 2**20),
     )(*bounds, q, k, v, seg_q, seg_k, out, lse, grad)
+
+
+def mesh_id(ctx, f):
+    return {"ctx": ctx, "fsdp": f}
+
+
+def swapped(i):
+    return i % 2 * 2 + i // 2
+
+
+class Place:
+    def __init__(self):
+        self.ctx = lax.axis_index("ctx")
+        self.f = lax.axis_index("fsdp")
+        self.per_group = lax.axis_size("ctx") // 4
+        self.g = self.ctx // self.per_group
+        self.b = self.ctx % 2
+        self.rest = self.ctx % self.per_group
+        self.core = self.f % 2
+        self.x = self.f // 2
+
+    def at(self, g=None, b=None, f=None):
+        ctx = self.ctx
+        if g is not None:
+            ctx = ctx + (g - self.g) * self.per_group
+        if b is not None:
+            ctx = ctx + (b - self.b)
+        return mesh_id(ctx, self.f if f is None else f)
+
+    def sibling(self):
+        return self.at(f=self.f + 1 - 2 * self.core)
+
+    def beside(self):
+        return self.at(f=(self.f + 2) % 4)
+
+    def across(self):
+        return self.at(b=1 - self.b)
+
+    def fsdp(self, k):
+        return self.at(f=(self.f + k) % 4)
+
+    def moved(self):
+        return mesh_id(swapped(self.f) * self.per_group + self.rest, swapped(self.g))
+
+    def stays(self):
+        return swapped(self.f) == self.g
+
+
+def remote(src, dst, send, recv, where):
+    return pltpu.make_async_remote_copy(
+        src_ref=src, dst_ref=dst, send_sem=send, recv_sem=recv,
+        device_id=where, device_id_type=pl.DeviceIdType.MESH,
+    )
+
+
+def meet(me, targets, moves):
+    barrier = pltpu.get_barrier_semaphore()
+    for t in targets:
+        pl.semaphore_signal(barrier, 1, device_id=t, device_id_type=pl.DeviceIdType.MESH)
+    if not moves:
+        pl.semaphore_wait(barrier, len(targets))
+        return
+
+    @pl.when(jnp.logical_not(me.stays()))
+    def _():
+        pl.semaphore_signal(barrier, 1, device_id=me.moved(), device_id_type=pl.DeviceIdType.MESH)
+
+    pl.semaphore_wait(barrier, len(targets) + jnp.where(me.stays(), 0, 1))
+
+
+def tail_kernel(
+    x_ref, g3_ref, w3_ref, down_ref, up_ref, out_ref, mid_ref, vec_ref,
+    down_out, up_out, o_out, three_out, dx_ref, sums_ref,
+    dxp, dx1, t1, xa, yb, t2a, t2b, ra, rb, moved_buf,
+    yr_down, yr_up, zl, zr, zs, up_send, up_got,
+    o_got, o_sum, yr_o, ol, orr, os_,
+    gq, ql, qr, qs, q_send,
+    vs, vr,
+    s_dx, r_dx, s_y, r_y, s_z, r_zl, r_zr, s_u, r_u, s_o, r_o, s_oz, r_ol, r_or, s_q, r_ql, r_qr,
+    s_qf, r_qf, s_v, r_v, s_ag, r_ag, s_ay, r_ay, loc,
+):
+    me = Place()
+    g, b, f = me.g, me.b, me.f
+    z_others = [me.at(g=(g + k) % 4) for k in (1, 2, 3)]
+    meet(me, [me.across()] + [me.fsdp(k) for k in (1, 2, 3)] + z_others, True)
+
+    y_copies = {}
+    for p in (3, 0, 2, 1):
+        y_copies[p] = (
+            remote(down_ref.at[1 - b, p], yr_down.at[p], s_y.at[0, p], r_y.at[0, p], me.across()),
+            remote(up_ref.at[:, 1 - b, p], yr_up.at[p], s_y.at[1, p], r_y.at[1, p], me.across()),
+        )
+        for c in y_copies[p]:
+            c.start()
+    o_copies = []
+    for k in (1, 2, 3):
+        c = remote(out_ref.at[(f + k) % 4], o_got.at[k - 1], s_o.at[k - 1], r_o.at[k - 1], me.fsdp(k))
+        c.start()
+        o_copies.append(c)
+
+    def dx_step(i, carry):
+        rows = pl.ds(pl.multiple_of(i * 256, 256), 256)
+        part = dense_back(g3_ref[rows, :], w3_ref[...]).astype(BF)
+        dxp[pl.ds(2 * i, 2)] = part.reshape(2, 2, 2, 2, 16, 1024)
+        return carry
+
+    lax.fori_loop(0, 8, dx_step, 0)
+    c_core = remote(dxp.at[:, 1 - me.core], dx1, s_dx.at[0], r_dx.at[0], me.sibling())
+    c_core.start()
+
+    hops = [me.sibling(), me.beside(), me.across(), me.at(g=g + 1 - 2 * (g % 2)), me.at(g=(g + 2) % 4)]
+    vec = vec_ref[...]
+
+    def hop(i, vec):
+        vs[i] = vec
+        c = remote(vs.at[i], vr.at[i], s_v.at[i], r_v.at[i], hops[i])
+        c.start()
+        return c
+
+    v_copies = [hop(0, vec)]
+
+    def hop_end(i, vec):
+        v_copies[i].wait()
+        return vec + vr[i]
+
+    def q_step(i, carry):
+        cols = pl.ds(pl.multiple_of(i * 256, 256), 256)
+        part = dense_in(x_ref[:, cols], g3_ref[...]).astype(BF)
+        for j in range(3):
+            gq[i, j] = part[:, j * 128 : (j + 1) * 128].reshape(4, 64, 128)
+        return carry
+
+    lax.fori_loop(0, 4, q_step, 0)
+
+    vec = hop_end(0, vec)
+    v_copies.append(hop(1, vec))
+
+    c_core.wait()
+
+    def t1_step(i, carry):
+        t1[i] = (dxp[i, me.core].astype(F32) + dx1[i].astype(F32)).astype(BF)
+        return carry
+
+    lax.fori_loop(0, 16, t1_step, 0)
+    lo, hi = pl.ds(0, 8), pl.ds(8, 8)
+    c_xa = remote(t1.at[lo, 1 - me.x], xa, s_dx.at[1], r_dx.at[1], me.beside())
+    c_yb = remote(t1.at[hi, :, 1 - b], yb, s_dx.at[2], r_dx.at[2], me.across())
+    c_xa.start()
+    c_yb.start()
+
+    vec = hop_end(1, vec)
+    v_copies.append(hop(2, vec))
+
+    def flow(p, own, left, right, send, s_sem, l_sem, r_sem):
+        @pl.when(g < p)
+        def _():
+            @pl.when(g > 0)
+            def _():
+                remote(send.at[p], left.at[p], s_sem.at[p], l_sem.at[p], me.across()).wait_recv()
+                send[p] = (own(p) + left[p].astype(F32)).astype(BF)
+
+            @pl.when(g == 0)
+            def _():
+                send[p] = own(p).astype(BF)
+
+            remote(send.at[p], left.at[p], s_sem.at[p], l_sem.at[p], me.at(g=g + 1)).start()
+
+        @pl.when(g > p)
+        def _():
+            @pl.when(g < 3)
+            def _():
+                remote(send.at[p], right.at[p], s_sem.at[p], r_sem.at[p], me.across()).wait_recv()
+                send[p] = (own(p) + right[p].astype(F32)).astype(BF)
+
+            @pl.when(g == 3)
+            def _():
+                send[p] = own(p).astype(BF)
+
+            remote(send.at[p], right.at[p], s_sem.at[p], r_sem.at[p], me.at(g=g - 1)).start()
+
+    def flow_end(own, left, right, send, s_sem, l_sem, r_sem):
+        send[g] = own(g).astype(BF)
+
+        @pl.when(g > 0)
+        def _():
+            remote(send.at[g], left.at[g], s_sem.at[g], l_sem.at[g], me.across()).wait_recv()
+            send[g] = (send[g].astype(F32) + left[g].astype(F32)).astype(BF)
+
+        @pl.when(g < 3)
+        def _():
+            remote(send.at[g], right.at[g], s_sem.at[g], r_sem.at[g], me.across()).wait_recv()
+            send[g] = (send[g].astype(F32) + right[g].astype(F32)).astype(BF)
+
+        for p in range(4):
+            @pl.when(g != p)
+            def _():
+                remote(send.at[p], left.at[p], s_sem.at[p], l_sem.at[p], me.across()).wait_send()
+
+    def own_q(p):
+        return gq[:, :, p].astype(F32)
+
+    q_bufs = (ql, qr, qs, s_q, r_ql, r_qr)
+    for p in (3, 0, 2, 1):
+        flow(p, own_q, *q_bufs)
+
+    for c in o_copies:
+        c.wait()
+    o_sum[...] = (
+        out_ref[f].astype(F32) + o_got[0].astype(F32) + o_got[1].astype(F32) + o_got[2].astype(F32)
+    ).astype(BF)
+    c_oy = remote(o_sum.at[1 - b], yr_o, s_y.at[0, 4], r_y.at[0, 4], me.across())
+    c_oy.start()
+
+    vec = hop_end(2, vec)
+    v_copies.append(hop(3, vec))
+
+    def own_big(p):
+        return jnp.concatenate(
+            [
+                down_ref[b, p].astype(F32) + yr_down[p].astype(F32),
+                (up_ref[:, b, p].astype(F32) + yr_up[p].astype(F32)).reshape(128, 1024),
+            ],
+            axis=0,
+        )
+
+    big_bufs = (zl, zr, zs, s_z, r_zl, r_zr)
+    for p in (3, 0, 2, 1):
+        for c in y_copies[p]:
+            c.wait()
+        flow(p, own_big, *big_bufs)
+
+    c_xa.wait()
+    t2a[...] = (t1[lo, me.x].astype(F32) + xa[...].astype(F32)).astype(BF)
+    c_ra = remote(t2a.at[:, 1 - b], ra, s_dx.at[3], r_dx.at[3], me.across())
+    c_ra.start()
+    c_yb.wait()
+    t2b[...] = (t1[hi, :, b].astype(F32) + yb[...].astype(F32)).astype(BF)
+    c_rb = remote(t2b.at[:, 1 - me.x], rb, s_dx.at[4], r_dx.at[4], me.beside())
+    c_rb.start()
+
+    vec = hop_end(3, vec)
+    v_copies.append(hop(4, vec))
+
+    c_oy.wait()
+
+    def own_o(p):
+        return o_sum[b, p].astype(F32) + yr_o[p].astype(F32)
+
+    o_bufs = (ol, orr, os_, s_oz, r_ol, r_or)
+    for p in (3, 0, 2, 1):
+        flow(p, own_o, *o_bufs)
+
+    c_ra.wait()
+    c_rb.wait()
+    moved_buf[lo] = (t2a[:, b].astype(F32) + ra[...].astype(F32) + mid_ref[lo]).astype(BF)
+    moved_buf[hi] = (t2b[:, me.x].astype(F32) + rb[...].astype(F32) + mid_ref[hi]).astype(BF)
+
+    @pl.when(me.stays())
+    def _():
+        c = pltpu.make_async_copy(moved_buf, dx_ref, loc.at[0])
+        c.start()
+        c.wait()
+
+    @pl.when(jnp.logical_not(me.stays()))
+    def _():
+        remote(moved_buf, dx_ref, s_dx.at[5], r_dx.at[5], me.moved()).start()
+
+    def rows(size, q, other=False):
+        half = 1 - b if other else b
+        return pl.ds(pl.multiple_of((half * 4 + q) * size, size), size)
+
+    def unit_cols(src):
+        return pl.ds(pl.multiple_of(src * 1024, 1024), 1024)
+
+    def head_cols(src):
+        return pl.ds(pl.multiple_of((b * 4 + swapped(src)) * 128, 128), 128)
+
+    def q_rows(q):
+        return pl.ds(pl.multiple_of(q * 64, 64), 64)
+
+    flow_end(own_q, *q_bufs)
+    q_send[...] = qs[g]
+    three_out[:, q_rows(g), head_cols(f)] = q_send[f]
+    q_out = []
+    for k in (1, 2, 3):
+        c = remote(q_send.at[(f + k) % 4], three_out.at[:, q_rows(g), head_cols(f)], s_qf.at[k - 1], r_qf.at[f], me.fsdp(k))
+        c.start()
+        q_out.append(c)
+
+    flow_end(own_big, *big_bufs)
+    up_send[...] = zs[g, pl.ds(128, 128)].reshape(4, 32, 1024)
+    down_out[rows(128, g), :] = zs[g, pl.ds(0, 128)]
+    up_out[rows(32, g), unit_cols(f)] = up_send[f]
+    u_out = []
+    for k in (1, 2, 3):
+        c = remote(up_send.at[(f + k) % 4], up_out.at[rows(32, g), unit_cols(f)], s_u.at[k - 1], r_u.at[f], me.fsdp(k))
+        c.start()
+        u_out.append(c)
+    flow_end(own_o, *o_bufs)
+    o_out[rows(32, g), :] = os_[g]
+
+    for k in (1, 2, 3):
+        src = (f + k) % 4
+        remote(q_send.at[0], three_out.at[:, q_rows(g), head_cols(src)], s_qf.at[k - 1], r_qf.at[src], me.fsdp(k)).wait_recv()
+        remote(up_send.at[0], up_out.at[rows(32, g), unit_cols(src)], s_u.at[k - 1], r_u.at[src], me.fsdp(k)).wait_recv()
+        q_out[k - 1].wait_send()
+        u_out[k - 1].wait_send()
+
+    def pieces(q, send, recv, where, other=False):
+        half = 1 - b if other else b
+        parts = (
+            down_out.at[rows(128, q, other), :],
+            up_out.at[rows(32, q, other), :],
+            o_out.at[rows(32, q, other), :],
+            three_out.at[:, q_rows(q), pl.ds(pl.multiple_of(half * 512, 512), 512)],
+        )
+        return [remote(part, part, send.at[i, q], recv.at[i, q], where) for i, part in enumerate(parts)]
+
+    def spread(q, to_right, to_left):
+        for c in pieces(q, s_ay, r_ay, me.across()):
+            c.start()
+        if to_right:
+            @pl.when(g < 3)
+            def _():
+                for c in pieces(q, s_ag.at[0], r_ag, me.at(g=g + 1)):
+                    c.start()
+        if to_left:
+            @pl.when(g > 0)
+            def _():
+                for c in pieces(q, s_ag.at[1], r_ag, me.at(g=g - 1)):
+                    c.start()
+
+    spread(g, True, True)
+    for d in (1, 2, 3):
+        @pl.when(g >= d)
+        def _():
+            for c in pieces(g - d, s_ag.at[0], r_ag, me.across()):
+                c.wait_recv()
+            spread(g - d, True, False)
+
+        @pl.when(g + d <= 3)
+        def _():
+            for c in pieces(g + d, s_ag.at[1], r_ag, me.across()):
+                c.wait_recv()
+            spread(g + d, False, True)
+
+    vec = hop_end(4, vec)
+    sums_ref[...] = vec
+
+    @pl.when(jnp.logical_not(me.stays()))
+    def _():
+        remote(moved_buf, dx_ref, s_dx.at[5], r_dx.at[5], me.moved()).wait()
+
+    for q in range(4):
+        for c in pieces(q, s_ay, r_ay, me.across()):
+            c.wait_send()
+
+        @pl.when((g >= q) & (g < 3))
+        def _():
+            for c in pieces(q, s_ag.at[0], r_ag, me.across()):
+                c.wait_send()
+
+        @pl.when((g <= q) & (g > 0))
+        def _():
+            for c in pieces(q, s_ag.at[1], r_ag, me.across()):
+                c.wait_send()
+
+        for c in pieces(q, s_ay, r_ay, me.across(), other=True):
+            c.wait_recv()
+
+
+def tail(x_all, g3, w3, down, up, out, mid, vec):
+    dma = pltpu.SemaphoreType.DMA
+    v = pltpu.VMEM
+    scratch = [
+        v((16, 2, 2, 2, 16, 1024), BF), v((16, 2, 2, 16, 1024), BF), v((16, 2, 2, 16, 1024), BF),
+        v((8, 2, 16, 1024), BF), v((8, 2, 16, 1024), BF), v((8, 2, 16, 1024), BF), v((8, 2, 16, 1024), BF),
+        v((8, 16, 1024), BF), v((8, 16, 1024), BF), v((16, 16, 1024), BF),
+        v((4, 128, 1024), BF), v((4, 4, 32, 1024), BF), v((4, 256, 1024), BF), v((4, 256, 1024), BF),
+        v((4, 256, 1024), BF), v((4, 32, 1024), BF), v((4, 32, 1024), BF),
+        v((3, 2, 4, 32, 1024), BF), v((2, 4, 32, 1024), BF), v((4, 32, 1024), BF),
+        v((4, 32, 1024), BF), v((4, 32, 1024), BF), v((4, 32, 1024), BF),
+        v((4, 3, 4, 64, 128), BF), v((4, 4, 3, 64, 128), BF), v((4, 4, 3, 64, 128), BF), v((4, 4, 3, 64, 128), BF),
+        v((4, 3, 64, 128), BF),
+        v((5, 16, 1024), F32), v((5, 16, 1024), F32),
+        dma((6,)), dma((6,)), dma((2, 5)), dma((2, 5)), dma((4,)), dma((4,)), dma((4,)),
+        dma((3,)), dma((4,)), dma((3,)), dma((3,)), dma((4,)), dma((4,)), dma((4,)), dma((4,)), dma((4,)), dma((4,)),
+        dma((3,)), dma((4,)), dma((5,)), dma((5,)), dma((2, 4, 4)), dma((4, 4)), dma((4, 4)), dma((4, 4)), dma((1,)),
+    ]
+    return pl.pallas_call(
+        tail_kernel,
+        out_shape=(
+            jax.ShapeDtypeStruct((1024, 1024), BF),
+            jax.ShapeDtypeStruct((256, 4096), BF),
+            jax.ShapeDtypeStruct((256, 1024), BF),
+            jax.ShapeDtypeStruct((3, 256, 1024), BF),
+            jax.ShapeDtypeStruct((16, 16, 1024), BF),
+            jax.ShapeDtypeStruct((16, 1024), F32),
+        ),
+        in_specs=[VMEM] * 8,
+        out_specs=(VMEM,) * 6,
+        scratch_shapes=scratch,
+        compiler_params=pltpu.CompilerParams(collective_id=1, has_side_effects=True, vmem_limit_bytes=60 * 2**20),
+        cost_estimate=pl.CostEstimate(flops=4 * 10**9, bytes_accessed=40 * 2**20, transcendentals=0),
+    )(x_all, g3, w3, down.reshape(2, 4, 128, 1024), up.reshape(4, 2, 4, 32, 1024), out.reshape(4, 2, 4, 32, 1024), mid.reshape(16, 16, 1024), vec)
 
 
 def body(
@@ -239,10 +644,11 @@
 
     def to_tokens(block):
         parts = block.reshape(laps, GROUP, stripe, PAIR).transpose(1, 0, 2, 3).reshape(GROUP, mine, PAIR)
-        return swap_group(parts).transpose(1, 0, 2).reshape(mine, width)
+        got = swap_group(parts).reshape(n_f, 2, mine, PAIR)
+        return got.transpose(2, 1, 0, 3).reshape(mine, width)
 
     def to_heads(block):
-        parts = block.reshape(mine, GROUP, PAIR).transpose(1, 0, 2)
+        parts = block.reshape(mine, 2, n_f, PAIR).transpose(2, 1, 0, 3)
         got = swap_group(parts).reshape(GROUP, laps, stripe, PAIR)
         return got.transpose(1, 0, 2, 3).reshape(GROUP * mine, PAIR)
 
@@ -250,9 +656,6 @@
         return lax.all_to_all(w.reshape(w.shape[0], n_f, -1).transpose(1, 0, 2), "fsdp", 0, 0).reshape(
             n_f * w.shape[0], -1
         )
-
-    def rows_back(w):
-        return lax.all_to_all(w.reshape(n_f, w.shape[0] // n_f, w.shape[1]), "fsdp", 0, 0)
 
     row_id = swap[g]
     ordered_all = jnp.sum(
@@ -290,11 +693,11 @@
     inputs = relocate(tokens.reshape(mine, width))
     upstream = relocate(cotangent.reshape(mine, width)).astype(F32)
     x_all = gather_group(inputs)
-    w_three = jnp.stack([query_w, key_w, value_w]).reshape(3, -1, n_f, 2, PAIR)
-    w_three = lax.dynamic_index_in_dim(w_three, b, 3, keepdims=False)
+    w_three = jnp.stack([query_w, key_w, value_w]).reshape(3, -1, 2, n_f, PAIR)
+    w_three = lax.dynamic_index_in_dim(w_three, b, 2, keepdims=False)
     w_three = order(w_three.transpose(2, 1, 0, 3).reshape(n_f, -1, 3 * PAIR))
     w_three = lax.all_to_all(w_three, "fsdp", 0, 0).reshape(width, 3 * PAIR)
-    here = u * PAIR
+    here = (b * n_f + swap[f]) * PAIR
     bias3 = jnp.concatenate(
         [
             lax.dynamic_slice_in_dim(query_b, here, PAIR),
@@ -333,15 +736,13 @@
     grad_ffn = lax.all_gather(grad_ffn_own, "fsdp", axis=0, tiled=True)
     part_down = dense_in(hidden, grad_ffn).astype(BF)
     grad_pre = (dense_back(grad_ffn, reduce_w) * gelu_slope(pre_act)).astype(BF)
-    grad_expand_b = lax.dynamic_update_slice_in_dim(
-        jnp.zeros_like(expand_b), jnp.sum(grad_pre.astype(F32), axis=0), f * units, 0
-    )
+    grad_expand_b = jnp.sum(grad_pre.astype(F32), axis=0)
     part_up = dense_in(normed_low, grad_pre).astype(BF)
     grad_normed = lax.psum_scatter(dense_back(grad_pre, w_up).astype(BF), "fsdp", tiled=True).astype(F32) + grad_mid2
     grad_mid1, grad_attn_gain, grad_attn_shift = norm_back(grad_normed, x_hat1, inv_std1, attn_gain)
     grad_branch = grad_mid1.astype(BF)
     grad_output_b = jnp.sum(grad_branch.astype(F32), axis=0)
-    part_out = lax.psum_scatter(dense_in(attended, grad_branch).astype(BF), "fsdp", tiled=True)
+    part_out = dense_in(attended, grad_branch).astype(BF)
     grad_att = to_heads(dense_back(grad_branch, w_output).astype(BF))
 
     grad_q, grad_k, grad_v = attend_back(
@@ -358,32 +759,29 @@
     sums3 = jnp.sum(grad_three.astype(F32), axis=0)
     grad_query_b = lax.dynamic_update_slice_in_dim(jnp.zeros_like(query_b), sums3[:PAIR], here, 0)
     grad_value_b = lax.dynamic_update_slice_in_dim(jnp.zeros_like(value_b), sums3[2 * PAIR :], here, 0)
-    part_three = dense_in(x_all, grad_three).astype(BF)
-    back = dense_back(grad_three, w_three).astype(BF)
-    back = back.reshape(laps, GROUP, stripe, width).transpose(1, 0, 2, 3).reshape(n_f, 2, mine, width)
-    back = lax.psum_scatter(order(back), "fsdp", scatter_dimension=0)
-    back = lax.psum_scatter(back, "ctx", scatter_dimension=0, axis_index_groups=pairs)
-    grad_inputs = relocate(back.astype(F32) + grad_mid1).reshape(tok_shape)
-
-    got = order(rows_back(part_three)).reshape(n_f, -1, 3, PAIR)
-    got = got.transpose(2, 1, 0, 3)[:, :, :, None, :]
-    mask = (jnp.arange(2) == b)[None, None, None, :, None]
-    share_three = jnp.where(mask, got, BF(0)).reshape(3, got.shape[1], width)
-    share_up = rows_back(part_up).transpose(1, 0, 2).reshape(-1, n_f * units)
-    share_three, share_out, share_up, share_down = lax.psum(
-        (share_three, part_out, share_up, part_down), "ctx"
-    )
-    share_three = share_three.astype(F32)
+    here_rows = jnp.zeros((n_f, units), F32)
+    sums = jnp.concatenate(
+        [
+            jnp.stack(
+                [grad_query_b, grad_value_b, grad_output_b, grad_attn_gain, grad_attn_shift, grad_reduce_b, grad_ffn_gain, grad_ffn_shift]
+            ),
+            lax.dynamic_update_slice_in_dim(here_rows, grad_expand_b[None], f, 0),
+            here_rows,
+        ]
+    )
+    share_down, share_up, share_out, share_three, moved, sums = tail(
+        x_all, grad_three, w_three, part_down, part_up, part_out, grad_mid1, sums
+    )
+    grad_inputs = moved.reshape(tok_shape).astype(F32)
+    shares = tuple(part.astype(F32) for part in (share_three, share_out, share_up, share_down)) + (sums,)
+    if chunks > 1:
+        shares = lax.psum(shares, "ctx", axis_index_groups=same_place)
+    share_three, share_out, share_up, share_down, sums = shares
     (
-        grad_query_b, grad_value_b, grad_output_b, grad_attn_gain, grad_attn_shift, grad_expand_b,
-        grad_reduce_b, grad_ffn_gain, grad_ffn_shift,
-    ) = lax.psum(
-        (
-            grad_query_b, grad_value_b, grad_output_b, grad_attn_gain, grad_attn_shift, grad_expand_b,
-            grad_reduce_b, grad_ffn_gain, grad_ffn_shift,
-        ),
-        ("ctx", "fsdp"),
-    )
+        grad_query_b, grad_value_b, grad_output_b, grad_attn_gain, grad_attn_shift, grad_reduce_b,
+        grad_ffn_gain, grad_ffn_shift,
+    ) = (sums[i] for i in range(8))
+    grad_expand_b = sums[8 : 8 + n_f].reshape(-1)
     return (
         layer_out,
         grad_inputs,
@@ -392,13 +790,13 @@
         share_three[1],
         share_three[2],
         grad_value_b,
-        share_out.astype(F32),
+        share_out,
         grad_output_b,
         grad_attn_gain,
         grad_attn_shift,
-        share_up.astype(F32),
+        share_up,
         grad_expand_b,
-        share_down.astype(F32),
+        share_down,
         grad_reduce_b,
         grad_ffn_gain,
         grad_ffn_shift,

time: 788 us -> 656 us (0.83)
  Pallas kernels: 41.3 us -> 269 us
  waiting for transfers between devices: 382 us -> 165 us
  blocking collectives: 168 us -> 37.6 us
    pallas_call x0 -> x1, Pallas kernels: none -> 228 us  [tail(): pl.pallas_call(tail_kernel, out_shape=(jax.ShapeDtypeStruct((1024, 1024),...]
    psum x1 -> x0, waiting for transfers between devices: 133 us -> none  [body(): lax.psum((share_three, part_out, share_up, part_down), 'ctx')]
    psum x1 -> x0, blocking collectives: 109 us -> none  [body(): lax.psum((grad_query_b, grad_value_b, grad_output_b, grad_attn_gain, grad...]
    reduce_scatter x3 -> x0, waiting for transfers between devices: 79.1 us -> none  [the longest x1 49.5 us: body(): back = lax.psum_scatter(order(back), 'fsdp', scatter_dimension=0)]
    all_to_all x2 -> x1, blocking collectives: 22.5 us -> 11.2 us  [swap_group(): block = lax.all_to_all(block, 'fsdp', 0, 0)]
    reduce_scatter x1, waiting for transfers between devices: 31.5 us -> 21.2 us  [body(): lax.psum_scatter(dense_back(grad_pre, w_up).astype(BF), 'fsdp', tiled=True)]
    all_to_all x2 -> x1, blocking collectives: 20.6 us -> 10.3 us  [swap_group(): block = lax.all_to_all(block, 'ctx', 1, 1, axis_index_groups=pairs)]
    unnamed x88 -> x83, local copies, waits for them, and re-layouts: 19.1 us -> 23.6 us
  transfers between devices with their start and end apart: 19 -> 14, of which waited for: 11 -> 8; matrix products, arithmetic and copies ran while one was open for 11% -> 8% of each run, Pallas kernels for 2% -> 3%
where the time goes in v3:
time: 656 us; the launch traced here: 647 us
  Pallas kernels  269 us (41%)
  waiting for transfers between devices  165 us (25%)
  local copies, waits for them, and re-layouts  50.2 us (8%)
  matrix products  48.8 us (7%)
  blocking collectives  37.6 us (6%)
  starting transfers between devices  31.1 us (5%)
  other arithmetic  26.9 us (4%)
  between operations  18.7 us (3%)
    pallas_call x1, Pallas kernels, tail(): pl.pallas_call(tail_kernel, out_shape=(jax.ShapeDtypeStruct((1024, 1024),...  228 us
    all_gather x1, waiting for transfers between devices, gather_group(): both = lax.all_gather(block, 'ctx', axis_index_groups=pairs)  43.2 us
    all_to_all x1, waiting for transfers between devices, columns(): lax.all_to_all(w.reshape(w.shape[0], n_f, -1).transpose(1, 0, 2), 'fsdp',...  36.1 us
    reduce_scatter x1, waiting for transfers between devices, body(): lax.psum_scatter(dense(hidden, reduce_w).astype(BF), 'fsdp', tiled=True)  28 us
    all_gather x1, waiting for transfers between devices, body(): grad_ffn = lax.all_gather(grad_ffn_own, 'fsdp', axis=0, tiled=True)  24.9 us
    unnamed x83, local copies, waits for them, and re-layouts  23.6 us
    dot_general x4, matrix products, dense(): return jnp.dot(left, right, preferred_element_type=F32)  22.9 us
    pallas_call x1, Pallas kernels, attend_back(): pl.pallas_call(functools.partial(attend_back_kernel, BQ, BK, chunks), out...  22.8 us
  transfers between devices with their start and end apart: 14, of which 8 were waited for; matrix products, arithmetic and copies ran while one was open for 8% of the time, Pallas kernels for 3%

profile of v3, /device:TPU:0, one launch (start us, length us, event | category | flops | bytes accessed | tf_op | source)
XLA Modules:
  0.0 646.9 jit_solution(15765389069041406370)
XLA Ops:
  10.0 43.2 %all-gather.15.cloned.1.call-done = bf16[512,1024]{1,0:T(8,128)(2,1)} async-done(((bf16[256,1024]{1,0:T(8,128)(2,1)}), bf16[512,1024]{1,0:T(8,128)(2,1)}) %all-gather.15.cloned.1.call-update) | async-done | bytes 1048592 | tf_op jit(solution)/shard_map/all_gather | solution.py:634
  63.8 4.2 all-to-all-start
  72.5 16.1 %all-reduce.1 = s32[4,3]{1,0:T(4,128)S(1)} all-reduce(s32[4,3]{1,0:T(4,128)S(1)} %reshape.359), channel_id=2, replica_groups=mesh['ctx'=8,'fsdp'=4] {'fsdp'}, use_global_device_ids=true, to_apply=%add | all-reduce | flops 12 | bytes 96
  93.1 2.6 copy.149
  97.8 2.6 slice_bitcast_fusion.6
  104.9 18.4 %shard_map.323 = (bf16[2048,128]{1,0:T(8,128)(2,1)S(1)}, f32[4096,1]{1,0:T(8,128)S(1)}) custom-call(s32[8,1]{1,0:T(8,128)S(1)} %copy.150.lo_ref, s32[8,1]{1,0:T(8,128)S(1)} %copy.151.hi_ref, bf16[2048,128]{1,0:T(8,128)(2,1)S(1)} %get-tuple-element.65.q_ref, bf16[2048,128]{1,0:T(8,128)(2,1)S(1)} %get-tuple-element.64.k_ref, ...), custom_call_target="tpu_custom_call" | custom-call | tf_op jit(solution)/shard_map/pallas_call | solution.py:170
  123.5 11.2 %all_to_all.30 = bf16[4,2,256,128]{3,2,1,0:T(8,128)(2,1)S(1)} all-to-all(bf16[4,2,256,128]{3,2,1,0:T(8,128)(2,1)S(1)} %pad_maximum_fusion.2), channel_id=1, replica_groups=mesh['ctx'=8,'fsdp'=4] {'fsdp'}, dimensions={0} | all-to-all | bytes 1048576 | tf_op jit(solution)/shard_map/all_to_all | solution.py:641
  134.8 10.3 %all_to_all.31 = bf16[4,2,256,128]{3,2,0,1:T(8,128)(2,1)S(1)} all-to-all(bf16[4,2,256,128]{3,2,0,1:T(8,128)(2,1)S(1)} %copy.154), channel_id=1, replica_groups={{0,4},{8,12},{16,20},{24,28},{1,5},{9,13},{17,21},{25,29},{2,6},{10,14}..., dimensions={1} | all-to-all | bytes 1048576 | tf_op jit(solution)/shard_map/all_to_all | solution.py:642
  146.6 2.7 fusion.58
  150.6 4.1 copy.159
  154.7 4.5 all-to-all-start.3
  160.1 36.1 %all-to-all-done.3 = bf16[4,256,1024]{1,2,0:T(8,128)(2,1)} async-done(((bf16[4,256,1024]{1,2,0:T(8,128)(2,1)}), bf16[4,256,1024]{1,2,0:T(8,128)(2,1)}, u32[]{:S(2)}, u32[]{:S(2)}) %all-to-all-start.3) | async-done | bytes 2097184 | tf_op jit(solution)/shard_map/all_to_all | solution.py:656
  196.2 4.0 copy.160
  200.1 14.2 %fusion.2 = (bf16[1024,1024]{1,0:T(8,128)(2,1)S(1)}, f32[1024,1024]{1,0:T(8,128)}) fusion(f32[1024]{0:T(1024)S(1)} %dynamic_slice.28, bf16[1024,1024]{1,0:T(8,128)(2,1)} %all-gather.11.cloned.1.call-done, bf16[1024,1024]{1,0:T(8,128)(2,1)} %bitcast.138), kind=kOutput, calls=%fused_computation.4 | convolution fusion | flops 2216689664 | bytes 10489856 | tf_op jit(solution)/shard_map/dot_general | solution.py:19
  215.6 3.7 convolution_convert_fusion.4
  219.4 5.4 collective-permute-start.2
  224.8 28.0 %reduce-scatter.3.cloned.1.call-done = bf16[256,1024]{1,0:T(8,128)(2,1)} async-done(((bf16[1024,1024]{1,0:T(8,128)(2,1)}), bf16[256,1024]{1,0:T(8,128)(2,1)}) %reduce-scatter.3.cloned.1.call-update) | async-done | bytes 524304 | tf_op jit(solution)/shard_map/reduce_scatter | solution.py:730
  256.1 2.8 convert_reduce_fusion.3
  259.3 24.9 %all-gather.13.cloned.1.call-done = bf16[1024,1024]{1,0:T(8,128)(2,1)} async-done(((bf16[256,1024]{1,0:T(8,128)(2,1)}), bf16[1024,1024]{1,0:T(8,128)(2,1)}) %all-gather.13.cloned.1.call-update) | async-done | bytes 2097168 | tf_op jit(solution)/shard_map/all_gather | solution.py:736
  284.2 6.3 convert_reduce_fusion
  291.8 3.7 convolution_convert_fusion.3
  295.5 5.4 collective-permute-start.1
  301.0 6.0 convolution_convert_fusion.2
  307.0 21.2 %reduce-scatter.5.cloned.1.call-done = bf16[256,1024]{1,0:T(8,128)(2,1)} async-done(((bf16[1024,1024]{1,0:T(8,128)(2,1)}), bf16[256,1024]{1,0:T(8,128)(2,1)}) %reduce-scatter.5.cloned.1.call-update) | async-done | bytes 524304 | tf_op jit(solution)/shard_map/reduce_scatter | solution.py:741
  335.1 4.7 all-to-all-start.4
  339.9 6.0 convolution_convert_fusion.1
  345.9 3.6 all-to-all-done.4
  351.4 4.5 all-to-all-start.5
  355.9 3.1 convolution_convert_fusion
  359.0 4.9 all-to-all-done.5
  365.9 22.8 %shard_map.324 = (bf16[2048,128]{1,0:T(8,128)(2,1)}, bf16[2048,128]{1,0:T(8,128)(2,1)}, bf16[2048,128]{1,0:T(8,128)(2,1)}) custom-call(s32[8,1]{1,0:T(8,128)} %copy-done.8, s32[8,1]{1,0:T(8,128)} %copy-done.9, bf16[2048,128]{1,0:T(8,128)(2,1)} %copy-done.4, bf16[2048,128]{1,0:T(8,128)(2,1)} %copy-done.3, bf16[2048,128]{1,0:T(8,128)(2,1)} %copy-done.2, ...), custom_call_target="tpu_custom_call" | custom-call | tf_op jit(solution)/shard_map/pallas_call | solution.py:182
  395.1 227.6 %shard_map.325 = (bf16[1024,1024]{1,0:T(8,128)(2,1)}, bf16[256,4096]{1,0:T(8,128)(2,1)}, bf16[256,1024]{1,0:T(8,128)(2,1)}, bf16[3,256,1024]{2,1,0:T(8,128)(2,1)...) custom-call(bf16[2048,1024]{1,0:T(8,128)(2,1)} %bitcast.132, bf16[2048,384]{1,0:T(8,128)(2,1)} %copy-done.14, ...), custom_call_target="tpu_custom_call" | custom-call | flops 4000000000 | bytes 41943040 | tf_op jit(solution)/shard_map/pallas_call | solution.py:583
  (183 shorter events, 69.5 us)
Async XLA Ops:
  7.2 208.5 %copy-start = (bf16[1024,1024]{1,0:T(8,128)(2,1)S(1)}, bf16[1024,1024]{1,0:T(8,128)(2,1)}, u32[]{:S(2)}) copy-start(bf16[1024,1024]{1,0:T(8,128)(2,1)} %param.34) | copy-start | bytes 6291460
  7.2 46.0 %all-gather.15.cloned.1.call-start = ((), (), s32[]{:S(2)}) async-start(), calls=%async_computation.13 | async-start | bytes 1572864 | tf_op jit(solution)/shard_map/all_gather | solution.py:634
  7.2 1.8 collective-permute-start
  9.9 87.9 %all-gather.17.cloned.1.call-start = ((), (), s32[]{:S(2)}) async-start(), calls=%async_computation.14 | async-start | bytes 5242880 | tf_op jit(solution)/shard_map/all_gather | solution.py:635
  59.7 9.2 %copy-start.28 = (s32[1,3]{1,0:T(1,128)S(1)}, s32[1,3]{1,0:T(1,128)}, u32[]{:S(2)}) copy-start(s32[1,3]{1,0:T(1,128)} %param.21) | copy-start | bytes 40
  59.7 9.4 %copy-start.30 = (u32[32]{0:T(128)S(1)}, u32[32]{0:T(128)}, u32[]{:S(2)}) copy-start(u32[32]{0:T(128)} %constant.223) | copy-start | bytes 388
  59.7 10.9 %copy-start.27 = (s32[4]{0:T(128)S(1)}, s32[4]{0:T(128)}, u32[]{:S(2)}) copy-start(s32[4]{0:T(128)} %constant.216.clone) | copy-start | bytes 52
  63.8 29.2 %all-to-all-start = ((bf16[4,256,384]{1,2,0:T(8,128)(2,1)}), bf16[4,256,384]{1,2,0:T(8,128)(2,1)}, u32[]{:S(2)}, u32[]{:S(2)}) async-start(bf16[4,256,384]{1,2,0:T(8,128)(2,1)} %pad_maximum_fusion.1), calls=%async_computation | async-start | bytes 1572864 | tf_op jit(solution)/shard_map/all_to_all | solution.py:699
  68.0 78.5 %all-gather.9.cloned.1.call-start = ((), (), s32[]{:S(2)}) async-start(), calls=%async_computation.8 | async-start | bytes 2621440 | tf_op jit(solution)/shard_map/all_gather | solution.py:720
  68.8 131.3 %all-gather.11.cloned.1.call-start = ((), (), s32[]{:S(2)}) async-start(), calls=%async_computation.9 | async-start | bytes 2621440 | tf_op jit(solution)/shard_map/all_gather | solution.py:724
  89.5 15.3 %copy-start.7 = (s32[2048]{0:T(1024)}, s32[2048]{0:T(1024)S(1)}, u32[]{:S(2)}) copy-start(s32[2048]{0:T(1024)S(1)} %get-tuple-element.48) | copy-start | bytes 24580
  90.2 14.7 %copy-start.8 = (s32[8,1]{1,0:T(8,128)}, s32[8,1]{1,0:T(8,128)S(1)}, u32[]{:S(2)}) copy-start(s32[8,1]{1,0:T(8,128)S(1)} %copy.150.lo_ref) | copy-start | bytes 100
  90.4 14.4 %copy-start.9 = (s32[8,1]{1,0:T(8,128)}, s32[8,1]{1,0:T(8,128)S(1)}, u32[]{:S(2)}) copy-start(s32[8,1]{1,0:T(8,128)S(1)} %copy.151.hi_ref) | copy-start | bytes 100
  93.0 11.9 %copy-start.1 = (s32[2048,1]{1,0:T(8,128)}, s32[2048,1]{1,0:T(8,128)S(1)}, u32[]{:S(2)}) copy-start(s32[2048,1]{1,0:T(8,128)S(1)} %copy.152.sq_ref) | copy-start | bytes 24580
  104.8 40.3 %copy-start.2 = (bf16[2048,128]{1,0:T(8,128)(2,1)}, bf16[2048,128]{1,0:T(8,128)(2,1)S(1)}, u32[]{:S(2)}) copy-start(bf16[2048,128]{1,0:T(8,128)(2,1)S(1)} %get-tuple-element.63.v_ref) | copy-start | bytes 1572868
  104.8 40.3 %copy-start.3 = (bf16[2048,128]{1,0:T(8,128)(2,1)}, bf16[2048,128]{1,0:T(8,128)(2,1)S(1)}, u32[]{:S(2)}) copy-start(bf16[2048,128]{1,0:T(8,128)(2,1)S(1)} %get-tuple-element.64.k_ref) | copy-start | bytes 1572868
  104.8 40.3 %copy-start.4 = (bf16[2048,128]{1,0:T(8,128)(2,1)}, bf16[2048,128]{1,0:T(8,128)(2,1)S(1)}, u32[]{:S(2)}) copy-start(bf16[2048,128]{1,0:T(8,128)(2,1)S(1)} %get-tuple-element.65.q_ref) | copy-start | bytes 1572868
  123.3 21.9 %copy-start.5 = (f32[4096,1]{1,0:T(8,128)}, f32[4096,1]{1,0:T(8,128)S(1)}, u32[]{:S(2)}) copy-start(f32[4096,1]{1,0:T(8,128)S(1)} %get-tuple-element.29.lse_ref) | copy-start | bytes 49156
  123.4 21.9 %copy-start.6 = (bf16[2048,128]{1,0:T(8,128)(2,1)}, bf16[2048,128]{1,0:T(8,128)(2,1)S(1)}, u32[]{:S(2)}) copy-start(bf16[2048,128]{1,0:T(8,128)(2,1)S(1)} %get-tuple-element.28.o_ref) | copy-start | bytes 1572868
  123.4 23.2 %copy-start.22 = (f32[1024]{0:T(1024)S(1)}, f32[1024]{0:T(1024)}, u32[]{:S(2)}) copy-start(f32[1024]{0:T(1024)} %param.29) | copy-start | bytes 12292
  154.7 41.5 %all-to-all-start.3 = ((bf16[4,256,1024]{1,2,0:T(8,128)(2,1)}), bf16[4,256,1024]{1,2,0:T(8,128)(2,1)}, u32[]{:S(2)}, u32[]{:S(2)}) async-start(bf16[4,256,1024]{1,2,0:T(8,128)(2,1)} %bitcast.128), calls=%async_computation.3 | async-start | bytes 4194304 | tf_op jit(solution)/shard_map/all_to_all | solution.py:656
  159.2 93.6 %reduce-scatter.3.cloned.1.call-start = ((), (), s32[]{:S(2)}) async-start(), calls=%async_computation.10 | async-start | bytes 2621440 | tf_op jit(solution)/shard_map/reduce_scatter | solution.py:730
  215.6 37.1 %copy-start.25 = (f32[1024]{0:T(1024)S(1)}, f32[1024]{0:T(1024)}, u32[]{:S(2)}) copy-start(f32[1024]{0:T(1024)} %param.35) | copy-start | bytes 12292
  219.3 35.2 %copy-start.24 = (f32[1024]{0:T(1024)S(1)}, f32[1024]{0:T(1024)}, u32[]{:S(2)}) copy-start(f32[1024]{0:T(1024)} %param.36) | copy-start | bytes 12292
  219.3 36.8 %copy-start.26 = (f32[1024]{0:T(1024)S(1)}, f32[1024]{0:T(1024)}, u32[]{:S(2)}) copy-start(f32[1024]{0:T(1024)} %param.37) | copy-start | bytes 12292
  219.4 64.8 %all-gather.13.cloned.1.call-start = ((), (), s32[]{:S(2)}) async-start(), calls=%async_computation.11 | async-start | bytes 2621440 | tf_op jit(solution)/shard_map/all_gather | solution.py:736
  219.4 35.1 %collective-permute-start.2 = (bf16[256,1024]{1,0:T(8,128)(2,1)}, bf16[256,1024]{1,0:T(8,128)(2,1)}, u32[]{:S(2)}, u32[]{:S(2)}) collective-permute-start(bf16[256,1024]{1,0:T(8,128)(2,1)} %bitcast.175), channel_id=1, source_target_pairs={{0,0},{1,16},{2,8},{3,24},{4,4},{5,20},{6,12},{7,28},{8,2},{9,18},... | collective-permute-start | bytes 1572872 | tf_op jit(solution)/shard_map/ppermute | solution.py:628
  259.0 69.2 %reduce-scatter.5.cloned.1.call-start = ((), (), s32[]{:S(2)}) async-start(), calls=%async_computation.12 | async-start | bytes 2621440 | tf_op jit(solution)/shard_map/reduce_scatter | solution.py:741
  295.5 5.4 collective-permute-start.1
  335.1 14.4 %all-to-all-start.4 = ((bf16[4,2,256,128]{3,2,1,0:T(8,128)(2,1)}), bf16[4,2,256,128]{3,2,1,0:T(8,128)(2,1)}, u32[]{:S(2)}, u32[]{:S(2)}) async-start(bf16[4,2,256,128]{3,2,1,0:T(8,128)(2,1)} %pad_maximum_fusion.4), calls=%async_computation.6 | async-start | bytes 1048576 | tf_op jit(solution)/shard_map/all_to_all | solution.py:641
  339.9 16.0 %copy-start.11 = (f32[256,1024]{1,0:T(8,128)S(1)}, f32[256,1024]{1,0:T(8,128)}, u32[]{:S(2)}) copy-start(f32[256,1024]{1,0:T(8,128)} %copy-done.10) | copy-start | bytes 3145732
  351.4 12.5 %all-to-all-start.5 = ((bf16[4,2,256,128]{3,2,0,1:T(8,128)(2,1)}), bf16[4,2,256,128]{3,2,0,1:T(8,128)(2,1)}, u32[]{:S(2)}, u32[]{:S(2)}) async-start(bf16[4,2,256,128]{3,2,0,1:T(8,128)(2,1)} %copy.162), calls=%async_computation.7 | async-start | bytes 1048576 | tf_op jit(solution)/shard_map/all_to_all | solution.py:642
  (15 other events, 49.1 us)
Sparse Core Ops, SparseCore 0:
  10.2 42.9 all-gather.14
  54.7 42.9 all-gather.16
  99.3 22.5 all-gather.8
  150.7 36.5 all-gather.10
  219.5 33.1 reduce-scatter.2
  259.1 25.0 all-gather.12
  295.7 32.4 reduce-scatter.4

commit v4 on v3

--- a/solution.py
+++ b/solution.py
@@ -598,6 +598,233 @@
     )(x_all, g3, w3, down.reshape(2, 4, 128, 1024), up.reshape(4, 2, 4, 32, 1024), out.reshape(4, 2, 4, 32, 1024), mid.reshape(16, 16, 1024), vec)
 
 
+def tile_cols(i, size):
+    return pl.ds(pl.multiple_of(i * size, size), size)
+
+
+def middle_kernel(
+    heads_ref, x_ref, up_ref, wo_ref, wu_ref, wd_ref, par_ref,
+    layer_ref, down_out, upg_out, og_out, gatt_ref, mid1_ref, vec_ref,
+    att, nl, gff, slope, hid, gpre, normed, xhat, rstd, work, moved_buf, gbr, gas, ps, pr,
+    s_a, r_a, s_b, r_b, s_g, r_g, s_p, r_p, s_m, r_m, loc,
+):
+    me = Place()
+    f, b = me.f, me.b
+    sib = f + 1 - 2 * me.core
+    xs = (f + 2) % 4
+    xo = xs + 1 - 2 * me.core
+    peers = [me.at(f=(f + k % 4) % 4, b=(b + k // 4) % 2) for k in range(1, 8)]
+    meet(me, peers, True)
+    slot = swapped(f) * 2 + b
+    unit = b * 4 + swapped(f)
+
+    def peer_slot(k, sign):
+        pf, pb = (f + sign * (k % 4) + 4) % 4, (b + k // 4) % 2
+        return swapped(pf) * 2 + pb, pb * 4 + swapped(pf)
+
+    def lanes(index):
+        return pl.ds(pl.multiple_of(index * PAIR, PAIR), PAIR)
+
+    for k in range(1, 8):
+        where, _ = peer_slot(k, 1)
+        remote(heads_ref.at[:, where], att.at[:, :, lanes(unit)], s_a.at[k - 1], r_a.at[k - 1], peers[k - 1]).start()
+    att[:, :, lanes(unit)] = heads_ref[:, slot]
+    for k in range(1, 8):
+        _, theirs = peer_slot(k, -1)
+        remote(heads_ref.at[:, slot], att.at[:, :, lanes(theirs)], s_a.at[k - 1], r_a.at[k - 1], peers[k - 1]).wait()
+
+    def row(i):
+        return par_ref[pl.ds(i, 1), :]
+
+    def att_rows():
+        return att[...].reshape(256, 1024)
+
+    def proj(i, carry):
+        cols = tile_cols(i, 512)
+        work[:, cols] = dense(att_rows(), wo_ref[:, cols])
+        return carry
+
+    lax.fori_loop(0, 2, proj, 0)
+    value, x_hat, inv = norm_fwd(x_ref[...].astype(F32) + work[...] + row(0), row(1), row(2))
+    normed[...] = value
+    xhat[...] = x_hat
+    rstd[...] = inv
+    nl[f] = value.astype(BF)
+
+    def share(buf, t):
+        to_sib = remote(buf.at[f], buf.at[f], s_g.at[t, 0], r_g.at[t, 0], me.sibling())
+        to_x = remote(buf.at[f], buf.at[f], s_g.at[t, 1], r_g.at[t, 1], me.beside())
+        to_x.start()
+        to_sib.start()
+
+        def from_sib():
+            to_sib.wait_send()
+            remote(buf.at[sib], buf.at[sib], s_g.at[t, 0], r_g.at[t, 0], me.sibling()).wait_recv()
+
+        def from_x():
+            to_x.wait_send()
+            remote(buf.at[xs], buf.at[xs], s_g.at[t, 1], r_g.at[t, 1], me.beside()).wait_recv()
+            remote(buf.at[xs], buf.at[xs], s_g.at[t, 2], r_g.at[t, 2], me.sibling()).start()
+
+        def from_other():
+            remote(buf.at[xs], buf.at[xs], s_g.at[t, 2], r_g.at[t, 2], me.sibling()).wait_send()
+            remote(buf.at[xo], buf.at[xo], s_g.at[t, 2], r_g.at[t, 2], me.sibling()).wait_recv()
+
+        return from_sib, from_x, from_other
+
+    def scatter(t, i, where):
+        return remote(ps.at[t, i], pr.at[t, i], s_p.at[t, i], r_p.at[t, i], where)
+
+    def run(t, block, buf, beside_x):
+        from_sib, from_x, from_other = share(buf, t)
+        block(f, 3)
+        from_sib()
+        block(sib, 0)
+        scatter(t, 0, me.sibling()).start()
+        from_x()
+        block(xs, 2)
+        from_other()
+        block(xo, 1)
+        scatter(t, 1, me.sibling()).start()
+        scatter(t, 1, me.sibling()).wait()
+        ps[t, 2] = (ps[t, 2].astype(F32) + pr[t, 1].astype(F32)).astype(BF)
+        scatter(t, 2, me.beside()).start()
+        beside_x()
+        scatter(t, 0, me.sibling()).wait()
+        scatter(t, 2, me.beside()).wait()
+        return ps[t, 3].astype(F32) + pr[t, 0].astype(F32) + pr[t, 2].astype(F32)
+
+    def forward(index, into):
+        def up_tile(i, carry):
+            cols = tile_cols(i, 256)
+            pre = dense(nl[index], wu_ref[:, cols]) + par_ref[pl.ds(6, 1), cols]
+            cdf = 0.5 * (1.0 + lax.erf(pre * 0.7071067811865476))
+            hid[index, :, cols] = (pre * cdf).astype(BF)
+            slope[index, :, cols] = cdf + pre * jnp.exp(-0.5 * pre * pre) * 0.3989422804014327
+            return carry
+
+        def down_tile(i, carry):
+            cols = tile_cols(i, 512)
+            ps[0, into, :, cols] = dense(hid[index], wd_ref[:, cols]).astype(BF)
+            return carry
+
+        lax.fori_loop(0, 4, up_tile, 0)
+        lax.fori_loop(0, 2, down_tile, 0)
+
+    ffn = run(0, forward, nl, lambda: None)
+    value, x_hat, inv = norm_fwd(normed[...] + ffn + row(3), row(4), row(5))
+    moved_buf[...] = value.astype(BF)
+
+    @pl.when(me.stays())
+    def _():
+        pltpu.make_async_copy(moved_buf, layer_ref, loc.at[0]).start()
+
+    @pl.when(jnp.logical_not(me.stays()))
+    def _():
+        remote(moved_buf, layer_ref, s_m.at[0], r_m.at[0], me.moved()).start()
+
+    grad2, gain2, shift2 = norm_back(up_ref[...].astype(F32), x_hat, inv, row(4))
+    work[...] = grad2
+    low2 = grad2.astype(BF)
+    gff[f] = low2
+    vec_ref[pl.ds(4, 1), :] = jnp.sum(low2.astype(F32), axis=0, keepdims=True)
+    vec_ref[pl.ds(5, 1), :] = gain2[None]
+    vec_ref[pl.ds(6, 1), :] = shift2[None]
+
+    def backward(index, into):
+        def pre_tile(i, carry):
+            cols = tile_cols(i, 512)
+            part = dense_back(gff[index], wd_ref[cols, :])
+            gpre[index, :, cols] = (part * slope[index, :, cols]).astype(BF)
+            return carry
+
+        def in_tile(i, carry):
+            cols = tile_cols(i, 512)
+            ps[1, into, :, cols] = dense_back(gpre[index], wu_ref[cols, :]).astype(BF)
+            return carry
+
+        lax.fori_loop(0, 2, pre_tile, 0)
+        lax.fori_loop(0, 2, in_tile, 0)
+
+    def weight_grads():
+        def tile(i, carry):
+            cols = tile_cols(i, 256)
+            down_out[cols, :] = dense_in(hid[:, :, cols].reshape(1024, 256), gff[...].reshape(1024, 1024)).astype(BF)
+            upg_out[cols, :] = dense_in(nl[:, :, cols].reshape(1024, 256), gpre[...].reshape(1024, 1024)).astype(BF)
+            return carry
+
+        lax.fori_loop(0, 4, tile, 0)
+        vec_ref[pl.ds(3, 1), :] = jnp.sum(gpre[...].reshape(1024, 1024).astype(F32), axis=0, keepdims=True)
+
+    back = run(1, backward, gff, weight_grads)
+    grad1, gain1, shift1 = norm_back(back + work[...], xhat[...], rstd[...], row(1))
+    mid1_ref[...] = grad1
+    low1 = grad1.astype(BF)
+    gbr[...] = low1
+    vec_ref[pl.ds(0, 1), :] = jnp.sum(low1.astype(F32), axis=0, keepdims=True)
+    vec_ref[pl.ds(1, 1), :] = gain1[None]
+    vec_ref[pl.ds(2, 1), :] = shift1[None]
+    vec_ref[pl.ds(7, 1), :] = jnp.zeros((1, 1024), F32)
+
+    def att_tile(i, carry):
+        part = dense_back(gbr[...], wo_ref[tile_cols(i, 256), :]).astype(BF)
+        for j in range(2):
+            gas[2 * i + j] = part[:, j * PAIR : (j + 1) * PAIR].reshape(16, 16, PAIR)
+        return carry
+
+    lax.fori_loop(0, 4, att_tile, 0)
+    for k in range(1, 8):
+        _, theirs = peer_slot(k, 1)
+        remote(gas.at[theirs], gatt_ref.at[:, slot], s_b.at[k - 1], r_b.at[k - 1], peers[k - 1]).start()
+    gatt_ref[:, slot] = gas[unit]
+
+    def o_tile(i, carry):
+        cols = tile_cols(i, 256)
+        og_out[cols, :] = dense_in(att[:, :, cols].reshape(256, 256), gbr[...]).astype(BF)
+        return carry
+
+    lax.fori_loop(0, 4, o_tile, 0)
+    for k in range(1, 8):
+        where, _ = peer_slot(k, -1)
+        remote(gas.at[0], gatt_ref.at[:, where], s_b.at[k - 1], r_b.at[k - 1], peers[k - 1]).wait()
+
+    @pl.when(me.stays())
+    def _():
+        pltpu.make_async_copy(moved_buf, layer_ref, loc.at[0]).wait()
+
+    @pl.when(jnp.logical_not(me.stays()))
+    def _():
+        remote(moved_buf, layer_ref, s_m.at[0], r_m.at[0], me.moved()).wait()
+
+
+def middle(heads, x, upstream, w_output, w_up, w_down, params):
+    dma = pltpu.SemaphoreType.DMA
+    v = pltpu.VMEM
+    block = (4, 256, 1024)
+    scratch = [
+        v((16, 16, 1024), BF), v(block, BF), v(block, BF), v(block, F32), v(block, BF), v(block, BF),
+        v((256, 1024), F32), v((256, 1024), F32), v((256, 1), F32), v((256, 1024), F32), v((256, 1024), BF),
+        v((256, 1024), BF), v((8, 16, 16, PAIR), BF), v((2, 4, 256, 1024), BF), v((2, 3, 256, 1024), BF),
+        dma((7,)), dma((7,)), dma((7,)), dma((7,)), dma((2, 3)), dma((2, 3)), dma((2, 3)), dma((2, 3)),
+        dma((1,)), dma((1,)), dma((1,)),
+    ]
+    square = jax.ShapeDtypeStruct((1024, 1024), BF)
+    return pl.pallas_call(
+        middle_kernel,
+        out_shape=(
+            jax.ShapeDtypeStruct((256, 1024), BF), square, square, square,
+            jax.ShapeDtypeStruct((16, 8, 16, PAIR), BF),
+            jax.ShapeDtypeStruct((256, 1024), F32),
+            jax.ShapeDtypeStruct((8, 1024), F32),
+        ),
+        in_specs=[VMEM] * 7,
+        out_specs=(VMEM,) * 7,
+        scratch_shapes=scratch,
+        compiler_params=pltpu.CompilerParams(collective_id=2, has_side_effects=True, vmem_limit_bytes=60 * 2**20),
+        cost_estimate=pl.CostEstimate(flops=14 * 10**9, bytes_accessed=20 * 2**20, transcendentals=2**21),
+    )(heads.reshape(16, 8, 16, PAIR), x, upstream, w_output, w_up, w_down, params)
+
+
 def body(
     tokens, lengths, packing, query_w, query_b, key_w, value_w, value_b, output_w, output_b,
     attn_gain, attn_shift, expand_w, expand_b, reduce_w, reduce_b, ffn_gain, ffn_shift, cotangent,
@@ -636,22 +863,6 @@
         everyone = everyone.reshape(GROUP, laps, stripe, -1)
         return everyone.transpose(1, 0, 2, 3).reshape(GROUP * mine, -1)
 
-    def swap_group(block):
-        block = order(block.reshape(n_f, 2, mine, -1))
-        block = lax.all_to_all(block, "fsdp", 0, 0)
-        block = lax.all_to_all(block, "ctx", 1, 1, axis_index_groups=pairs)
-        return order(block).reshape(GROUP, mine, -1)
-
-    def to_tokens(block):
-        parts = block.reshape(laps, GROUP, stripe, PAIR).transpose(1, 0, 2, 3).reshape(GROUP, mine, PAIR)
-        got = swap_group(parts).reshape(n_f, 2, mine, PAIR)
-        return got.transpose(2, 1, 0, 3).reshape(mine, width)
-
-    def to_heads(block):
-        parts = block.reshape(mine, 2, n_f, PAIR).transpose(2, 1, 0, 3)
-        got = swap_group(parts).reshape(GROUP, laps, stripe, PAIR)
-        return got.transpose(1, 0, 2, 3).reshape(GROUP * mine, PAIR)
-
     def columns(w):
         return lax.all_to_all(w.reshape(w.shape[0], n_f, -1).transpose(1, 0, 2), "fsdp", 0, 0).reshape(
             n_f * w.shape[0], -1
@@ -691,7 +902,7 @@
     seg_k = seg_k[None, :]
 
     inputs = relocate(tokens.reshape(mine, width))
-    upstream = relocate(cotangent.reshape(mine, width)).astype(F32)
+    upstream = relocate(cotangent.reshape(mine, width))
     x_all = gather_group(inputs)
     w_three = jnp.stack([query_w, key_w, value_w]).reshape(3, -1, 2, n_f, PAIR)
     w_three = lax.dynamic_index_in_dim(w_three, b, 2, keepdims=False)
@@ -718,32 +929,19 @@
     att_heads, lse = attend(bounds, q, k, v, seg_q, seg_k, chunks)
 
     w_output = lax.all_gather(output_w, "fsdp", axis=0, tiled=True)
-    attended = to_tokens(att_heads)
-    branch = dense(attended, w_output) + output_b
-    normed, x_hat1, inv_std1 = norm_fwd(inputs.astype(F32) + branch, attn_gain, attn_shift)
-    normed_low = lax.all_gather(normed.astype(BF), "fsdp", axis=0, tiled=True)
-
     w_up = columns(expand_w)
     units = w_up.shape[1]
-    pre_act = dense(normed_low, w_up) + lax.dynamic_slice_in_dim(expand_b, f * units, units)
-    hidden = jax.nn.gelu(pre_act, approximate=False).astype(BF)
-    ffn_out = lax.psum_scatter(dense(hidden, reduce_w).astype(BF), "fsdp", tiled=True).astype(F32) + reduce_b
-    outputs, x_hat2, inv_std2 = norm_fwd(normed + ffn_out, ffn_gain, ffn_shift)
-    layer_out = relocate(outputs.astype(BF)).reshape(tok_shape)
-    grad_mid2, grad_ffn_gain, grad_ffn_shift = norm_back(upstream, x_hat2, inv_std2, ffn_gain)
-    grad_ffn_own = grad_mid2.astype(BF)
-    grad_reduce_b = jnp.sum(grad_ffn_own.astype(F32), axis=0)
-    grad_ffn = lax.all_gather(grad_ffn_own, "fsdp", axis=0, tiled=True)
-    part_down = dense_in(hidden, grad_ffn).astype(BF)
-    grad_pre = (dense_back(grad_ffn, reduce_w) * gelu_slope(pre_act)).astype(BF)
-    grad_expand_b = jnp.sum(grad_pre.astype(F32), axis=0)
-    part_up = dense_in(normed_low, grad_pre).astype(BF)
-    grad_normed = lax.psum_scatter(dense_back(grad_pre, w_up).astype(BF), "fsdp", tiled=True).astype(F32) + grad_mid2
-    grad_mid1, grad_attn_gain, grad_attn_shift = norm_back(grad_normed, x_hat1, inv_std1, attn_gain)
-    grad_branch = grad_mid1.astype(BF)
-    grad_output_b = jnp.sum(grad_branch.astype(F32), axis=0)
-    part_out = dense_in(attended, grad_branch).astype(BF)
-    grad_att = to_heads(dense_back(grad_branch, w_output).astype(BF))
+    params = jnp.stack(
+        [
+            output_b, attn_gain, attn_shift, reduce_b, ffn_gain, ffn_shift,
+            lax.dynamic_slice_in_dim(expand_b, f * units, units), jnp.zeros_like(output_b),
+        ]
+    )
+    layer_out, part_down, part_up, part_out, grad_att, grad_mid1, vec = middle(
+        att_heads, inputs, upstream, w_output, w_up, reduce_w, params
+    )
+    layer_out = layer_out.reshape(tok_shape)
+    grad_att = grad_att.reshape(GROUP * mine, PAIR)
 
     grad_q, grad_k, grad_v = attend_back(
         bounds, q, k, v, seg_q, seg_k, att_heads, lse, grad_att, chunks
@@ -762,10 +960,10 @@
     here_rows = jnp.zeros((n_f, units), F32)
     sums = jnp.concatenate(
         [
-            jnp.stack(
-                [grad_query_b, grad_value_b, grad_output_b, grad_attn_gain, grad_attn_shift, grad_reduce_b, grad_ffn_gain, grad_ffn_shift]
-            ),
-            lax.dynamic_update_slice_in_dim(here_rows, grad_expand_b[None], f, 0),
+            jnp.stack([grad_query_b, grad_value_b]),
+            vec[:3],
+            vec[4:7],
+            lax.dynamic_update_slice_in_dim(here_rows, vec[3:4], f, 0),
             here_rows,
         ]
     )

time: 656 us -> 529 us (0.81); the launches traced: 647 us -> 529 us
  waiting for transfers between devices: 165 us -> 54 us
  Pallas kernels: 269 us -> 377 us
  matrix products: 48.8 us -> 2.42 us
  local copies, waits for them, and re-layouts: 50.2 us -> 29.6 us
  starting transfers between devices: 31.1 us -> 11.4 us
  other arithmetic: 26.9 us -> 11.7 us
  blocking collectives: 37.6 us -> 24.5 us
    pallas_call x0 -> x1, Pallas kernels: none -> 106 us  [middle(): pl.pallas_call(middle_kernel, out_shape=(jax.ShapeDtypeStruct((256, 1024)...]
    reduce_scatter x2 -> x0, waiting for transfers between devices: 49.1 us -> none  [the longest x1 28 us: body(): lax.psum_scatter(dense(hidden, reduce_w).astype(BF), 'fsdp', tiled=True)]
    all_to_all x1, waiting for transfers between devices: 36.1 us -> 8.87 us  [columns(): lax.all_to_all(w.reshape(w.shape[0], n_f, -1).transpose(1, 0, 2), 'fsdp',...]
    dot_general x6 -> x0, matrix products: 25.9 us -> none  [the longest x3 15.1 us: dense_in(): lax.dot_general(left, right, (((0,), (0,)), ((), ())), preferred_element_...]
    all_gather x2 -> x0, waiting for transfers between devices: 24.9 us -> none  [the longest x1 24.9 us: body(): grad_ffn = lax.all_gather(grad_ffn_own, 'fsdp', axis=0, tiled=True)]
    all_to_all x2 -> x0, blocking collectives: 21.5 us -> none  [the longest x1 11.2 us: swap_group(): block = lax.all_to_all(block, 'fsdp', 0, 0)]
    dot_general x4 -> x1, matrix products: 22.9 us -> 2.42 us  [dense(): return jnp.dot(left, right, preferred_element_type=F32)]
    unnamed x83 -> x77, local copies, waits for them, and re-layouts: 23.6 us -> 10 us
  transfers between devices with their start and end apart: 14 -> 7, of which waited for: 8 -> 3; matrix products, arithmetic and copies ran while one was open for 8% -> 4% of each run, Pallas kernels for 3% -> 3%
where the time goes in v4:
time: 529 us
  Pallas kernels  377 us (71%)
  waiting for transfers between devices  54 us (10%)
  local copies, waits for them, and re-layouts  29.6 us (6%)
  blocking collectives  24.5 us (5%)
  between operations  17.7 us (3%)
  other arithmetic  11.7 us (2%)
  starting transfers between devices  11.4 us (2%)
    pallas_call x1, Pallas kernels, tail(): pl.pallas_call(tail_kernel, out_shape=(jax.ShapeDtypeStruct((1024, 1024),...  230 us
    pallas_call x1, Pallas kernels, middle(): pl.pallas_call(middle_kernel, out_shape=(jax.ShapeDtypeStruct((256, 1024)...  106 us
    all_gather x1, waiting for transfers between devices, gather_group(): both = lax.all_gather(block, 'ctx', axis_index_groups=pairs)  43.2 us
    unnamed x1, blocking collectives  24.5 us
    pallas_call x1, Pallas kernels, attend_back(): pl.pallas_call(functools.partial(attend_back_kernel, BQ, BK, chunks), out...  22.8 us
    pallas_call x1, Pallas kernels, attend(): pl.pallas_call(functools.partial(attend_kernel, BQ, BK, chunks), out_shap...  18.4 us
  transfers between devices with their start and end apart: 7, of which 3 were waited for; matrix products, arithmetic and copies ran while one was open for 4% of the time, Pallas kernels for 3%

profile of v4, /device:TPU:0, one launch (start us, length us, event | category | flops | bytes accessed | tf_op | source)
XLA Modules:
  0.0 528.5 jit_solution(13273293599644977221)
XLA Ops:
  7.3 1.8 collective-permute-start
  10.0 43.2 %all-gather.9.cloned.1.call-done = bf16[512,1024]{1,0:T(8,128)(2,1)} async-done(((bf16[256,1024]{1,0:T(8,128)(2,1)}), bf16[512,1024]{1,0:T(8,128)(2,1)}) %all-gather.9.cloned.1.call-update) | async-done | bytes 1048592 | tf_op jit(solution)/shard_map/all_gather | solution.py:861
  55.8 1.0 pad_maximum_fusion.1
  56.8 3.5 all-to-all-start
  62.1 1.5 collective-permute-start.1
  63.6 24.5 %all-reduce.1 = s32[4,3]{1,0:T(4,128)S(1)} all-reduce(s32[4,3]{1,0:T(4,128)S(1)} %reshape.300), channel_id=2, replica_groups=mesh['ctx'=8,'fsdp'=4] {'fsdp'}, use_global_device_ids=true, to_apply=%add | all-reduce | flops 12 | bytes 96
  94.5 3.2 copy.110
  99.1 4.5 all-to-all-start.1
  104.0 2.9 slice_bitcast_fusion.6
  107.5 0.8 copy.89
  108.3 2.4 add_convert_fusion
  111.1 18.4 %shard_map.323 = (bf16[2048,128]{1,0:T(8,128)(2,1)S(1)}, f32[4096,1]{1,0:T(8,128)S(1)}) custom-call(s32[8,1]{1,0:T(8,128)S(1)} %copy.99.lo_ref, s32[8,1]{1,0:T(8,128)S(1)} %copy.100.hi_ref, bf16[2048,128]{1,0:T(8,128)(2,1)S(1)} %get-tuple-element.64.q_ref, bf16[2048,128]{1,0:T(8,128)(2,1)S(1)} %get-tuple-element.63.k_ref, ...), custom_call_target="tpu_custom_call" | custom-call | tf_op jit(solution)/shard_map/pallas_call | solution.py:170
  129.6 1.3 copy-done.4
  130.9 0.8 copy-done.5
  131.7 8.9 %all-to-all-done.1 = bf16[4,256,1024]{2,1,0:T(8,128)(2,1)} async-done(((bf16[4,256,1024]{2,1,0:T(8,128)(2,1)}), bf16[4,256,1024]{2,1,0:T(8,128)(2,1)}, u32[]{:S(2)}, u32[]{:S(2)}) %all-to-all-start.1) | async-done | bytes 2097184 | tf_op jit(solution)/shard_map/all_to_all | solution.py:867
  140.6 1.2 all-gather.7.cloned.1.call-done.wo_ref
  141.8 105.6 %shard_map.324 = (bf16[256,1024]{1,0:T(8,128)(2,1)}, bf16[1024,1024]{1,0:T(8,128)(2,1)}, bf16[1024,1024]{1,0:T(8,128)(2,1)}, bf16[1024,1024]{1,0:T(8,128)(2,1)},...) custom-call(bf16[16,8,16,128]{3,2,1,0:T(8,128)(2,1)} %bitcast.87, ...), custom_call_target="tpu_custom_call" | custom-call | flops 14000000000 | bytes 20971520 | tf_op jit(solution)/shard_map/pallas_call | solution.py:812
  248.2 0.8 fusion.25
  249.1 22.8 %shard_map.325 = (bf16[2048,128]{1,0:T(8,128)(2,1)}, bf16[2048,128]{1,0:T(8,128)(2,1)}, bf16[2048,128]{1,0:T(8,128)(2,1)}) custom-call(s32[8,1]{1,0:T(8,128)} %copy-done.8, s32[8,1]{1,0:T(8,128)} %copy-done.7, bf16[2048,128]{1,0:T(8,128)(2,1)} %copy-done.3, bf16[2048,128]{1,0:T(8,128)(2,1)} %copy-done.2, bf16[2048,128]{1,0:T(8,128)(2,1)} %copy-done.1, ...), custom_call_target="tpu_custom_call" | custom-call | tf_op jit(solution)/shard_map/pallas_call | solution.py:182
  271.9 1.2 constant_dynamic-update-slice_fusion.2
  273.1 1.2 constant_dynamic-update-slice_fusion.1
  274.9 1.3 concatenate.12.vec_ref
  276.2 230.3 %shard_map.326 = (bf16[1024,1024]{1,0:T(8,128)(2,1)}, bf16[256,4096]{1,0:T(8,128)(2,1)}, bf16[256,1024]{1,0:T(8,128)(2,1)}, bf16[3,256,1024]{2,1,0:T(8,128)(2,1)...) custom-call(bf16[2048,1024]{1,0:T(8,128)(2,1)} %bitcast.92, bf16[2048,384]{1,0:T(8,128)(2,1)} %copy-done.10, ...), custom_call_target="tpu_custom_call" | custom-call | flops 4000000000 | bytes 41943040 | tf_op jit(solution)/shard_map/pallas_call | solution.py:583
  506.5 1.7 fusion.24
  508.9 1.8 convert_element_type.60
  510.7 1.7 slice_bitcast_fusion
  512.5 1.0 copy-done.12
  513.5 2.5 convert_element_type.62
  516.0 2.5 convert_element_type.63
  518.4 1.1 bitcast_convert_fusion
  519.5 1.1 convert_element_type.61
  521.2 0.8 copy.119
  (124 shorter events, 13.5 us)
Async XLA Ops:
  7.2 46.8 %copy-start.16 = (bf16[256,1024]{1,0:T(8,128)(2,1)S(1)}, bf16[256,1024]{1,0:T(8,128)(2,1)}, u32[]{:S(2)}) copy-start(bf16[256,1024]{1,0:T(8,128)(2,1)} %param.23) | copy-start | bytes 1572868
  7.2 47.0 %copy-start.17 = (bf16[256,1024]{1,0:T(8,128)(2,1)S(1)}, bf16[256,1024]{1,0:T(8,128)(2,1)}, u32[]{:S(2)}) copy-start(bf16[256,1024]{1,0:T(8,128)(2,1)} %param.25) | copy-start | bytes 1572868
  7.2 46.0 %all-gather.9.cloned.1.call-start = ((), (), s32[]{:S(2)}) async-start(), calls=%async_computation.3 | async-start | bytes 1572864 | tf_op jit(solution)/shard_map/all_gather | solution.py:861
  7.3 1.8 collective-permute-start
  9.1 45.3 %copy-start.18 = (bf16[256,1024]{1,0:T(8,128)(2,1)S(1)}, bf16[256,1024]{1,0:T(8,128)(2,1)}, u32[]{:S(2)}) copy-start(bf16[256,1024]{1,0:T(8,128)(2,1)} %param.26) | copy-start | bytes 1572868
  9.9 94.1 %all-gather.11.cloned.1.call-start = ((), (), s32[]{:S(2)}) async-start(), calls=%async_computation.4 | async-start | bytes 5242880 | tf_op jit(solution)/shard_map/all_gather | solution.py:862
  53.2 88.6 %all-gather.7.cloned.1.call-start = ((), (), s32[]{:S(2)}) async-start(), calls=%async_computation.2 | async-start | bytes 2621440 | tf_op jit(solution)/shard_map/all_gather | solution.py:931
  55.3 5.0 copy-start.32
  55.3 6.2 %copy-start.30 = (s32[1,3]{1,0:T(1,128)S(1)}, s32[1,3]{1,0:T(1,128)}, u32[]{:S(2)}) copy-start(s32[1,3]{1,0:T(1,128)} %param.21) | copy-start | bytes 40
  55.3 6.2 %copy-start.31 = (s32[1,3]{1,0:T(1,128)S(1)}, s32[1,3]{1,0:T(1,128)}, u32[]{:S(2)}) copy-start(s32[1,3]{1,0:T(1,128)} %param.22) | copy-start | bytes 40
  55.4 6.7 %copy-start.29 = (bf16[1,16,16,1024]{3,2,1,0:T(8,128)(2,1)S(1)}, bf16[1,16,16,1024]{3,2,1,0:T(8,128)(2,1)}, u32[]{:S(2)}) copy-start(bf16[1,16,16,1024]{3,2,1,0:T(8,128)(2,1)} %param.38) | copy-start | bytes 1572868
  55.5 32.6 %copy-start.28 = (s32[4]{0:T(128)S(1)}, s32[4]{0:T(128)}, u32[]{:S(2)}) copy-start(s32[4]{0:T(128)} %constant.142.clone) | copy-start | bytes 52
  56.8 42.3 %all-to-all-start = ((bf16[4,256,384]{1,2,0:T(8,128)(2,1)}), bf16[4,256,384]{1,2,0:T(8,128)(2,1)S(1)}, u32[]{:S(2)}, u32[]{:S(2)}) async-start(bf16[4,256,384]{1,2,0:T(8,128)(2,1)} %pad_maximum_fusion.1), calls=%async_computation | async-start | bytes 1572864 | tf_op jit(solution)/shard_map/all_to_all | solution.py:910
  62.1 69.6 %collective-permute-start.1 = (bf16[256,1024]{1,0:T(8,128)(2,1)S(1)}, bf16[256,1024]{1,0:T(8,128)(2,1)}, u32[]{:S(2)}, u32[]{:S(2)}) collective-permute-start(bf16[256,1024]{1,0:T(8,128)(2,1)S(1)} %bitcast.127), channel_id=1, source_target_pairs={{0,0},{1,16},{2,8},{3,24},{4,4},{5,20},{6,12},{7,28},{8,2},{9,18},... | collective-permute-start | bytes 1572872 | tf_op jit(solution)/shard_map/ppermute | solution.py:855
  90.9 20.1 %copy-start.6 = (s32[2048]{0:T(1024)}, s32[2048]{0:T(1024)S(1)}, u32[]{:S(2)}) copy-start(s32[2048]{0:T(1024)S(1)} %get-tuple-element.54) | copy-start | bytes 24580
  93.9 17.2 %copy-start = (s32[2048,1]{1,0:T(8,128)}, s32[2048,1]{1,0:T(8,128)S(1)}, u32[]{:S(2)}) copy-start(s32[2048,1]{1,0:T(8,128)S(1)} %copy.101.sq_ref) | copy-start | bytes 24580
  94.2 16.9 %copy-start.7 = (s32[8,1]{1,0:T(8,128)}, s32[8,1]{1,0:T(8,128)S(1)}, u32[]{:S(2)}) copy-start(s32[8,1]{1,0:T(8,128)S(1)} %copy.100.hi_ref) | copy-start | bytes 100
  94.4 16.7 %copy-start.8 = (s32[8,1]{1,0:T(8,128)}, s32[8,1]{1,0:T(8,128)S(1)}, u32[]{:S(2)}) copy-start(s32[8,1]{1,0:T(8,128)S(1)} %copy.99.lo_ref) | copy-start | bytes 100
  94.4 4.0 copy-start.22
  94.4 4.0 copy-start.23
  94.4 4.0 copy-start.24
  94.4 4.0 copy-start.25
  94.5 4.0 copy-start.26
  94.5 4.0 copy-start.27
  99.1 41.5 %all-to-all-start.1 = ((bf16[4,256,1024]{2,1,0:T(8,128)(2,1)}), bf16[4,256,1024]{2,1,0:T(8,128)(2,1)}, u32[]{:S(2)}, u32[]{:S(2)}) async-start(bf16[4,256,1024]{2,1,0:T(8,128)(2,1)} %bitcast.85), calls=%async_computation.1 | async-start | bytes 4194304 | tf_op jit(solution)/shard_map/all_to_all | solution.py:867
  104.0 4.4 copy-start.13
  111.1 136.4 %copy-start.1 = (bf16[2048,128]{1,0:T(8,128)(2,1)}, bf16[2048,128]{1,0:T(8,128)(2,1)S(1)}, u32[]{:S(2)}) copy-start(bf16[2048,128]{1,0:T(8,128)(2,1)S(1)} %get-tuple-element.62.v_ref) | copy-start | bytes 1572868
  111.1 136.4 %copy-start.2 = (bf16[2048,128]{1,0:T(8,128)(2,1)}, bf16[2048,128]{1,0:T(8,128)(2,1)S(1)}, u32[]{:S(2)}) copy-start(bf16[2048,128]{1,0:T(8,128)(2,1)S(1)} %get-tuple-element.63.k_ref) | copy-start | bytes 1572868
  111.1 136.4 %copy-start.3 = (bf16[2048,128]{1,0:T(8,128)(2,1)}, bf16[2048,128]{1,0:T(8,128)(2,1)S(1)}, u32[]{:S(2)}) copy-start(bf16[2048,128]{1,0:T(8,128)(2,1)S(1)} %get-tuple-element.64.q_ref) | copy-start | bytes 1572868
  510.7 2.7 copy-start.12
  516.0 3.6 copy-start.14
  518.4 2.8 copy-start.20
  (8 other events, 14.5 us)
Sparse Core Ops, SparseCore 0:
  10.2 42.9 all-gather.8
  54.7 48.9 all-gather.10
  105.3 36.4 all-gather.6

commit v5 on v4

--- a/solution.py
+++ b/solution.py
@@ -261,15 +261,73 @@
     pl.semaphore_wait(barrier, len(targets) + jnp.where(me.stays(), 0, 1))
 
 
+class Flow:
+    def __init__(self, me, own, buf, got, sent, came):
+        self.me, self.own, self.buf, self.got, self.sent, self.came = me, own, buf, got, sent, came
+        self.low = me.g < 2
+        self.inner = jnp.where((me.g == 1) | (me.g == 2), 1, 0)
+        step = jnp.where(self.low, 1, -1)
+        self.ahead = me.at(g=me.g + step)
+        self.back_to = me.at(g=me.g - step)
+
+    def piece(self, i):
+        return jnp.where(self.low, 3 - i, i)
+
+    def copy(self, p, side, where):
+        return remote(self.buf.at[p], self.got.at[side, p], self.sent.at[p], self.came.at[side, p], where)
+
+    def forward(self, i):
+        p = self.piece(i)
+
+        @pl.when(self.inner == 0)
+        def _():
+            self.buf[p] = self.own(p).astype(BF)
+            self.copy(p, 0, self.ahead).start()
+
+        if i < 2:
+            @pl.when(self.inner == 1)
+            def _():
+                self.copy(p, 0, self.back_to).wait_recv()
+                self.buf[p] = (self.own(p) + self.got[0, p].astype(F32)).astype(BF)
+                self.copy(p, 1, self.ahead).start()
+
+    def back(self):
+        p = self.piece(3)
+
+        @pl.when(self.inner == 1)
+        def _():
+            self.copy(p, 1, self.ahead).wait_recv()
+            self.buf[p] = (self.own(p) + self.got[1, p].astype(F32)).astype(BF)
+            self.copy(p, 1, self.back_to).start()
+
+    def end(self):
+        g = self.me.g
+
+        @pl.when(self.inner == 0)
+        def _():
+            self.copy(g, 1, self.ahead).wait_recv()
+            self.buf[g] = (self.own(g) + self.got[1, g].astype(F32)).astype(BF)
+
+        @pl.when(self.inner == 1)
+        def _():
+            self.copy(g, 0, self.back_to).wait_recv()
+            self.copy(g, 1, self.ahead).wait_recv()
+            self.buf[g] = (self.own(g) + self.got[0, g].astype(F32) + self.got[1, g].astype(F32)).astype(BF)
+
+        for p in range(4):
+            @pl.when(g != p)
+            def _():
+                self.copy(p, 0, self.ahead).wait_send()
+
+
 def tail_kernel(
     x_ref, g3_ref, w3_ref, down_ref, up_ref, out_ref, mid_ref, vec_ref,
     down_out, up_out, o_out, three_out, dx_ref, sums_ref,
     dxp, dx1, t1, xa, yb, t2a, t2b, ra, rb, moved_buf,
-    yr_down, yr_up, zl, zr, zs, up_send, up_got,
-    o_got, o_sum, yr_o, ol, orr, os_,
-    gq, ql, qr, qs, q_send,
-    vs, vr,
-    s_dx, r_dx, s_y, r_y, s_z, r_zl, r_zr, s_u, r_u, s_o, r_o, s_oz, r_ol, r_or, s_q, r_ql, r_qr,
+    yr_down, yr_up, dbuf, dgot, ubuf, ugot,
+    o_got, o_sum, yr_o, obuf, ogot,
+    gq, qbuf, qgot, vs, vr,
+    s_dx, r_dx, s_y, r_y, s_d, r_d, s_z, r_z, s_u, r_u, s_o, r_o, s_oz, r_oz, s_q, r_q,
     s_qf, r_qf, s_v, r_v, s_ag, r_ag, s_ay, r_ay, loc,
 ):
     me = Place()
@@ -277,44 +335,54 @@
     z_others = [me.at(g=(g + k) % 4) for k in (1, 2, 3)]
     meet(me, [me.across()] + [me.fsdp(k) for k in (1, 2, 3)] + z_others, True)
 
-    y_copies = {}
-    for p in (3, 0, 2, 1):
-        y_copies[p] = (
-            remote(down_ref.at[1 - b, p], yr_down.at[p], s_y.at[0, p], r_y.at[0, p], me.across()),
-            remote(up_ref.at[:, 1 - b, p], yr_up.at[p], s_y.at[1, p], r_y.at[1, p], me.across()),
+    def own_down(p):
+        return down_ref[b, p].astype(F32) + yr_down[p].astype(F32)
+
+    def own_up(p):
+        return up_ref[:, b, p].astype(F32) + yr_up[p].astype(F32)
+
+    def own_q(p):
+        return gq[:, :, p].astype(F32)
+
+    def own_o(p):
+        return o_sum[b, p].astype(F32) + yr_o[p].astype(F32)
+
+    flow_d = Flow(me, own_down, dbuf, dgot, s_d, r_d)
+    flow_u = Flow(me, own_up, ubuf, ugot, s_z, r_z)
+    flow_q = Flow(me, own_q, qbuf, qgot, s_q, r_q)
+    flow_o = Flow(me, own_o, obuf, ogot, s_oz, r_oz)
+
+    y_copies = []
+    for i in range(4):
+        p = flow_d.piece(i)
+        pair = (
+            remote(down_ref.at[1 - b, p], yr_down.at[p], s_y.at[0, i], r_y.at[0, i], me.across()),
+            remote(up_ref.at[:, 1 - b, p], yr_up.at[p], s_y.at[1, i], r_y.at[1, i], me.across()),
         )
-        for c in y_copies[p]:
+        for c in pair:
             c.start()
+        y_copies.append(pair)
+
+    hops = [me.sibling(), me.beside(), me.across(), me.at(g=g + 1 - 2 * (g % 2)), me.at(g=(g + 2) % 4)]
+    vec = vec_ref[...]
+
+    def hop(i, vec):
+        vs[i] = vec
+        c = remote(vs.at[i], vr.at[i], s_v.at[i], r_v.at[i], hops[i])
+        c.start()
+        return c
+
+    v_copies = [hop(0, vec)]
+
+    def hop_end(i, vec):
+        v_copies[i].wait()
+        return vec + vr[i]
+
     o_copies = []
     for k in (1, 2, 3):
         c = remote(out_ref.at[(f + k) % 4], o_got.at[k - 1], s_o.at[k - 1], r_o.at[k - 1], me.fsdp(k))
         c.start()
         o_copies.append(c)
-
-    def dx_step(i, carry):
-        rows = pl.ds(pl.multiple_of(i * 256, 256), 256)
-        part = dense_back(g3_ref[rows, :], w3_ref[...]).astype(BF)
-        dxp[pl.ds(2 * i, 2)] = part.reshape(2, 2, 2, 2, 16, 1024)
-        return carry
-
-    lax.fori_loop(0, 8, dx_step, 0)
-    c_core = remote(dxp.at[:, 1 - me.core], dx1, s_dx.at[0], r_dx.at[0], me.sibling())
-    c_core.start()
-
-    hops = [me.sibling(), me.beside(), me.across(), me.at(g=g + 1 - 2 * (g % 2)), me.at(g=(g + 2) % 4)]
-    vec = vec_ref[...]
-
-    def hop(i, vec):
-        vs[i] = vec
-        c = remote(vs.at[i], vr.at[i], s_v.at[i], r_v.at[i], hops[i])
-        c.start()
-        return c
-
-    v_copies = [hop(0, vec)]
-
-    def hop_end(i, vec):
-        v_copies[i].wait()
-        return vec + vr[i]
 
     def q_step(i, carry):
         cols = pl.ds(pl.multiple_of(i * 256, 256), 256)
@@ -324,9 +392,35 @@
         return carry
 
     lax.fori_loop(0, 4, q_step, 0)
-
     vec = hop_end(0, vec)
     v_copies.append(hop(1, vec))
+    for i in range(3):
+        @pl.when(flow_q.inner == 0)
+        def _():
+            flow_q.forward(i)
+
+    def dx_step(i, carry):
+        rows = pl.ds(pl.multiple_of(i * 256, 256), 256)
+        part = dense_back(g3_ref[rows, :], w3_ref[...]).astype(BF)
+        dxp[pl.ds(2 * i, 2)] = part.reshape(2, 2, 2, 2, 16, 1024)
+        return carry
+
+    lax.fori_loop(0, 8, dx_step, 0)
+    c_core = remote(dxp.at[:, 1 - me.core], dx1, s_dx.at[0], r_dx.at[0], me.sibling())
+    c_core.start()
+    vec = hop_end(1, vec)
+    v_copies.append(hop(2, vec))
+
+    @pl.when(flow_q.inner == 1)
+    def _():
+        flow_q.forward(0)
+        flow_q.forward(1)
+
+    def large(i):
+        for c in y_copies[i]:
+            c.wait()
+        flow_d.forward(i)
+        flow_u.forward(i)
 
     c_core.wait()
 
@@ -341,60 +435,9 @@
     c_xa.start()
     c_yb.start()
 
-    vec = hop_end(1, vec)
-    v_copies.append(hop(2, vec))
-
-    def flow(p, own, left, right, send, s_sem, l_sem, r_sem):
-        @pl.when(g < p)
-        def _():
-            @pl.when(g > 0)
-            def _():
-                remote(send.at[p], left.at[p], s_sem.at[p], l_sem.at[p], me.across()).wait_recv()
-                send[p] = (own(p) + left[p].astype(F32)).astype(BF)
-
-            @pl.when(g == 0)
-            def _():
-                send[p] = own(p).astype(BF)
-
-            remote(send.at[p], left.at[p], s_sem.at[p], l_sem.at[p], me.at(g=g + 1)).start()
-
-        @pl.when(g > p)
-        def _():
-            @pl.when(g < 3)
-            def _():
-                remote(send.at[p], right.at[p], s_sem.at[p], r_sem.at[p], me.across()).wait_recv()
-                send[p] = (own(p) + right[p].astype(F32)).astype(BF)
-
-            @pl.when(g == 3)
-            def _():
-                send[p] = own(p).astype(BF)
-
-            remote(send.at[p], right.at[p], s_sem.at[p], r_sem.at[p], me.at(g=g - 1)).start()
-
-    def flow_end(own, left, right, send, s_sem, l_sem, r_sem):
-        send[g] = own(g).astype(BF)
-
-        @pl.when(g > 0)
-        def _():
-            remote(send.at[g], left.at[g], s_sem.at[g], l_sem.at[g], me.across()).wait_recv()
-            send[g] = (send[g].astype(F32) + left[g].astype(F32)).astype(BF)
-
-        @pl.when(g < 3)
-        def _():
-            remote(send.at[g], right.at[g], s_sem.at[g], r_sem.at[g], me.across()).wait_recv()
-            send[g] = (send[g].astype(F32) + right[g].astype(F32)).astype(BF)
-
-        for p in range(4):
-            @pl.when(g != p)
-            def _():
-                remote(send.at[p], left.at[p], s_sem.at[p], l_sem.at[p], me.across()).wait_send()
-
-    def own_q(p):
-        return gq[:, :, p].astype(F32)
-
-    q_bufs = (ql, qr, qs, s_q, r_ql, r_qr)
-    for p in (3, 0, 2, 1):
-        flow(p, own_q, *q_bufs)
+    large(0)
+    flow_q.back()
+    large(1)
 
     for c in o_copies:
         c.wait()
@@ -404,59 +447,25 @@
     c_oy = remote(o_sum.at[1 - b], yr_o, s_y.at[0, 4], r_y.at[0, 4], me.across())
     c_oy.start()
 
-    vec = hop_end(2, vec)
-    v_copies.append(hop(3, vec))
-
-    def own_big(p):
-        return jnp.concatenate(
-            [
-                down_ref[b, p].astype(F32) + yr_down[p].astype(F32),
-                (up_ref[:, b, p].astype(F32) + yr_up[p].astype(F32)).reshape(128, 1024),
-            ],
-            axis=0,
-        )
-
-    big_bufs = (zl, zr, zs, s_z, r_zl, r_zr)
-    for p in (3, 0, 2, 1):
-        for c in y_copies[p]:
-            c.wait()
-        flow(p, own_big, *big_bufs)
-
+    large(2)
     c_xa.wait()
     t2a[...] = (t1[lo, me.x].astype(F32) + xa[...].astype(F32)).astype(BF)
     c_ra = remote(t2a.at[:, 1 - b], ra, s_dx.at[3], r_dx.at[3], me.across())
     c_ra.start()
+    for c in y_copies[3]:
+        c.wait()
+    flow_d.back()
+    flow_u.back()
+    vec = hop_end(2, vec)
+    v_copies.append(hop(3, vec))
+    c_oy.wait()
+    for i in range(3):
+        flow_o.forward(i)
     c_yb.wait()
     t2b[...] = (t1[hi, :, b].astype(F32) + yb[...].astype(F32)).astype(BF)
     c_rb = remote(t2b.at[:, 1 - me.x], rb, s_dx.at[4], r_dx.at[4], me.beside())
     c_rb.start()
-
-    vec = hop_end(3, vec)
-    v_copies.append(hop(4, vec))
-
-    c_oy.wait()
-
-    def own_o(p):
-        return o_sum[b, p].astype(F32) + yr_o[p].astype(F32)
-
-    o_bufs = (ol, orr, os_, s_oz, r_ol, r_or)
-    for p in (3, 0, 2, 1):
-        flow(p, own_o, *o_bufs)
-
-    c_ra.wait()
-    c_rb.wait()
-    moved_buf[lo] = (t2a[:, b].astype(F32) + ra[...].astype(F32) + mid_ref[lo]).astype(BF)
-    moved_buf[hi] = (t2b[:, me.x].astype(F32) + rb[...].astype(F32) + mid_ref[hi]).astype(BF)
-
-    @pl.when(me.stays())
-    def _():
-        c = pltpu.make_async_copy(moved_buf, dx_ref, loc.at[0])
-        c.start()
-        c.wait()
-
-    @pl.when(jnp.logical_not(me.stays()))
-    def _():
-        remote(moved_buf, dx_ref, s_dx.at[5], r_dx.at[5], me.moved()).start()
+    flow_o.back()
 
     def rows(size, q, other=False):
         half = 1 - b if other else b
@@ -471,31 +480,30 @@
     def q_rows(q):
         return pl.ds(pl.multiple_of(q * 64, 64), 64)
 
-    flow_end(own_q, *q_bufs)
-    q_send[...] = qs[g]
-    three_out[:, q_rows(g), head_cols(f)] = q_send[f]
+    flow_q.end()
+    three_out[:, q_rows(g), head_cols(f)] = qbuf[g, f]
     q_out = []
     for k in (1, 2, 3):
-        c = remote(q_send.at[(f + k) % 4], three_out.at[:, q_rows(g), head_cols(f)], s_qf.at[k - 1], r_qf.at[f], me.fsdp(k))
+        c = remote(qbuf.at[g, (f + k) % 4], three_out.at[:, q_rows(g), head_cols(f)], s_qf.at[k - 1], r_qf.at[f], me.fsdp(k))
         c.start()
         q_out.append(c)
 
-    flow_end(own_big, *big_bufs)
-    up_send[...] = zs[g, pl.ds(128, 128)].reshape(4, 32, 1024)
-    down_out[rows(128, g), :] = zs[g, pl.ds(0, 128)]
-    up_out[rows(32, g), unit_cols(f)] = up_send[f]
+    flow_u.end()
+    up_out[rows(32, g), unit_cols(f)] = ubuf[g, f]
     u_out = []
     for k in (1, 2, 3):
-        c = remote(up_send.at[(f + k) % 4], up_out.at[rows(32, g), unit_cols(f)], s_u.at[k - 1], r_u.at[f], me.fsdp(k))
+        c = remote(ubuf.at[g, (f + k) % 4], up_out.at[rows(32, g), unit_cols(f)], s_u.at[k - 1], r_u.at[f], me.fsdp(k))
         c.start()
         u_out.append(c)
-    flow_end(own_o, *o_bufs)
-    o_out[rows(32, g), :] = os_[g]
+    flow_d.end()
+    down_out[rows(128, g), :] = dbuf[g]
+    flow_o.end()
+    o_out[rows(32, g), :] = obuf[g]
 
     for k in (1, 2, 3):
         src = (f + k) % 4
-        remote(q_send.at[0], three_out.at[:, q_rows(g), head_cols(src)], s_qf.at[k - 1], r_qf.at[src], me.fsdp(k)).wait_recv()
-        remote(up_send.at[0], up_out.at[rows(32, g), unit_cols(src)], s_u.at[k - 1], r_u.at[src], me.fsdp(k)).wait_recv()
+        remote(qbuf.at[g, 0], three_out.at[:, q_rows(g), head_cols(src)], s_qf.at[k - 1], r_qf.at[src], me.fsdp(k)).wait_recv()
+        remote(ubuf.at[g, 0], up_out.at[rows(32, g), unit_cols(src)], s_u.at[k - 1], r_u.at[src], me.fsdp(k)).wait_recv()
         q_out[k - 1].wait_send()
         u_out[k - 1].wait_send()
 
@@ -524,6 +532,23 @@
                     c.start()
 
     spread(g, True, True)
+    c_ra.wait()
+    c_rb.wait()
+    moved_buf[lo] = (t2a[:, b].astype(F32) + ra[...].astype(F32) + mid_ref[lo]).astype(BF)
+    moved_buf[hi] = (t2b[:, me.x].astype(F32) + rb[...].astype(F32) + mid_ref[hi]).astype(BF)
+
+    @pl.when(me.stays())
+    def _():
+        c = pltpu.make_async_copy(moved_buf, dx_ref, loc.at[0])
+        c.start()
+        c.wait()
+
+    @pl.when(jnp.logical_not(me.stays()))
+    def _():
+        remote(moved_buf, dx_ref, s_dx.at[5], r_dx.at[5], me.moved()).start()
+
+    vec = hop_end(3, vec)
+    v_copies.append(hop(4, vec))
     for d in (1, 2, 3):
         @pl.when(g >= d)
         def _():
@@ -569,15 +594,14 @@
         v((16, 2, 2, 2, 16, 1024), BF), v((16, 2, 2, 16, 1024), BF), v((16, 2, 2, 16, 1024), BF),
         v((8, 2, 16, 1024), BF), v((8, 2, 16, 1024), BF), v((8, 2, 16, 1024), BF), v((8, 2, 16, 1024), BF),
         v((8, 16, 1024), BF), v((8, 16, 1024), BF), v((16, 16, 1024), BF),
-        v((4, 128, 1024), BF), v((4, 4, 32, 1024), BF), v((4, 256, 1024), BF), v((4, 256, 1024), BF),
-        v((4, 256, 1024), BF), v((4, 32, 1024), BF), v((4, 32, 1024), BF),
+        v((4, 128, 1024), BF), v((4, 4, 32, 1024), BF), v((4, 128, 1024), BF), v((2, 4, 128, 1024), BF),
+        v((4, 4, 32, 1024), BF), v((2, 4, 4, 32, 1024), BF),
         v((3, 2, 4, 32, 1024), BF), v((2, 4, 32, 1024), BF), v((4, 32, 1024), BF),
-        v((4, 32, 1024), BF), v((4, 32, 1024), BF), v((4, 32, 1024), BF),
-        v((4, 3, 4, 64, 128), BF), v((4, 4, 3, 64, 128), BF), v((4, 4, 3, 64, 128), BF), v((4, 4, 3, 64, 128), BF),
-        v((4, 3, 64, 128), BF),
+        v((4, 32, 1024), BF), v((2, 4, 32, 1024), BF),
+        v((4, 3, 4, 64, 128), BF), v((4, 4, 3, 64, 128), BF), v((2, 4, 4, 3, 64, 128), BF),
         v((5, 16, 1024), F32), v((5, 16, 1024), F32),
-        dma((6,)), dma((6,)), dma((2, 5)), dma((2, 5)), dma((4,)), dma((4,)), dma((4,)),
-        dma((3,)), dma((4,)), dma((3,)), dma((3,)), dma((4,)), dma((4,)), dma((4,)), dma((4,)), dma((4,)), dma((4,)),
+        dma((6,)), dma((6,)), dma((2, 5)), dma((2, 5)), dma((4,)), dma((2, 4)), dma((4,)), dma((2, 4)),
+        dma((3,)), dma((4,)), dma((3,)), dma((3,)), dma((4,)), dma((2, 4)), dma((4,)), dma((2, 4)),
         dma((3,)), dma((4,)), dma((5,)), dma((5,)), dma((2, 4, 4)), dma((4, 4)), dma((4, 4)), dma((4, 4)), dma((1,)),
     ]
     return pl.pallas_call(
@@ -825,6 +849,201 @@
     )(heads.reshape(16, 8, 16, PAIR), x, upstream, w_output, w_up, w_down, params)
 
 
+def start_kernel(
+    tok_ref, cot_ref, ends_ref, qw_ref, kw_ref, vw_ref, ow_ref, ew_ref, bias_ref,
+    x_ref, up_ref, ends_out, q_ref, k_ref, v_ref, w3_ref, wo_ref, wu_ref,
+    s_m, r_m, s_w, r_w, s_u, r_u, s_o, r_o, s_x, r_x, loc,
+):
+    me = Place()
+    g, b, f = me.g, me.b, me.f
+    sib = f + 1 - 2 * me.core
+    xs = (f + 2) % 4
+    xo = xs + 1 - 2 * me.core
+    meet(me, [me.across()] + [me.fsdp(k) for k in (1, 2, 3)], True)
+    slot = me.core * 4 + me.x * 2 + b
+    slot_x = me.core * 4 + (1 - me.x) * 2 + b
+    slot_y = slot + 1 - 2 * b
+    slot_d = slot_x + 1 - 2 * b
+    other = 4 - 8 * me.core
+    lo, hi = pl.ds(0, 8), pl.ds(8, 8)
+
+    def moves(i, src, dst):
+        return remote(src, dst, s_m.at[i], r_m.at[i], me.moved())
+
+    def relocate(i, src, dst):
+        @pl.when(me.stays())
+        def _():
+            pltpu.make_async_copy(src, dst, loc.at[i]).start()
+
+        @pl.when(jnp.logical_not(me.stays()))
+        def _():
+            moves(i, src, dst).start()
+
+    def relocated(i, src, dst):
+        @pl.when(me.stays())
+        def _():
+            pltpu.make_async_copy(src, dst, loc.at[i]).wait()
+
+        @pl.when(jnp.logical_not(me.stays()))
+        def _():
+            moves(i, src, dst).wait()
+
+    theirs = x_ref.at[:, g * 2 + b]
+    relocate(0, tok_ref, theirs)
+    relocate(1, ends_ref, ends_out)
+
+    def cols(index, size):
+        return pl.ds(pl.multiple_of(index * size, size), size)
+
+    def w3_rows(src):
+        return cols(src, 256)
+
+    weights = (qw_ref, kw_ref, vw_ref)
+    for k in (2, 3, 1):
+        dest = b * 4 + swapped((f + k) % 4)
+        for j in range(3):
+            remote(
+                weights[j].at[:, cols(dest, 128)], w3_ref.at[w3_rows(f), pl.ds(128 * j, 128)],
+                s_w.at[j, k - 1], r_w.at[j, k - 1], me.fsdp(k),
+            ).start()
+    for j in range(3):
+        pltpu.make_async_copy(
+            weights[j].at[:, cols(b * 4 + swapped(f), 128)], w3_ref.at[w3_rows(f), pl.ds(128 * j, 128)], loc.at[2 + j]
+        ).start()
+
+    half = cols(b, 128)
+
+    def wo_rows(src, which):
+        return pl.ds(pl.multiple_of(src * 256 + which * 128, 128), 128)
+
+    o_own = pltpu.make_async_copy(ow_ref, wo_ref.at[w3_rows(f)], loc.at[5])
+    o_own.start()
+    o_sib = remote(ow_ref, wo_ref.at[w3_rows(f)], s_o.at[0], r_o.at[0], me.sibling())
+    o_x = remote(ow_ref.at[half], wo_ref.at[wo_rows(f, b)], s_o.at[1], r_o.at[1], me.beside())
+    o_x.start()
+    o_sib.start()
+
+    u_own = pltpu.make_async_copy(ew_ref.at[:, cols(f, 1024)], wu_ref.at[w3_rows(f)], loc.at[6])
+    u_own.start()
+    u_sib = remote(ew_ref.at[:, cols(sib, 1024)], wu_ref.at[w3_rows(f)], s_u.at[0], r_u.at[0], me.sibling())
+    u_sib.start()
+    u_x = [
+        remote(ew_ref.at[half, cols(xs, 1024)], wu_ref.at[wo_rows(f, b)], s_u.at[1], r_u.at[1], me.beside()),
+        remote(ew_ref.at[half, cols(xo, 1024)], wu_ref.at[wo_rows(f, b)], s_u.at[2], r_u.at[2], me.at(f=xo)),
+    ]
+
+    def piece(i, ref, where):
+        return remote(ref, ref, s_x.at[i], r_x.at[i], where)
+
+    relocated(0, tok_ref, theirs)
+    relocate(7, cot_ref, up_ref)
+    own = x_ref.at[:, slot]
+    sends = [piece(1, own, me.beside()), piece(2, own, me.across()), piece(0, own, me.sibling())]
+    for c in sends:
+        c.start()
+    piece(1, x_ref.at[:, slot_x], me.beside()).wait_recv()
+    more = [piece(4, x_ref.at[hi, slot_x], me.across()), piece(3, x_ref.at[:, slot_x], me.sibling())]
+    for c in more:
+        c.start()
+    sends += more
+    piece(2, x_ref.at[:, slot_y], me.across()).wait_recv()
+    more = [piece(6, x_ref.at[lo, slot_y], me.beside()), piece(5, x_ref.at[:, slot_y], me.sibling())]
+    for c in more:
+        c.start()
+    sends += more
+    for c in u_x:
+        c.start()
+    o_x.wait()
+    o_fwd = [
+        remote(wo_ref.at[wo_rows(xs, b)], wo_ref.at[wo_rows(xs, b)], s_o.at[2], r_o.at[2], me.sibling()),
+        remote(wo_ref.at[wo_rows(xs, b)], wo_ref.at[wo_rows(xs, b)], s_o.at[3], r_o.at[3], me.across()),
+    ]
+    for c in o_fwd:
+        c.start()
+    piece(4, x_ref.at[hi, slot_d], me.across()).wait_recv()
+    more = [piece(8, x_ref.at[hi, slot_d], me.sibling())]
+    more[0].start()
+    piece(6, x_ref.at[lo, slot_d], me.beside()).wait_recv()
+    more.append(piece(7, x_ref.at[lo, slot_d], me.sibling()))
+    more[1].start()
+    sends += more
+    for k in (1, 2, 3):
+        src = (f + 4 - k) % 4
+        for j in range(3):
+            remote(
+                weights[j].at[:, cols(0, 128)], w3_ref.at[w3_rows(src), pl.ds(128 * j, 128)],
+                s_w.at[j, k - 1], r_w.at[j, k - 1], me.fsdp(k),
+            ).wait()
+    for j in range(3):
+        pltpu.make_async_copy(
+            weights[j].at[:, cols(b * 4 + swapped(f), 128)], w3_ref.at[w3_rows(f), pl.ds(128 * j, 128)], loc.at[2 + j]
+        ).wait()
+    o_fwd[0].wait()
+    o_fwd[1].wait()
+    late = remote(wo_ref.at[wo_rows(xs, 1 - b)], wo_ref.at[wo_rows(xs, 1 - b)], s_o.at[4], r_o.at[4], me.sibling())
+    late.start()
+    for i, where, part in (
+        (0, own, slot + other), (3, own, slot_x + other), (5, own, slot_y + other),
+    ):
+        piece(i, x_ref.at[:, part], me.sibling()).wait_recv()
+    piece(8, x_ref.at[hi, slot_d + other], me.sibling()).wait_recv()
+    piece(7, x_ref.at[lo, slot_d + other], me.sibling()).wait_recv()
+
+    def project(i, carry):
+        part = dense(x_ref[pl.ds(2 * i, 2)].reshape(256, 1024), w3_ref[...]) + bias_ref[...]
+        part = part.astype(BF)
+        rows = cols(i, 256)
+        q_ref[rows, :] = part[:, :PAIR]
+        k_ref[rows, :] = part[:, PAIR : 2 * PAIR]
+        v_ref[rows, :] = part[:, 2 * PAIR :]
+        return carry
+
+    lax.fori_loop(0, 8, project, 0)
+
+    for i, c in enumerate(u_x):
+        c.wait()
+    u_fwd = [
+        remote(wu_ref.at[wo_rows(src, b)], wu_ref.at[wo_rows(src, b)], s_u.at[3 + i], r_u.at[3 + i], me.across())
+        for i, src in enumerate((xs, xo))
+    ]
+    for c in u_fwd:
+        c.start()
+    for c in sends:
+        c.wait_send()
+    late.wait()
+    o_own.wait()
+    o_sib.wait()
+    u_own.wait()
+    u_sib.wait()
+    relocated(1, ends_ref, ends_out)
+    relocated(7, cot_ref, up_ref)
+    for c in u_fwd:
+        c.wait()
+
+
+def start(tokens, cotangent, ends, query_w, key_w, value_w, output_w, expand_w, bias3):
+    dma = pltpu.SemaphoreType.DMA
+    hbm = pl.BlockSpec(memory_space=pl.ANY)
+    heads = jax.ShapeDtypeStruct((2048, PAIR), BF)
+    square = jax.ShapeDtypeStruct((1024, 1024), BF)
+    return pl.pallas_call(
+        start_kernel,
+        out_shape=(
+            jax.ShapeDtypeStruct((16, GROUP, 16, 1024), BF), jax.ShapeDtypeStruct((16, 16, 1024), BF),
+            jax.ShapeDtypeStruct((8, 128), jnp.int32), heads, heads, heads,
+            jax.ShapeDtypeStruct((1024, 3 * PAIR), BF), square, square,
+        ),
+        in_specs=[hbm, hbm, VMEM] + [hbm] * 5 + [VMEM],
+        out_specs=(VMEM,) * 9,
+        scratch_shapes=[
+            dma((8,)), dma((8,)), dma((3, 3)), dma((3, 3)), dma((5,)), dma((5,)), dma((5,)), dma((5,)),
+            dma((9,)), dma((9,)), dma((8,)),
+        ],
+        compiler_params=pltpu.CompilerParams(collective_id=3, has_side_effects=True, vmem_limit_bytes=40 * 2**20),
+        cost_estimate=pl.CostEstimate(flops=2 * 10**9, bytes_accessed=20 * 2**20, transcendentals=0),
+    )(tokens, cotangent, ends, query_w, key_w, value_w, output_w, expand_w, bias3)
+
+
 def body(
     tokens, lengths, packing, query_w, query_b, key_w, value_w, value_b, output_w, output_b,
     attn_gain, attn_shift, expand_w, expand_b, reduce_w, reduce_b, ffn_gain, ffn_shift, cotangent,
@@ -841,35 +1060,12 @@
     g = ctx // per_group
     chunk = ctx % per_group // 2
     b = ctx % 2
-    swap = jnp.array(SWAP, jnp.int32)
-    u = swap[f] * 2 + b
-    pairs = [[2 * j, 2 * j + 1] for j in range(n_ctx // 2)]
-
-    route = []
-    for c0 in range(n_ctx):
-        for f0 in range(n_f):
-            g0, b0 = divmod(c0, per_group)
-            route.append((c0 * n_f + f0, (SWAP[f0] * per_group + b0) * n_f + SWAP[g0]))
-
-    def relocate(block):
-        return lax.ppermute(block, ("ctx", "fsdp"), route)
-
-    def order(block):
-        return jnp.stack([block[SWAP[i]] for i in range(n_f)])
-
-    def gather_group(block):
-        both = lax.all_gather(block, "ctx", axis_index_groups=pairs)
-        everyone = order(lax.all_gather(both, "fsdp"))
-        everyone = everyone.reshape(GROUP, laps, stripe, -1)
-        return everyone.transpose(1, 0, 2, 3).reshape(GROUP * mine, -1)
-
-    def columns(w):
-        return lax.all_to_all(w.reshape(w.shape[0], n_f, -1).transpose(1, 0, 2), "fsdp", 0, 0).reshape(
-            n_f * w.shape[0], -1
-        )
-
-    row_id = swap[g]
-    ordered_all = jnp.sum(
+    same_place = [
+        [(gg * chunks + s) * 2 + bb for s in range(chunks)] for gg in range(n_f) for bb in range(2)
+    ]
+    units = expand_w.shape[1] // n_f
+
+    ordered = jnp.sum(
         jnp.where(
             packing[0][:, None] == jnp.arange(lengths.shape[1], dtype=jnp.int32)[None, :],
             lengths[0][None, :],
@@ -877,9 +1073,27 @@
         ),
         axis=1,
     )
-    ordered = lax.all_gather(ordered_all, "fsdp")[row_id]
     slots = jnp.arange(ordered.shape[0], dtype=jnp.int32)
-    slot_ends = jnp.sum(jnp.where(slots[None, :] <= slots[:, None], ordered[None, :], 0), axis=1)
+    own_ends = jnp.sum(jnp.where(slots[None, :] <= slots[:, None], ordered[None, :], 0), axis=1)
+    own_ends = jnp.pad(own_ends[None], ((0, 7), (0, 128 - own_ends.shape[0])))
+
+    here = (b * n_f + swapped(f)) * PAIR
+    bias3 = jnp.concatenate(
+        [
+            lax.dynamic_slice_in_dim(query_b, here, PAIR),
+            jnp.zeros((PAIR,), F32),
+            lax.dynamic_slice_in_dim(value_b, here, PAIR),
+        ]
+    )[None]
+    acts = (laps, stripe, width)
+    x_all, upstream, ends, q, k_own, v_own, w_three, w_output, w_up = start(
+        tokens.reshape(acts), cotangent.reshape(acts), own_ends, query_w, key_w, value_w, output_w, expand_w, bias3
+    )
+    inputs = lax.dynamic_index_in_dim(x_all, swapped(f) * 2 + b, 1, keepdims=False).reshape(mine, width)
+    x_all = x_all.reshape(GROUP * mine, width)
+    upstream = upstream.reshape(mine, width)
+    slot_ends = ends[0, : ordered.shape[0]]
+
     span = GROUP * mine
     index = jnp.arange(span, dtype=jnp.int32)
 
@@ -901,26 +1115,6 @@
     seg_q = seg_q[:, None]
     seg_k = seg_k[None, :]
 
-    inputs = relocate(tokens.reshape(mine, width))
-    upstream = relocate(cotangent.reshape(mine, width))
-    x_all = gather_group(inputs)
-    w_three = jnp.stack([query_w, key_w, value_w]).reshape(3, -1, 2, n_f, PAIR)
-    w_three = lax.dynamic_index_in_dim(w_three, b, 2, keepdims=False)
-    w_three = order(w_three.transpose(2, 1, 0, 3).reshape(n_f, -1, 3 * PAIR))
-    w_three = lax.all_to_all(w_three, "fsdp", 0, 0).reshape(width, 3 * PAIR)
-    here = (b * n_f + swap[f]) * PAIR
-    bias3 = jnp.concatenate(
-        [
-            lax.dynamic_slice_in_dim(query_b, here, PAIR),
-            jnp.zeros((PAIR,), F32),
-            lax.dynamic_slice_in_dim(value_b, here, PAIR),
-        ]
-    )
-    three = (dense(x_all, w_three) + bias3).astype(BF)
-    q, k_own, v_own = three[:, :PAIR], three[:, PAIR : 2 * PAIR], three[:, 2 * PAIR :]
-    same_place = [
-        [(gg * chunks + s) * 2 + bb for s in range(chunks)] for gg in range(n_f) for bb in range(2)
-    ]
     if chunks == 1:
         k, v = k_own, v_own
     else:
@@ -928,9 +1122,6 @@
         v = lax.all_gather(v_own, "ctx", axis_index_groups=same_place, tiled=True)
     att_heads, lse = attend(bounds, q, k, v, seg_q, seg_k, chunks)
 
-    w_output = lax.all_gather(output_w, "fsdp", axis=0, tiled=True)
-    w_up = columns(expand_w)
-    units = w_up.shape[1]
     params = jnp.stack(
         [
             output_b, attn_gain, attn_shift, reduce_b, ffn_gain, ffn_shift,

time: 529 us -> 461 us (0.87)
  waiting for transfers between devices: 54 us -> 0 us
  Pallas kernels: 377 us -> 421 us
  blocking collectives: 24.5 us -> 0 us
  between operations: 17.7 us -> 1.09 us
  starting transfers between devices: 11.4 us -> 0 us
    pallas_call x0 -> x1, Pallas kernels: none -> 88.6 us  [start(): pl.pallas_call(start_kernel, out_shape=(jax.ShapeDtypeStruct((16, GROUP,...]
    pallas_call x1, Pallas kernels: 230 us -> 184 us  [tail(): pl.pallas_call(tail_kernel, out_shape=(jax.ShapeDtypeStruct((1024, 1024),...]
    all_gather x3 -> x0, waiting for transfers between devices: 44.4 us -> none  [the longest x1 43.2 us: gather_group(): both = lax.all_gather(block, 'ctx', axis_index_groups=pairs)]
    unnamed x1 -> x0, blocking collectives: 24.5 us -> none
    unnamed x77 -> x75, local copies, waits for them, and re-layouts: 10 us -> 19.1 us
    all_to_all x2 -> x0, waiting for transfers between devices: 8.87 us -> none  [the longest x1 8.87 us: columns(): lax.all_to_all(w.reshape(w.shape[0], n_f, -1).transpose(1, 0, 2), 'fsdp',...]
    all_to_all x2 -> x0, starting transfers between devices: 7.96 us -> none  [the longest x1 4.47 us: columns(): lax.all_to_all(w.reshape(w.shape[0], n_f, -1).transpose(1, 0, 2), 'fsdp',...]
  transfers between devices with their start and end apart: 7 -> 0, of which waited for: 3 -> 0; matrix products, arithmetic and copies ran while one was open for 4% -> 0% of each run, Pallas kernels for 3% -> 0%
where the time goes in v5:
time: 461 us; the launch traced here: 462 us
  Pallas kernels  421 us (91%)
  local copies, waits for them, and re-layouts  28.8 us (6%)
  other arithmetic  10.7 us (2%)
    pallas_call x1, Pallas kernels, tail(): pl.pallas_call(tail_kernel, out_shape=(jax.ShapeDtypeStruct((1024, 1024),...  184 us
    pallas_call x1, Pallas kernels, middle(): pl.pallas_call(middle_kernel, out_shape=(jax.ShapeDtypeStruct((256, 1024)...  108 us
    pallas_call x1, Pallas kernels, start(): pl.pallas_call(start_kernel, out_shape=(jax.ShapeDtypeStruct((16, GROUP,...  88.6 us
    pallas_call x1, Pallas kernels, attend_back(): pl.pallas_call(functools.partial(attend_back_kernel, BQ, BK, chunks), out...  22.8 us
    unnamed x75, local copies, waits for them, and re-layouts  19.1 us
    pallas_call x1, Pallas kernels, attend(): pl.pallas_call(functools.partial(attend_kernel, BQ, BK, chunks), out_shap...  18.5 us

profile of v5, /device:TPU:0, one launch (start us, length us, event | category | flops | bytes accessed | tf_op | source)
XLA Modules:
  0.0 462.0 jit_solution(379421120603672312)
XLA Ops:
  0.7 0.8 dynamic_slice.13
  2.2 0.9 select_reduce_fusion.1
  3.2 1.6 copy-done.9
  4.8 1.0 copy-done.10
  5.9 1.0 copy-done.11
  6.9 1.0 copy-done.12
  7.9 1.0 copy-done.13
  9.0 1.0 copy-done.14
  10.0 1.0 copy-done.15
  11.1 88.6 %shard_map.314 = (bf16[16,8,16,1024]{3,2,1,0:T(8,128)(2,1)}, bf16[16,16,1024]{2,1,0:T(8,128)(2,1)S(1)}, s32[8,128]{1,0:T(8,128)S(1)}, bf16[2048,128]{1,0:T(8,128...) custom-call(bf16[16,16,1024]{2,1,0:T(8,128)(2,1)S(1)} %bitcast.57, ...), custom_call_target="tpu_custom_call" | custom-call | flops 2000000000 | bytes 20971520 | tf_op jit(solution)/shard_map/pallas_call | solution.py:1029
  99.7 0.8 copy-done.16
  100.5 0.9 copy-done.17
  101.4 1.3 copy-done.18
  102.7 1.3 copy-done.19
  105.6 18.5 %shard_map.315 = (bf16[2048,128]{1,0:T(8,128)(2,1)S(1)}, f32[4096,1]{1,0:T(8,128)S(1)}) custom-call(s32[8,1]{1,0:T(8,128)S(1)} %copy.46.lo_ref, s32[8,1]{1,0:T(8,128)S(1)} %copy.47.hi_ref, bf16[2048,128]{1,0:T(8,128)(2,1)S(1)} %get-tuple-element.45.q_ref, bf16[2048,128]{1,0:T(8,128)(2,1)S(1)} %get-tuple-element.46.k_ref, ...), custom_call_target="tpu_custom_call" | custom-call | tf_op jit(solution)/shard_map/pallas_call | solution.py:170
  124.0 1.3 copy-done.1
  125.4 0.8 copy-done.5
  126.2 1.9 constant_dynamic-slice_fusion
  129.5 107.9 %shard_map.316 = (bf16[256,1024]{1,0:T(8,128)(2,1)}, bf16[1024,1024]{1,0:T(8,128)(2,1)}, bf16[1024,1024]{1,0:T(8,128)(2,1)}, bf16[1024,1024]{1,0:T(8,128)(2,1)},...) custom-call(bf16[16,8,16,128]{3,2,1,0:T(8,128)(2,1)} %bitcast.54, ...), custom_call_target="tpu_custom_call" | custom-call | flops 14000000000 | bytes 20971520 | tf_op jit(solution)/shard_map/pallas_call | solution.py:836
  237.4 22.8 %shard_map.317 = (bf16[2048,128]{1,0:T(8,128)(2,1)}, bf16[2048,128]{1,0:T(8,128)(2,1)}, bf16[2048,128]{1,0:T(8,128)(2,1)}) custom-call(s32[8,1]{1,0:T(8,128)} %copy-done.8, s32[8,1]{1,0:T(8,128)} %copy-done.7, bf16[2048,128]{1,0:T(8,128)(2,1)} %copy-done.2, bf16[2048,128]{1,0:T(8,128)(2,1)} %copy-done.3, bf16[2048,128]{1,0:T(8,128)(2,1)} %copy-done.4, ...), custom_call_target="tpu_custom_call" | custom-call | tf_op jit(solution)/shard_map/pallas_call | solution.py:182
  260.2 1.2 constant_dynamic-update-slice_fusion.2
  261.4 1.2 constant_dynamic-update-slice_fusion.1
  263.2 1.3 concatenate.11.vec_ref
  264.6 183.7 %shard_map.318 = (bf16[1024,1024]{1,0:T(8,128)(2,1)}, bf16[256,4096]{1,0:T(8,128)(2,1)}, bf16[256,1024]{1,0:T(8,128)(2,1)}, bf16[3,256,1024]{2,1,0:T(8,128)(2,1)...) custom-call(bf16[2048,1024]{1,0:T(8,128)(2,1)} %bitcast.63, bf16[2048,384]{1,0:T(8,128)(2,1)} %copy-done.20, ...), custom_call_target="tpu_custom_call" | custom-call | flops 4000000000 | bytes 41943040 | tf_op jit(solution)/shard_map/pallas_call | solution.py:607
  448.3 1.8 convert_element_type.56
  450.1 1.7 slice_bitcast_fusion
  451.8 1.0 copy-done.22
  452.8 2.5 convert_element_type.58
  455.3 2.5 convert_element_type.59
  457.8 1.1 bitcast_convert_fusion
  458.9 1.1 convert_element_type.57
  461.2 0.8 copy.61
  (91 shorter events, 5.6 us)
Async XLA Ops:
  3.2 1.6 copy-start.9
  4.8 1.0 copy-start.10
  5.9 1.0 copy-start.11
  6.9 1.0 copy-start.12
  7.9 1.0 copy-start.13
  9.0 1.0 copy-start.14
  10.0 1.0 copy-start.15
  101.4 1.3 copy-start.18
  102.7 1.3 copy-start.19
  104.0 24.1 %copy-start.2 = (bf16[2048,128]{1,0:T(8,128)(2,1)}, bf16[2048,128]{1,0:T(8,128)(2,1)S(1)}, u32[]{:S(2)}) copy-start(bf16[2048,128]{1,0:T(8,128)(2,1)S(1)} %get-tuple-element.45.q_ref) | copy-start | bytes 1572868
  104.0 24.1 %copy-start.3 = (bf16[2048,128]{1,0:T(8,128)(2,1)}, bf16[2048,128]{1,0:T(8,128)(2,1)S(1)}, u32[]{:S(2)}) copy-start(bf16[2048,128]{1,0:T(8,128)(2,1)S(1)} %get-tuple-element.46.k_ref) | copy-start | bytes 1572868
  104.0 24.1 %copy-start.4 = (bf16[2048,128]{1,0:T(8,128)(2,1)}, bf16[2048,128]{1,0:T(8,128)(2,1)S(1)}, u32[]{:S(2)}) copy-start(bf16[2048,128]{1,0:T(8,128)(2,1)S(1)} %get-tuple-element.47.v_ref) | copy-start | bytes 1572868
  104.2 23.9 %copy-start.6 = (s32[2048]{0:T(1024)}, s32[2048]{0:T(1024)S(1)}, u32[]{:S(2)}) copy-start(s32[2048]{0:T(1024)S(1)} %get-tuple-element.72) | copy-start | bytes 24580
  104.6 132.8 %copy-start = (s32[2048,1]{1,0:T(8,128)}, s32[2048,1]{1,0:T(8,128)S(1)}, u32[]{:S(2)}) copy-start(s32[2048,1]{1,0:T(8,128)S(1)} %copy.48.sq_ref) | copy-start | bytes 24580
  104.6 24.2 %copy-start.29 = (f32[1024]{0:T(1024)S(1)}, f32[1024]{0:T(1024)}, u32[]{:S(2)}) copy-start(f32[1024]{0:T(1024)} %param.28) | copy-start | bytes 12292
  104.6 24.2 %copy-start.30 = (f32[1024]{0:T(1024)S(1)}, f32[1024]{0:T(1024)}, u32[]{:S(2)}) copy-start(f32[1024]{0:T(1024)} %param.29) | copy-start | bytes 12292
  104.6 24.2 %copy-start.31 = (f32[1024]{0:T(1024)S(1)}, f32[1024]{0:T(1024)}, u32[]{:S(2)}) copy-start(f32[1024]{0:T(1024)} %param.30) | copy-start | bytes 12292
  104.6 24.2 %copy-start.32 = (f32[1024]{0:T(1024)S(1)}, f32[1024]{0:T(1024)}, u32[]{:S(2)}) copy-start(f32[1024]{0:T(1024)} %param.34) | copy-start | bytes 12292
  104.6 24.2 %copy-start.33 = (f32[1024]{0:T(1024)S(1)}, f32[1024]{0:T(1024)}, u32[]{:S(2)}) copy-start(f32[1024]{0:T(1024)} %param.35) | copy-start | bytes 12292
  104.6 24.2 %copy-start.34 = (f32[1024]{0:T(1024)S(1)}, f32[1024]{0:T(1024)}, u32[]{:S(2)}) copy-start(f32[1024]{0:T(1024)} %param.36) | copy-start | bytes 12292
  105.1 132.3 %copy-start.7 = (s32[8,1]{1,0:T(8,128)}, s32[8,1]{1,0:T(8,128)S(1)}, u32[]{:S(2)}) copy-start(s32[8,1]{1,0:T(8,128)S(1)} %copy.47.hi_ref) | copy-start | bytes 100
  105.6 131.8 %copy-start.8 = (s32[8,1]{1,0:T(8,128)}, s32[8,1]{1,0:T(8,128)S(1)}, u32[]{:S(2)}) copy-start(s32[8,1]{1,0:T(8,128)S(1)} %copy.46.lo_ref) | copy-start | bytes 100
  124.0 1.4 copy-start.1
  260.2 2.4 copy-start.26
  261.4 1.7 copy-start.27
  262.7 1.9 copy-start.20
  450.1 2.7 copy-start.22
  452.8 2.5 copy-start.21
  455.3 2.5 copy-start.24
  455.3 3.6 copy-start.23
  457.8 2.2 copy-start.28
  457.8 3.4 copy-start.25
  (3 other events, 2.5 us)

commit v6 on v5

--- a/solution.py
+++ b/solution.py
@@ -86,7 +86,7 @@
             same = seg2 == sk_ref[:, keys]
             scores = jnp.where(same, scores, -1e30)
             new_max = jnp.maximum(run_max, jnp.max(scores, axis=1, keepdims=True))
-            probs = jnp.where(same, jnp.exp(scores - new_max), 0.0)
+            probs = jnp.exp(scores - new_max)
             scale = jnp.exp(run_max - new_max)
             run_sum = run_sum * scale + jnp.sum(probs, axis=1, keepdims=True)
             accum = accum * scale + dense(probs.astype(BF), v_ref[keys, :])
@@ -108,6 +108,42 @@
     lax.fori_loop(0, nq, q_step, 0)
 
 
+def attend_back_rows(i, bq, bk, ranges, q_ref, k_ref, v_ref, sq_ref, sk_ref, o_ref, lse_ref, g_ref, dk_sum, dv_sum):
+    rows = pl.ds(pl.multiple_of(i * bq, bq), bq)
+    q2 = both_heads(q_ref[rows, :] * BF(0.125))
+    grad = g_ref[rows, :]
+    g2 = both_heads(grad)
+    prod = grad.astype(F32) * o_ref[rows, :].astype(F32)
+    left = first_half(prod.shape)
+    delta = jnp.concatenate(
+        [
+            jnp.sum(jnp.where(left, prod, 0.0), axis=1, keepdims=True),
+            jnp.sum(jnp.where(left, 0.0, prod), axis=1, keepdims=True),
+        ],
+        axis=0,
+    )
+    lse = lse_ref[pl.ds(pl.multiple_of(2 * i * bq, 2 * bq), 2 * bq), :]
+    seg = sq_ref[rows, :]
+    seg2 = jnp.concatenate([seg, seg], axis=0)
+
+    def k_step(j, dq2):
+        keys = pl.ds(pl.multiple_of(j * bk, bk), bk)
+        key_rows = k_ref[keys, :]
+        scores = dense_back(q2, key_rows)
+        same = seg2 == sk_ref[:, keys]
+        probs = jnp.exp(jnp.where(same, scores, -1e30) - lse)
+        grad_prob = dense_back(g2, v_ref[keys, :])
+        grad_score = (probs * (grad_prob - delta)).astype(BF)
+        dv_sum[keys, :] += dense_in(probs.astype(BF), g2)
+        dk_sum[keys, :] += dense_in(grad_score, q2)
+        return dq2 + dense(grad_score, key_rows)
+
+    dq2 = jnp.zeros((2 * bq, PAIR), F32)
+    for first, last in ranges:
+        dq2 = lax.fori_loop(first, last, k_step, dq2)
+    return (0.125 * by_head(dq2)).astype(BF)
+
+
 def attend_back_kernel(
     bq, bk, chunks, lo_ref, hi_ref, q_ref, k_ref, v_ref, sq_ref, sk_ref, o_ref, lse_ref, g_ref,
     dq_ref, dk_ref, dv_ref, dk_sum, dv_sum,
@@ -118,40 +154,10 @@
     dv_sum[...] = jnp.zeros_like(dv_sum)
 
     def q_step(i, carry):
-        rows = pl.ds(pl.multiple_of(i * bq, bq), bq)
-        q2 = both_heads(q_ref[rows, :] * BF(0.125))
-        grad = g_ref[rows, :]
-        g2 = both_heads(grad)
-        prod = grad.astype(F32) * o_ref[rows, :].astype(F32)
-        left = first_half(prod.shape)
-        delta = jnp.concatenate(
-            [
-                jnp.sum(jnp.where(left, prod, 0.0), axis=1, keepdims=True),
-                jnp.sum(jnp.where(left, 0.0, prod), axis=1, keepdims=True),
-            ],
-            axis=0,
+        ranges = [(s * per_chunk + lo_ref[i, s], s * per_chunk + hi_ref[i, s]) for s in range(chunks)]
+        dq_ref[pl.ds(pl.multiple_of(i * bq, bq), bq), :] = attend_back_rows(
+            i, bq, bk, ranges, q_ref, k_ref, v_ref, sq_ref, sk_ref, o_ref, lse_ref, g_ref, dk_sum, dv_sum
         )
-        lse = lse_ref[pl.ds(pl.multiple_of(2 * i * bq, 2 * bq), 2 * bq), :]
-        seg = sq_ref[rows, :]
-        seg2 = jnp.concatenate([seg, seg], axis=0)
-
-        def k_step(j, dq2):
-            keys = pl.ds(pl.multiple_of(j * bk, bk), bk)
-            key_rows = k_ref[keys, :]
-            scores = dense_back(q2, key_rows)
-            same = seg2 == sk_ref[:, keys]
-            probs = jnp.where(same, jnp.exp(jnp.where(same, scores, -1e30) - lse), 0.0)
-            grad_prob = dense_back(g2, v_ref[keys, :])
-            grad_score = (probs * (grad_prob - delta)).astype(BF)
-            dv_sum[keys, :] += dense_in(probs.astype(BF), g2)
-            dk_sum[keys, :] += dense_in(grad_score, q2)
-            return dq2 + dense(grad_score, key_rows)
-
-        dq2 = jnp.zeros((2 * bq, PAIR), F32)
-        for s in range(chunks):
-            base = s * per_chunk
-            dq2 = lax.fori_loop(base + lo_ref[i, s], base + hi_ref[i, s], k_step, dq2)
-        dq_ref[rows, :] = (0.125 * by_head(dq2)).astype(BF)
         return carry
 
     lax.fori_loop(0, nq, q_step, 0)
@@ -320,11 +326,23 @@
                 self.copy(p, 0, self.ahead).wait_send()
 
 
-def tail_kernel(
+QUARTERS = ((0, 2), (0, 3), (1, 4), (2, 4))
+
+
+def tail_kernel(fused, *refs):
+    if fused:
+        attention, refs, (g3_ref, dk_sum, dv_sum) = refs[:8], refs[8:-3], refs[-3:]
+        tail_steps(attention, dk_sum, dv_sum, refs[0], g3_ref, *refs[1:])
+    else:
+        tail_steps(None, None, None, *refs)
+
+
+def tail_steps(
+    attention, dk_sum, dv_sum,
     x_ref, g3_ref, w3_ref, down_ref, up_ref, out_ref, mid_ref, vec_ref,
     down_out, up_out, o_out, three_out, dx_ref, sums_ref,
     dxp, dx1, t1, xa, yb, t2a, t2b, ra, rb, moved_buf,
-    yr_down, yr_up, dbuf, dgot, ubuf, ugot,
+    yr_up, dbuf, dgot, ubuf, ugot,
     o_got, o_sum, yr_o, obuf, ogot,
     gq, qbuf, qgot, vs, vr,
     s_dx, r_dx, s_y, r_y, s_d, r_d, s_z, r_z, s_u, r_u, s_o, r_o, s_oz, r_oz, s_q, r_q,
@@ -336,7 +354,7 @@
     meet(me, [me.across()] + [me.fsdp(k) for k in (1, 2, 3)] + z_others, True)
 
     def own_down(p):
-        return down_ref[b, p].astype(F32) + yr_down[p].astype(F32)
+        return down_ref[p].astype(F32)
 
     def own_up(p):
         return up_ref[:, b, p].astype(F32) + yr_up[p].astype(F32)
@@ -352,120 +370,94 @@
     flow_q = Flow(me, own_q, qbuf, qgot, s_q, r_q)
     flow_o = Flow(me, own_o, obuf, ogot, s_oz, r_oz)
 
+    edge, inner = flow_d.inner == 0, flow_d.inner == 1
+
+    def at(which, *steps):
+        @pl.when(which)
+        def _():
+            for step in steps:
+                step()
+
     y_copies = []
     for i in range(4):
-        p = flow_d.piece(i)
-        pair = (
-            remote(down_ref.at[1 - b, p], yr_down.at[p], s_y.at[0, i], r_y.at[0, i], me.across()),
-            remote(up_ref.at[:, 1 - b, p], yr_up.at[p], s_y.at[1, i], r_y.at[1, i], me.across()),
-        )
-        for c in pair:
-            c.start()
-        y_copies.append(pair)
-
-    hops = [me.sibling(), me.beside(), me.across(), me.at(g=g + 1 - 2 * (g % 2)), me.at(g=(g + 2) % 4)]
-    vec = vec_ref[...]
-
-    def hop(i, vec):
-        vs[i] = vec
-        c = remote(vs.at[i], vr.at[i], s_v.at[i], r_v.at[i], hops[i])
+        p = flow_u.piece(i)
+        c = remote(up_ref.at[:, 1 - b, p], yr_up.at[p], s_y.at[0, i], r_y.at[0, i], me.across())
         c.start()
-        return c
-
-    v_copies = [hop(0, vec)]
-
-    def hop_end(i, vec):
-        v_copies[i].wait()
-        return vec + vr[i]
+        y_copies.append(c)
 
     o_copies = []
     for k in (1, 2, 3):
         c = remote(out_ref.at[(f + k) % 4], o_got.at[k - 1], s_o.at[k - 1], r_o.at[k - 1], me.fsdp(k))
         c.start()
         o_copies.append(c)
-
-    def q_step(i, carry):
-        cols = pl.ds(pl.multiple_of(i * 256, 256), 256)
-        part = dense_in(x_ref[:, cols], g3_ref[...]).astype(BF)
-        for j in range(3):
-            gq[i, j] = part[:, j * 128 : (j + 1) * 128].reshape(4, 64, 128)
-        return carry
-
-    lax.fori_loop(0, 4, q_step, 0)
-    vec = hop_end(0, vec)
-    v_copies.append(hop(1, vec))
-    for i in range(3):
-        @pl.when(flow_q.inner == 0)
-        def _():
-            flow_q.forward(i)
-
-    def dx_step(i, carry):
-        rows = pl.ds(pl.multiple_of(i * 256, 256), 256)
-        part = dense_back(g3_ref[rows, :], w3_ref[...]).astype(BF)
-        dxp[pl.ds(2 * i, 2)] = part.reshape(2, 2, 2, 2, 16, 1024)
-        return carry
-
-    lax.fori_loop(0, 8, dx_step, 0)
-    c_core = remote(dxp.at[:, 1 - me.core], dx1, s_dx.at[0], r_dx.at[0], me.sibling())
-    c_core.start()
-    vec = hop_end(1, vec)
-    v_copies.append(hop(2, vec))
-
-    @pl.when(flow_q.inner == 1)
-    def _():
-        flow_q.forward(0)
-        flow_q.forward(1)
-
-    def large(i):
-        for c in y_copies[i]:
+    c_oy = remote(o_sum.at[1 - b], yr_o, s_y.at[1, 0], r_y.at[1, 0], me.across())
+
+    def up_forward(i):
+        y_copies[i].wait()
+        flow_u.forward(i)
+
+    def up_back():
+        y_copies[3].wait()
+        flow_u.back()
+
+    def output_rows():
+        for c in o_copies:
             c.wait()
-        flow_d.forward(i)
-        flow_u.forward(i)
-
-    c_core.wait()
-
-    def t1_step(i, carry):
-        t1[i] = (dxp[i, me.core].astype(F32) + dx1[i].astype(F32)).astype(BF)
-        return carry
-
-    lax.fori_loop(0, 16, t1_step, 0)
-    lo, hi = pl.ds(0, 8), pl.ds(8, 8)
-    c_xa = remote(t1.at[lo, 1 - me.x], xa, s_dx.at[1], r_dx.at[1], me.beside())
-    c_yb = remote(t1.at[hi, :, 1 - b], yb, s_dx.at[2], r_dx.at[2], me.across())
-    c_xa.start()
-    c_yb.start()
-
-    large(0)
-    flow_q.back()
-    large(1)
-
-    for c in o_copies:
-        c.wait()
-    o_sum[...] = (
-        out_ref[f].astype(F32) + o_got[0].astype(F32) + o_got[1].astype(F32) + o_got[2].astype(F32)
-    ).astype(BF)
-    c_oy = remote(o_sum.at[1 - b], yr_o, s_y.at[0, 4], r_y.at[0, 4], me.across())
-    c_oy.start()
-
-    large(2)
-    c_xa.wait()
-    t2a[...] = (t1[lo, me.x].astype(F32) + xa[...].astype(F32)).astype(BF)
-    c_ra = remote(t2a.at[:, 1 - b], ra, s_dx.at[3], r_dx.at[3], me.across())
-    c_ra.start()
-    for c in y_copies[3]:
-        c.wait()
-    flow_d.back()
-    flow_u.back()
-    vec = hop_end(2, vec)
-    v_copies.append(hop(3, vec))
-    c_oy.wait()
-    for i in range(3):
-        flow_o.forward(i)
-    c_yb.wait()
-    t2b[...] = (t1[hi, :, b].astype(F32) + yb[...].astype(F32)).astype(BF)
-    c_rb = remote(t2b.at[:, 1 - me.x], rb, s_dx.at[4], r_dx.at[4], me.beside())
-    c_rb.start()
-    flow_o.back()
+        o_sum[...] = (
+            out_ref[f].astype(F32) + o_got[0].astype(F32) + o_got[1].astype(F32) + o_got[2].astype(F32)
+        ).astype(BF)
+        c_oy.start()
+
+    at(edge, *(functools.partial(flow_d.forward, i) for i in range(3)))
+    do = functools.partial
+    between = (
+        ((edge, do(up_forward, 0)), (inner, do(flow_d.forward, 0))),
+        ((True, output_rows), (edge, do(up_forward, 1)), (inner, do(flow_d.forward, 1), do(up_forward, 0))),
+        ((edge, do(up_forward, 2)), (inner, flow_d.back, do(up_forward, 1))),
+        ((edge, y_copies[3].wait), (inner, y_copies[2].wait, up_back)),
+    )
+    if attention is not None:
+        dk_sum[...] = jnp.zeros_like(dk_sum)
+        dv_sum[...] = jnp.zeros_like(dv_sum)
+    per = 2048 // BQ // 4
+    for quarter, (first, last) in enumerate(QUARTERS):
+        ranges = [(first * 512 // BK, last * 512 // BK)]
+
+        def rows_step(i, carry):
+            g3_ref[pl.ds(pl.multiple_of(i * BQ, BQ), BQ), pl.ds(0, PAIR)] = attend_back_rows(
+                i, BQ, BK, ranges, *attention, dk_sum, dv_sum
+            )
+            return carry
+
+        if attention is not None:
+            lax.fori_loop(quarter * per, (quarter + 1) * per, rows_step, 0)
+        for which, *steps in between[quarter]:
+            if which is True:
+                for step in steps:
+                    step()
+            else:
+                at(which, *steps)
+    if attention is not None:
+        g3_ref[:, pl.ds(PAIR, PAIR)] = dk_sum[...].astype(BF)
+        g3_ref[:, pl.ds(2 * PAIR, PAIR)] = dv_sum[...].astype(BF)
+
+    hops = [me.sibling(), me.beside(), me.across(), me.at(g=g + 1 - 2 * (g % 2)), me.at(g=(g + 2) % 4)]
+    vs[0] = vec_ref[...]
+    here = pl.ds(pl.multiple_of((b * 4 + swapped(f)) * PAIR, PAIR), PAIR)
+    sums3 = jnp.sum(g3_ref[...].astype(F32), axis=0, keepdims=True)
+    vs[0, pl.ds(0, 1), here] = sums3[:, :PAIR]
+    vs[0, pl.ds(1, 1), here] = sums3[:, 2 * PAIR :]
+
+    def hop(i):
+        if i > 0:
+            hop_copy(i - 1).wait()
+            vs[i] = vs[i - 1] + vr[i - 1]
+        hop_copy(i).start()
+
+    def hop_copy(i):
+        return remote(vs.at[i], vr.at[i], s_v.at[i], r_v.at[i], hops[i])
+
+    hop(0)
 
     def rows(size, q, other=False):
         half = 1 - b if other else b
@@ -480,13 +472,43 @@
     def q_rows(q):
         return pl.ds(pl.multiple_of(q * 64, 64), 64)
 
-    flow_q.end()
-    three_out[:, q_rows(g), head_cols(f)] = qbuf[g, f]
-    q_out = []
-    for k in (1, 2, 3):
-        c = remote(qbuf.at[g, (f + k) % 4], three_out.at[:, q_rows(g), head_cols(f)], s_qf.at[k - 1], r_qf.at[f], me.fsdp(k))
-        c.start()
-        q_out.append(c)
+    def pieces(kind, q, send, recv, where, other=False):
+        half = 1 - b if other else b
+        if kind == 0:
+            parts = (down_out.at[rows(128, q, other), :], up_out.at[rows(32, q, other), :])
+        else:
+            parts = (
+                o_out.at[rows(32, q, other), :],
+                three_out.at[:, q_rows(q), pl.ds(pl.multiple_of(half * 512, 512), 512)],
+            )
+        return [remote(part, part, send.at[2 * kind + i, q], recv.at[2 * kind + i, q], where) for i, part in enumerate(parts)]
+
+    def spread(kind, q, to_right, to_left):
+        if to_right:
+            @pl.when(g < 3)
+            def _():
+                for c in pieces(kind, q, s_ag.at[0], r_ag, me.at(g=g + 1)):
+                    c.start()
+        if to_left:
+            @pl.when(g > 0)
+            def _():
+                for c in pieces(kind, q, s_ag.at[1], r_ag, me.at(g=g - 1)):
+                    c.start()
+        for c in pieces(kind, q, s_ay, r_ay, me.across()):
+            c.start()
+
+    def pass_on(kind, d):
+        @pl.when(g >= d)
+        def _():
+            for c in pieces(kind, g - d, s_ag.at[0], r_ag, me.across()):
+                c.wait_recv()
+            spread(kind, g - d, True, False)
+
+        @pl.when(g + d <= 3)
+        def _():
+            for c in pieces(kind, g + d, s_ag.at[1], r_ag, me.across()):
+                c.wait_recv()
+            spread(kind, g + d, False, True)
 
     flow_u.end()
     up_out[rows(32, g), unit_cols(f)] = ubuf[g, f]
@@ -497,41 +519,79 @@
         u_out.append(c)
     flow_d.end()
     down_out[rows(128, g), :] = dbuf[g]
+
+    def q_step(i, carry):
+        cols = pl.ds(pl.multiple_of(i * 256, 256), 256)
+        part = dense_in(x_ref[:, cols], g3_ref[...]).astype(BF)
+        for j in range(3):
+            gq[i, j] = part[:, j * 128 : (j + 1) * 128].reshape(4, 64, 128)
+        return carry
+
+    lax.fori_loop(0, 4, q_step, 0)
+    for k in (1, 2, 3):
+        src = (f + k) % 4
+        remote(ubuf.at[g, 0], up_out.at[rows(32, g), unit_cols(src)], s_u.at[k - 1], r_u.at[src], me.fsdp(k)).wait_recv()
+        u_out[k - 1].wait_send()
+    spread(0, g, True, True)
+    at(edge, *(do(flow_q.forward, i) for i in range(3)))
+    c_oy.wait()
+    at(edge, *(do(flow_o.forward, i) for i in range(3)))
+    hop(1)
+
+    def dx_step(i, carry):
+        rows = pl.ds(pl.multiple_of(i * 256, 256), 256)
+        part = dense_back(g3_ref[rows, :], w3_ref[...]).astype(BF)
+        dxp[pl.ds(2 * i, 2)] = part.reshape(2, 2, 2, 2, 16, 1024)
+        return carry
+
+    lax.fori_loop(0, 8, dx_step, 0)
+    c_core = remote(dxp.at[:, 1 - me.core], dx1, s_dx.at[0], r_dx.at[0], me.sibling())
+    c_core.start()
+    at(inner, do(flow_q.forward, 0), do(flow_q.forward, 1), do(flow_o.forward, 0), do(flow_o.forward, 1))
+    hop(2)
+
+    c_core.wait()
+
+    def t1_step(i, carry):
+        t1[i] = (dxp[i, me.core].astype(F32) + dx1[i].astype(F32)).astype(BF)
+        return carry
+
+    lax.fori_loop(0, 16, t1_step, 0)
+    lo, hi = pl.ds(0, 8), pl.ds(8, 8)
+    c_xa = remote(t1.at[lo, 1 - me.x], xa, s_dx.at[1], r_dx.at[1], me.beside())
+    c_yb = remote(t1.at[hi, :, 1 - b], yb, s_dx.at[2], r_dx.at[2], me.across())
+    c_xa.start()
+    c_yb.start()
+    pass_on(0, 1)
+    flow_q.back()
+    flow_o.back()
+
+    flow_q.end()
+    three_out[:, q_rows(g), head_cols(f)] = qbuf[g, f]
+    q_out = []
+    for k in (1, 2, 3):
+        c = remote(qbuf.at[g, (f + k) % 4], three_out.at[:, q_rows(g), head_cols(f)], s_qf.at[k - 1], r_qf.at[f], me.fsdp(k))
+        c.start()
+        q_out.append(c)
     flow_o.end()
     o_out[rows(32, g), :] = obuf[g]
-
+    c_xa.wait()
+    t2a[...] = (t1[lo, me.x].astype(F32) + xa[...].astype(F32)).astype(BF)
+    c_ra = remote(t2a.at[:, 1 - b], ra, s_dx.at[3], r_dx.at[3], me.across())
+    c_ra.start()
     for k in (1, 2, 3):
         src = (f + k) % 4
         remote(qbuf.at[g, 0], three_out.at[:, q_rows(g), head_cols(src)], s_qf.at[k - 1], r_qf.at[src], me.fsdp(k)).wait_recv()
-        remote(ubuf.at[g, 0], up_out.at[rows(32, g), unit_cols(src)], s_u.at[k - 1], r_u.at[src], me.fsdp(k)).wait_recv()
         q_out[k - 1].wait_send()
-        u_out[k - 1].wait_send()
-
-    def pieces(q, send, recv, where, other=False):
-        half = 1 - b if other else b
-        parts = (
-            down_out.at[rows(128, q, other), :],
-            up_out.at[rows(32, q, other), :],
-            o_out.at[rows(32, q, other), :],
-            three_out.at[:, q_rows(q), pl.ds(pl.multiple_of(half * 512, 512), 512)],
-        )
-        return [remote(part, part, send.at[i, q], recv.at[i, q], where) for i, part in enumerate(parts)]
-
-    def spread(q, to_right, to_left):
-        for c in pieces(q, s_ay, r_ay, me.across()):
-            c.start()
-        if to_right:
-            @pl.when(g < 3)
-            def _():
-                for c in pieces(q, s_ag.at[0], r_ag, me.at(g=g + 1)):
-                    c.start()
-        if to_left:
-            @pl.when(g > 0)
-            def _():
-                for c in pieces(q, s_ag.at[1], r_ag, me.at(g=g - 1)):
-                    c.start()
-
-    spread(g, True, True)
+    spread(1, g, True, True)
+    pass_on(0, 2)
+    pass_on(1, 1)
+    c_yb.wait()
+    t2b[...] = (t1[hi, :, b].astype(F32) + yb[...].astype(F32)).astype(BF)
+    c_rb = remote(t2b.at[:, 1 - me.x], rb, s_dx.at[4], r_dx.at[4], me.beside())
+    c_rb.start()
+    hop(3)
+    pass_on(0, 3)
     c_ra.wait()
     c_rb.wait()
     moved_buf[lo] = (t2a[:, b].astype(F32) + ra[...].astype(F32) + mid_ref[lo]).astype(BF)
@@ -547,54 +607,44 @@
     def _():
         remote(moved_buf, dx_ref, s_dx.at[5], r_dx.at[5], me.moved()).start()
 
-    vec = hop_end(3, vec)
-    v_copies.append(hop(4, vec))
-    for d in (1, 2, 3):
-        @pl.when(g >= d)
-        def _():
-            for c in pieces(g - d, s_ag.at[0], r_ag, me.across()):
-                c.wait_recv()
-            spread(g - d, True, False)
-
-        @pl.when(g + d <= 3)
-        def _():
-            for c in pieces(g + d, s_ag.at[1], r_ag, me.across()):
-                c.wait_recv()
-            spread(g + d, False, True)
-
-    vec = hop_end(4, vec)
-    sums_ref[...] = vec
+    pass_on(1, 2)
+    hop(4)
+    pass_on(1, 3)
+    hop_copy(4).wait()
+    sums_ref[...] = vs[4] + vr[4]
 
     @pl.when(jnp.logical_not(me.stays()))
     def _():
         remote(moved_buf, dx_ref, s_dx.at[5], r_dx.at[5], me.moved()).wait()
 
-    for q in range(4):
-        for c in pieces(q, s_ay, r_ay, me.across()):
-            c.wait_send()
-
-        @pl.when((g >= q) & (g < 3))
-        def _():
-            for c in pieces(q, s_ag.at[0], r_ag, me.across()):
+    for kind in (0, 1):
+        for q in range(4):
+            for c in pieces(kind, q, s_ay, r_ay, me.across()):
                 c.wait_send()
 
-        @pl.when((g <= q) & (g > 0))
-        def _():
-            for c in pieces(q, s_ag.at[1], r_ag, me.across()):
-                c.wait_send()
-
-        for c in pieces(q, s_ay, r_ay, me.across(), other=True):
-            c.wait_recv()
-
-
-def tail(x_all, g3, w3, down, up, out, mid, vec):
+            @pl.when((g >= q) & (g < 3))
+            def _():
+                for c in pieces(kind, q, s_ag.at[0], r_ag, me.across()):
+                    c.wait_send()
+
+            @pl.when((g <= q) & (g > 0))
+            def _():
+                for c in pieces(kind, q, s_ag.at[1], r_ag, me.across()):
+                    c.wait_send()
+
+            for c in pieces(kind, q, s_ay, r_ay, me.across(), other=True):
+                c.wait_recv()
+
+
+def tail(attention, x_all, g3, w3, down, up, out, mid, vec):
+    fused = attention is not None
     dma = pltpu.SemaphoreType.DMA
     v = pltpu.VMEM
     scratch = [
         v((16, 2, 2, 2, 16, 1024), BF), v((16, 2, 2, 16, 1024), BF), v((16, 2, 2, 16, 1024), BF),
         v((8, 2, 16, 1024), BF), v((8, 2, 16, 1024), BF), v((8, 2, 16, 1024), BF), v((8, 2, 16, 1024), BF),
         v((8, 16, 1024), BF), v((8, 16, 1024), BF), v((16, 16, 1024), BF),
-        v((4, 128, 1024), BF), v((4, 4, 32, 1024), BF), v((4, 128, 1024), BF), v((2, 4, 128, 1024), BF),
+        v((4, 4, 32, 1024), BF), v((4, 128, 1024), BF), v((2, 4, 128, 1024), BF),
         v((4, 4, 32, 1024), BF), v((2, 4, 4, 32, 1024), BF),
         v((3, 2, 4, 32, 1024), BF), v((2, 4, 32, 1024), BF), v((4, 32, 1024), BF),
         v((4, 32, 1024), BF), v((2, 4, 32, 1024), BF),
@@ -604,8 +654,17 @@
         dma((3,)), dma((4,)), dma((3,)), dma((3,)), dma((4,)), dma((2, 4)), dma((4,)), dma((2, 4)),
         dma((3,)), dma((4,)), dma((5,)), dma((5,)), dma((2, 4, 4)), dma((4, 4)), dma((4, 4)), dma((4, 4)), dma((1,)),
     ]
+    if fused:
+        scratch += [v((2048, 3 * PAIR), BF), v((2048, PAIR), F32), v((2048, PAIR), F32)]
+        operands = (*attention, x_all)
+    else:
+        operands = (x_all, g3)
+    operands += (
+        w3, down.reshape(4, 128, 1024), up.reshape(4, 2, 4, 32, 1024), out.reshape(4, 2, 4, 32, 1024),
+        mid.reshape(16, 16, 1024), vec,
+    )
     return pl.pallas_call(
-        tail_kernel,
+        functools.partial(tail_kernel, fused),
         out_shape=(
             jax.ShapeDtypeStruct((1024, 1024), BF),
             jax.ShapeDtypeStruct((256, 4096), BF),
@@ -614,12 +673,12 @@
             jax.ShapeDtypeStruct((16, 16, 1024), BF),
             jax.ShapeDtypeStruct((16, 1024), F32),
         ),
-        in_specs=[VMEM] * 8,
+        in_specs=[VMEM] * len(operands),
         out_specs=(VMEM,) * 6,
         scratch_shapes=scratch,
         compiler_params=pltpu.CompilerParams(collective_id=1, has_side_effects=True, vmem_limit_bytes=60 * 2**20),
         cost_estimate=pl.CostEstimate(flops=4 * 10**9, bytes_accessed=40 * 2**20, transcendentals=0),
-    )(x_all, g3, w3, down.reshape(2, 4, 128, 1024), up.reshape(4, 2, 4, 32, 1024), out.reshape(4, 2, 4, 32, 1024), mid.reshape(16, 16, 1024), vec)
+    )(*operands)
 
 
 def tile_cols(i, size):
@@ -629,8 +688,8 @@
 def middle_kernel(
     heads_ref, x_ref, up_ref, wo_ref, wu_ref, wd_ref, par_ref,
     layer_ref, down_out, upg_out, og_out, gatt_ref, mid1_ref, vec_ref,
-    att, nl, gff, slope, hid, gpre, normed, xhat, rstd, work, moved_buf, gbr, gas, ps, pr,
-    s_a, r_a, s_b, r_b, s_g, r_g, s_p, r_p, s_m, r_m, loc,
+    att, nl, gff, slope, hid, gpre, normed, xhat, rstd, work, moved_buf, gbr, gas, ps, pr, down, down_y,
+    s_a, r_a, s_b, r_b, s_g, r_g, s_p, r_p, s_m, r_m, s_y, r_y, loc,
 ):
     me = Place()
     f, b = me.f, me.b
@@ -770,14 +829,23 @@
         lax.fori_loop(0, 2, pre_tile, 0)
         lax.fori_loop(0, 2, in_tile, 0)
 
+    c_down = remote(down.at[1 - b], down_y, s_y.at[0], r_y.at[0], me.across())
+
     def weight_grads():
-        def tile(i, carry):
+        def down_tile(i, carry):
             cols = tile_cols(i, 256)
-            down_out[cols, :] = dense_in(hid[:, :, cols].reshape(1024, 256), gff[...].reshape(1024, 1024)).astype(BF)
+            part = dense_in(hid[:, :, cols].reshape(1024, 256), gff[...].reshape(1024, 1024)).astype(BF)
+            down[i // 2, pl.ds(pl.multiple_of(i % 2 * 256, 256), 256)] = part
+            return carry
+
+        def up_tile(i, carry):
+            cols = tile_cols(i, 256)
             upg_out[cols, :] = dense_in(nl[:, :, cols].reshape(1024, 256), gpre[...].reshape(1024, 1024)).astype(BF)
             return carry
 
-        lax.fori_loop(0, 4, tile, 0)
+        lax.fori_loop(0, 4, down_tile, 0)
+        c_down.start()
+        lax.fori_loop(0, 4, up_tile, 0)
         vec_ref[pl.ds(3, 1), :] = jnp.sum(gpre[...].reshape(1024, 1024).astype(F32), axis=0, keepdims=True)
 
     back = run(1, backward, gff, weight_grads)
@@ -811,6 +879,8 @@
     for k in range(1, 8):
         where, _ = peer_slot(k, -1)
         remote(gas.at[0], gatt_ref.at[:, where], s_b.at[k - 1], r_b.at[k - 1], peers[k - 1]).wait()
+    c_down.wait()
+    down_out[...] = (down[b].astype(F32) + down_y[...].astype(F32)).astype(BF)
 
     @pl.when(me.stays())
     def _():
@@ -829,14 +899,15 @@
         v((16, 16, 1024), BF), v(block, BF), v(block, BF), v(block, F32), v(block, BF), v(block, BF),
         v((256, 1024), F32), v((256, 1024), F32), v((256, 1), F32), v((256, 1024), F32), v((256, 1024), BF),
         v((256, 1024), BF), v((8, 16, 16, PAIR), BF), v((2, 4, 256, 1024), BF), v((2, 3, 256, 1024), BF),
+        v((2, 512, 1024), BF), v((512, 1024), BF),
         dma((7,)), dma((7,)), dma((7,)), dma((7,)), dma((2, 3)), dma((2, 3)), dma((2, 3)), dma((2, 3)),
-        dma((1,)), dma((1,)), dma((1,)),
+        dma((1,)), dma((1,)), dma((1,)), dma((1,)), dma((1,)),
     ]
     square = jax.ShapeDtypeStruct((1024, 1024), BF)
     return pl.pallas_call(
         middle_kernel,
         out_shape=(
-            jax.ShapeDtypeStruct((256, 1024), BF), square, square, square,
+            jax.ShapeDtypeStruct((256, 1024), BF), jax.ShapeDtypeStruct((512, 1024), BF), square, square,
             jax.ShapeDtypeStruct((16, 8, 16, PAIR), BF),
             jax.ShapeDtypeStruct((256, 1024), F32),
             jax.ShapeDtypeStruct((8, 1024), F32),
@@ -898,7 +969,58 @@
     def w3_rows(src):
         return cols(src, 256)
 
+    def wo_rows(src, which):
+        return pl.ds(pl.multiple_of(src * 256 + which * 128, 128), 128)
+
+    half = cols(b, 128)
+    u_x = [
+        remote(ew_ref.at[half, cols(xs, 1024)], wu_ref.at[wo_rows(f, b)], s_u.at[1], r_u.at[1], me.beside()),
+        remote(ew_ref.at[half, cols(xo, 1024)], wu_ref.at[wo_rows(f, b)], s_u.at[2], r_u.at[2], me.at(f=xo)),
+    ]
+    o_x = remote(ow_ref.at[half], wo_ref.at[wo_rows(f, b)], s_o.at[1], r_o.at[1], me.beside())
+    u_sib = remote(ew_ref.at[:, cols(sib, 1024)], wu_ref.at[w3_rows(f)], s_u.at[0], r_u.at[0], me.sibling())
+    o_sib = remote(ow_ref, wo_ref.at[w3_rows(f)], s_o.at[0], r_o.at[0], me.sibling())
+    for c in u_x + [o_x, u_sib, o_sib]:
+        c.start()
+    o_own = pltpu.make_async_copy(ow_ref, wo_ref.at[w3_rows(f)], loc.at[5])
+    u_own = pltpu.make_async_copy(ew_ref.at[:, cols(f, 1024)], wu_ref.at[w3_rows(f)], loc.at[6])
+    o_own.start()
+    u_own.start()
     weights = (qw_ref, kw_ref, vw_ref)
+
+    def w3_own(j):
+        return pltpu.make_async_copy(
+            weights[j].at[:, cols(b * 4 + swapped(f), 128)], w3_ref.at[w3_rows(f), pl.ds(128 * j, 128)], loc.at[2 + j]
+        )
+
+    for j in range(3):
+        w3_own(j).start()
+    for c in u_x:
+        c.wait()
+    u_fwd = [
+        remote(wu_ref.at[wo_rows(src, b)], wu_ref.at[wo_rows(src, b)], s_u.at[3 + i], r_u.at[3 + i], me.across())
+        for i, src in enumerate((xs, xo))
+    ]
+    for c in u_fwd:
+        c.start()
+    o_x.wait()
+    o_fwd = [
+        remote(wo_ref.at[wo_rows(xs, b)], wo_ref.at[wo_rows(xs, b)], s_o.at[2], r_o.at[2], me.sibling()),
+        remote(wo_ref.at[wo_rows(xs, b)], wo_ref.at[wo_rows(xs, b)], s_o.at[3], r_o.at[3], me.across()),
+    ]
+    for c in o_fwd:
+        c.start()
+
+    def piece(i, ref, where):
+        return remote(ref, ref, s_x.at[i], r_x.at[i], where)
+
+    relocated(0, tok_ref, theirs)
+    own = x_ref.at[:, slot]
+    sends = [piece(1, own, me.beside()), piece(2, own, me.across()), piece(0, own, me.sibling())]
+    for c in sends:
+        c.start()
+    relocate(7, cot_ref, up_ref)
+
     for k in (2, 3, 1):
         dest = b * 4 + swapped((f + k) % 4)
         for j in range(3):
@@ -906,41 +1028,14 @@
                 weights[j].at[:, cols(dest, 128)], w3_ref.at[w3_rows(f), pl.ds(128 * j, 128)],
                 s_w.at[j, k - 1], r_w.at[j, k - 1], me.fsdp(k),
             ).start()
-    for j in range(3):
-        pltpu.make_async_copy(
-            weights[j].at[:, cols(b * 4 + swapped(f), 128)], w3_ref.at[w3_rows(f), pl.ds(128 * j, 128)], loc.at[2 + j]
-        ).start()
-
-    half = cols(b, 128)
-
-    def wo_rows(src, which):
-        return pl.ds(pl.multiple_of(src * 256 + which * 128, 128), 128)
-
-    o_own = pltpu.make_async_copy(ow_ref, wo_ref.at[w3_rows(f)], loc.at[5])
-    o_own.start()
-    o_sib = remote(ow_ref, wo_ref.at[w3_rows(f)], s_o.at[0], r_o.at[0], me.sibling())
-    o_x = remote(ow_ref.at[half], wo_ref.at[wo_rows(f, b)], s_o.at[1], r_o.at[1], me.beside())
-    o_x.start()
-    o_sib.start()
-
-    u_own = pltpu.make_async_copy(ew_ref.at[:, cols(f, 1024)], wu_ref.at[w3_rows(f)], loc.at[6])
-    u_own.start()
-    u_sib = remote(ew_ref.at[:, cols(sib, 1024)], wu_ref.at[w3_rows(f)], s_u.at[0], r_u.at[0], me.sibling())
-    u_sib.start()
-    u_x = [
-        remote(ew_ref.at[half, cols(xs, 1024)], wu_ref.at[wo_rows(f, b)], s_u.at[1], r_u.at[1], me.beside()),
-        remote(ew_ref.at[half, cols(xo, 1024)], wu_ref.at[wo_rows(f, b)], s_u.at[2], r_u.at[2], me.at(f=xo)),
-    ]
-
-    def piece(i, ref, where):
-        return remote(ref, ref, s_x.at[i], r_x.at[i], where)
-
-    relocated(0, tok_ref, theirs)
-    relocate(7, cot_ref, up_ref)
-    own = x_ref.at[:, slot]
-    sends = [piece(1, own, me.beside()), piece(2, own, me.across()), piece(0, own, me.sibling())]
-    for c in sends:
-        c.start()
+
+    def project(which):
+        part = dense(x_ref[:, which].reshape(256, 1024), w3_ref[...]) + bias_ref[...]
+        part = part.astype(BF).reshape(16, 16, 3 * PAIR)
+        q_ref[:, which] = part[:, :, :PAIR]
+        k_ref[:, which] = part[:, :, PAIR : 2 * PAIR]
+        v_ref[:, which] = part[:, :, 2 * PAIR :]
+
     piece(1, x_ref.at[:, slot_x], me.beside()).wait_recv()
     more = [piece(4, x_ref.at[hi, slot_x], me.across()), piece(3, x_ref.at[:, slot_x], me.sibling())]
     for c in more:
@@ -951,22 +1046,10 @@
     for c in more:
         c.start()
     sends += more
-    for c in u_x:
-        c.start()
-    o_x.wait()
-    o_fwd = [
-        remote(wo_ref.at[wo_rows(xs, b)], wo_ref.at[wo_rows(xs, b)], s_o.at[2], r_o.at[2], me.sibling()),
-        remote(wo_ref.at[wo_rows(xs, b)], wo_ref.at[wo_rows(xs, b)], s_o.at[3], r_o.at[3], me.across()),
-    ]
-    for c in o_fwd:
-        c.start()
-    piece(4, x_ref.at[hi, slot_d], me.across()).wait_recv()
-    more = [piece(8, x_ref.at[hi, slot_d], me.sibling())]
-    more[0].start()
-    piece(6, x_ref.at[lo, slot_d], me.beside()).wait_recv()
-    more.append(piece(7, x_ref.at[lo, slot_d], me.sibling()))
-    more[1].start()
-    sends += more
+    o_fwd[0].wait()
+    o_fwd[1].wait()
+    late = remote(wo_ref.at[wo_rows(xs, 1 - b)], wo_ref.at[wo_rows(xs, 1 - b)], s_o.at[4], r_o.at[4], me.sibling())
+    late.start()
     for k in (1, 2, 3):
         src = (f + 4 - k) % 4
         for j in range(3):
@@ -975,39 +1058,25 @@
                 s_w.at[j, k - 1], r_w.at[j, k - 1], me.fsdp(k),
             ).wait()
     for j in range(3):
-        pltpu.make_async_copy(
-            weights[j].at[:, cols(b * 4 + swapped(f), 128)], w3_ref.at[w3_rows(f), pl.ds(128 * j, 128)], loc.at[2 + j]
-        ).wait()
-    o_fwd[0].wait()
-    o_fwd[1].wait()
-    late = remote(wo_ref.at[wo_rows(xs, 1 - b)], wo_ref.at[wo_rows(xs, 1 - b)], s_o.at[4], r_o.at[4], me.sibling())
-    late.start()
-    for i, where, part in (
-        (0, own, slot + other), (3, own, slot_x + other), (5, own, slot_y + other),
-    ):
+        w3_own(j).wait()
+    project(slot)
+    project(slot_x)
+    piece(4, x_ref.at[hi, slot_d], me.across()).wait_recv()
+    more = [piece(8, x_ref.at[hi, slot_d], me.sibling())]
+    more[0].start()
+    piece(6, x_ref.at[lo, slot_d], me.beside()).wait_recv()
+    more.append(piece(7, x_ref.at[lo, slot_d], me.sibling()))
+    more[1].start()
+    sends += more
+    project(slot_y)
+    for i, part in ((0, slot + other), (3, slot_x + other), (5, slot_y + other)):
         piece(i, x_ref.at[:, part], me.sibling()).wait_recv()
+        project(part)
+    project(slot_d)
     piece(8, x_ref.at[hi, slot_d + other], me.sibling()).wait_recv()
     piece(7, x_ref.at[lo, slot_d + other], me.sibling()).wait_recv()
-
-    def project(i, carry):
-        part = dense(x_ref[pl.ds(2 * i, 2)].reshape(256, 1024), w3_ref[...]) + bias_ref[...]
-        part = part.astype(BF)
-        rows = cols(i, 256)
-        q_ref[rows, :] = part[:, :PAIR]
-        k_ref[rows, :] = part[:, PAIR : 2 * PAIR]
-        v_ref[rows, :] = part[:, 2 * PAIR :]
-        return carry
-
-    lax.fori_loop(0, 8, project, 0)
-
-    for i, c in enumerate(u_x):
-        c.wait()
-    u_fwd = [
-        remote(wu_ref.at[wo_rows(src, b)], wu_ref.at[wo_rows(src, b)], s_u.at[3 + i], r_u.at[3 + i], me.across())
-        for i, src in enumerate((xs, xo))
-    ]
-    for c in u_fwd:
-        c.start()
+    project(slot_d + other)
+
     for c in sends:
         c.wait_send()
     late.wait()
@@ -1024,7 +1093,7 @@
 def start(tokens, cotangent, ends, query_w, key_w, value_w, output_w, expand_w, bias3):
     dma = pltpu.SemaphoreType.DMA
     hbm = pl.BlockSpec(memory_space=pl.ANY)
-    heads = jax.ShapeDtypeStruct((2048, PAIR), BF)
+    heads = jax.ShapeDtypeStruct((16, GROUP, 16, PAIR), BF)
     square = jax.ShapeDtypeStruct((1024, 1024), BF)
     return pl.pallas_call(
         start_kernel,
@@ -1034,12 +1103,12 @@
             jax.ShapeDtypeStruct((1024, 3 * PAIR), BF), square, square,
         ),
         in_specs=[hbm, hbm, VMEM] + [hbm] * 5 + [VMEM],
-        out_specs=(VMEM,) * 9,
+        out_specs=(VMEM, hbm, VMEM, VMEM, VMEM, VMEM, VMEM, hbm, hbm),
         scratch_shapes=[
             dma((8,)), dma((8,)), dma((3, 3)), dma((3, 3)), dma((5,)), dma((5,)), dma((5,)), dma((5,)),
             dma((9,)), dma((9,)), dma((8,)),
         ],
-        compiler_params=pltpu.CompilerParams(collective_id=3, has_side_effects=True, vmem_limit_bytes=40 * 2**20),
+        compiler_params=pltpu.CompilerParams(collective_id=3, has_side_effects=True, vmem_limit_bytes=60 * 2**20),
         cost_estimate=pl.CostEstimate(flops=2 * 10**9, bytes_accessed=20 * 2**20, transcendentals=0),
     )(tokens, cotangent, ends, query_w, key_w, value_w, output_w, expand_w, bias3)
 
@@ -1089,6 +1158,7 @@
     x_all, upstream, ends, q, k_own, v_own, w_three, w_output, w_up = start(
         tokens.reshape(acts), cotangent.reshape(acts), own_ends, query_w, key_w, value_w, output_w, expand_w, bias3
     )
+    q, k_own, v_own = (part.reshape(GROUP * mine, PAIR) for part in (q, k_own, v_own))
     inputs = lax.dynamic_index_in_dim(x_all, swapped(f) * 2 + b, 1, keepdims=False).reshape(mine, width)
     x_all = x_all.reshape(GROUP * mine, width)
     upstream = upstream.reshape(mine, width)
@@ -1134,24 +1204,22 @@
     layer_out = layer_out.reshape(tok_shape)
     grad_att = grad_att.reshape(GROUP * mine, PAIR)
 
-    grad_q, grad_k, grad_v = attend_back(
-        bounds, q, k, v, seg_q, seg_k, att_heads, lse, grad_att, chunks
-    )
+    attention = (q, k, v, seg_q, seg_k, att_heads, lse, grad_att)
+    grad_three = None
     if chunks > 1:
+        grad_q, grad_k, grad_v = attend_back(bounds, *attention, chunks)
+        attention = None
         grad_k = lax.psum_scatter(
             grad_k.astype(BF), "ctx", axis_index_groups=same_place, tiled=True
         )
         grad_v = lax.psum_scatter(
             grad_v.astype(BF), "ctx", axis_index_groups=same_place, tiled=True
         )
-    grad_three = jnp.concatenate([grad_q, grad_k, grad_v], axis=1)
-    sums3 = jnp.sum(grad_three.astype(F32), axis=0)
-    grad_query_b = lax.dynamic_update_slice_in_dim(jnp.zeros_like(query_b), sums3[:PAIR], here, 0)
-    grad_value_b = lax.dynamic_update_slice_in_dim(jnp.zeros_like(value_b), sums3[2 * PAIR :], here, 0)
+        grad_three = jnp.concatenate([grad_q, grad_k, grad_v], axis=1)
     here_rows = jnp.zeros((n_f, units), F32)
     sums = jnp.concatenate(
         [
-            jnp.stack([grad_query_b, grad_value_b]),
+            jnp.zeros((2, width), F32),
             vec[:3],
             vec[4:7],
             lax.dynamic_update_slice_in_dim(here_rows, vec[3:4], f, 0),
@@ -1159,7 +1227,7 @@
         ]
     )
     share_down, share_up, share_out, share_three, moved, sums = tail(
-        x_all, grad_three, w_three, part_down, part_up, part_out, grad_mid1, sums
+        attention, x_all, grad_three, w_three, part_down, part_up, part_out, grad_mid1, sums
     )
     grad_inputs = moved.reshape(tok_shape).astype(F32)
     shares = tuple(part.astype(F32) for part in (share_three, share_out, share_up, share_down)) + (sums,)

time: 461 us -> 415 us (0.900)
  Pallas kernels: 421 us -> 382 us
  local copies, waits for them, and re-layouts: 28.8 us -> 20.3 us
    pallas_call x2 -> x1, Pallas kernels: 206 us -> 170 us  [tail(): pl.pallas_call(functools.partial(tail_kernel, fused), out_shape=(jax.Shap...]
    pallas_call x1, Pallas kernels: 88.6 us -> 73.7 us  [start(): pl.pallas_call(start_kernel, out_shape=(jax.ShapeDtypeStruct((16, GROUP,...]
    unnamed x75 -> x25, local copies, waits for them, and re-layouts: 19.1 us -> 5.41 us
    pallas_call x1, Pallas kernels: 108 us -> 121 us  [middle(): pl.pallas_call(middle_kernel, out_shape=(jax.ShapeDtypeStruct((256, 1024)...]
where the time goes in v6:
time: 415 us
  Pallas kernels  382 us (92%)
  local copies, waits for them, and re-layouts  20.3 us (5%)
  other arithmetic  11.1 us (3%)
    pallas_call x1, Pallas kernels, tail(): pl.pallas_call(functools.partial(tail_kernel, fused), out_shape=(jax.Shap...  170 us
    pallas_call x1, Pallas kernels, middle(): pl.pallas_call(middle_kernel, out_shape=(jax.ShapeDtypeStruct((256, 1024)...  121 us
    pallas_call x1, Pallas kernels, start(): pl.pallas_call(start_kernel, out_shape=(jax.ShapeDtypeStruct((16, GROUP,...  73.7 us
    pallas_call x1, Pallas kernels, attend(): pl.pallas_call(functools.partial(attend_kernel, BQ, BK, chunks), out_shap...  17.9 us

profile of v6, /device:TPU:0, one launch (start us, length us, event | category | flops | bytes accessed | tf_op | source)
XLA Modules:
  0.0 414.7 jit_solution(5894525896937426472)
XLA Ops:
  0.7 0.9 select_reduce_fusion.1
  1.7 0.8 dynamic_slice.13
  2.5 0.8 dynamic_slice.14
  3.2 0.6 broadcast_in_dim.55.bias_ref
  3.8 0.6 pad.4.ends_ref
  4.4 0.7 dynamic_slice.16
  5.1 1.4 stack.31.par_ref
  6.6 73.7 %shard_map.314 = (bf16[16,8,16,1024]{3,2,1,0:T(8,128)(2,1)}, bf16[16,16,1024]{2,1,0:T(8,128)(2,1)}, s32[8,128]{1,0:T(8,128)}, bf16[16,8,16,128]{3,2,1,0:T(8,128)...) custom-call(bf16[16,16,1024]{2,1,0:T(8,128)(2,1)} %bitcast.90, ...), custom_call_target="tpu_custom_call" | custom-call | flops 2000000000 | bytes 20971520 | tf_op jit(solution)/shard_map/pallas_call | solution.py:1098
  80.3 0.8 slice_bitcast_fusion.4
  81.5 0.2 convert_reduce_fusion.2
  81.8 0.2 convert_reduce_fusion.3
  82.1 1.9 constant_dynamic-slice_fusion
  84.0 0.4 copy.44.sq_ref.refs_3_
  84.4 17.9 %shard_map.315 = (bf16[2048,128]{1,0:T(8,128)(2,1)S(1)}, f32[4096,1]{1,0:T(8,128)S(1)}) custom-call(s32[8,1]{1,0:T(8,128)S(1)} %copy.42.lo_ref, s32[8,1]{1,0:T(8,128)S(1)} %copy.43.hi_ref, bf16[2048,128]{1,0:T(8,128)(2,1)S(1)} %bitcast.54, bf16[2048,128]{1,0:T(8,128)(2,1)S(1)} %bitcast.56, bf16[2048,128]{1,0:T(8,128)(2,1)S(1)} %bitcast.58, ...), custom_call_target="tpu_custom_call" | custom-call | tf_op jit(solution)/shard_map/pallas_call | solution.py:176
  102.4 1.3 copy-done.1
  103.7 0.8 copy-done.5
  104.5 121.1 %shard_map.316 = (bf16[256,1024]{1,0:T(8,128)(2,1)}, bf16[512,1024]{1,0:T(8,128)(2,1)}, bf16[1024,1024]{1,0:T(8,128)(2,1)}, bf16[1024,1024]{1,0:T(8,128)(2,1)}, ...) custom-call(bf16[16,8,16,128]{3,2,1,0:T(8,128)(2,1)} %bitcast.59, ...), custom_call_target="tpu_custom_call" | custom-call | flops 14000000000 | bytes 20971520 | tf_op jit(solution)/shard_map/pallas_call | solution.py:907
  225.5 0.8 slice.67
  226.4 0.8 fusion.20
  227.2 1.3 concatenate.7.refs_14_
  228.5 169.6 %shard_map.317 = (bf16[1024,1024]{1,0:T(8,128)(2,1)}, bf16[256,4096]{1,0:T(8,128)(2,1)}, bf16[256,1024]{1,0:T(8,128)(2,1)}, bf16[3,256,1024]{2,1,0:T(8,128)(2,1)...) custom-call(bf16[2048,128]{1,0:T(8,128)(2,1)} %bitcast.53, bf16[2048,128]{1,0:T(8,128)(2,1)} %bitcast.55, ...), custom_call_target="tpu_custom_call" | custom-call | flops 4000000000 | bytes 41943040 | tf_op jit(solution)/shard_map/pallas_call | solution.py:666
  398.2 0.9 slice_bitcast_fusion.3
  399.0 1.8 fusion.19
  400.9 0.6 copy.48
  401.5 2.1 bitcast_convert_fusion
  403.6 2.1 convert_element_type.53
  405.7 0.4 convert_element_type.52
  406.2 1.7 slice_bitcast_fusion
  407.9 1.0 copy-done.8
  408.9 2.5 convert_element_type.54
  411.4 2.5 convert_element_type.55
  413.9 0.8 copy.51
  (35 shorter events, 0.9 us)
Async XLA Ops:
  80.2 4.1 copy-start.2
  80.2 4.1 copy-start.3
  80.3 4.1 copy-start.4
  81.2 21.1 %copy-start.6 = (s32[2048]{0:T(1024)}, s32[2048]{0:T(1024)S(1)}, u32[]{:S(2)}) copy-start(s32[2048]{0:T(1024)S(1)} %get-tuple-element.66) | copy-start | bytes 24580
  84.4 141.1 %copy-start = (s32[2048,1]{1,0:T(8,128)}, s32[2048,1]{1,0:T(8,128)S(1)}, u32[]{:S(2)}) copy-start(s32[2048,1]{1,0:T(8,128)S(1)} %copy.44.sq_ref.refs_3_) | copy-start | bytes 24580
  102.3 1.3 copy-start.1
  103.7 0.8 copy-start.5
  398.1 7.6 %copy-start.9 = (bf16[3,256,1024]{2,1,0:T(8,128)(2,1)S(1)}, bf16[3,256,1024]{2,1,0:T(8,128)(2,1)}, u32[]{:S(2)}) copy-start(bf16[3,256,1024]{2,1,0:T(8,128)(2,1)} %get-tuple-element.60) | copy-start | bytes 4718596
  406.1 2.7 copy-start.8
  408.9 2.5 copy-start.7
  411.4 2.5 copy-start.10
